TPU v7x, 32 devices: a whole 2x2x4 slice. The times are simulated.
32 devices in a mesh: parts: 2 (over y), tensor: 4 (over x, core), dp: 4 (over z).
Axes of the slice: x: 2, y: 2, z: 4, core: 2. Of those that a mesh axis runs over, the one named last changes fastest.
Arguments:
- rows_in: bfloat16 [2048, 8192], P(('parts', 'tensor'), 'dp'), parts along dimension 0, may hold values from -6 to 6
- up_weight: bfloat16 [8192, 32768], P('dp', 'tensor'), may hold values from -0.0625 to 0.0625
- up_bias: float32 [32768], P('tensor'), may hold values from -3 to 3
- down_weight: bfloat16 [32768, 8192], P('tensor', 'dp'), may hold values from -0.09375 to 0.09375
- down_bias: float32 [8192], P('dp'), may hold values from -3 to 3
- active_ids: int32 [16, 4, 8], P('parts', 'tensor'), parts along dimension 0, may hold values from 0 to 255, as said below
- active_counts: int32 [16, 4], P('parts', 'tensor'), parts along dimension 0, may hold values from 1 to 8, as said below
Outputs:
- ffn_out: float32 [2048, 8192], P(('parts', 'tensor'), 'dp'), parts along dimension 0
There are 2 independent parts, one for each index of `parts`. A program takes and returns all parts, laid end to end along the dimension named above; an argument that names none is the same for every part. Nothing has to cross between parts.
Inputs may be any that keep to these rules, and one draw needn't show every extreme that they name: active_ids[b, t, :] are 8 distinct block ids of tensor index t's own range, t * 64 up to (t+1) * 64 - 1; entries of slots that are not live are such ids too. `active_counts`: in every row block some tensor index has exactly 8 live slots.
All inputs are finite; a program needn't handle non-finite values.
Results may differ from a plain program's by a relative error of at most 0.012.
Values may be sent and summed in bfloat16 or wider, within the bound.
No kernel may reach another device: no remote copies, remote signals or barrier semaphores. Data moves between devices by JAX's collectives and lax.ppermute only.
A program may use at most 320 MiB of HBM per device.

v0:
```python
import jax
import jax.numpy as jnp
from jax import lax
from jax.sharding import PartitionSpec as P

BLK = 128


def finish(summed, bias, live):
    return (jnp.maximum(summed + bias, 0.0) * live).astype(jnp.bfloat16)


def shards(rows_in, up_weight, up_bias, down_weight, down_bias, active_ids, active_counts):
    gathered = lax.all_gather(rows_in, "tensor", axis=0, tiled=True)
    total_rows, width_part = gathered.shape
    block_rows = total_rows // BLK
    per_shard = up_weight.shape[1] // BLK
    slots = active_ids.shape[2]
    local_ids = active_ids[:, 0, :] - lax.axis_index("tensor") * per_shard
    flat = local_ids.reshape(-1)
    grouped = gathered.reshape(block_rows, BLK, width_part)
    up_chosen = jnp.take(up_weight.reshape(width_part, per_shard, BLK), flat, axis=1)
    up_chosen = up_chosen.reshape(width_part, block_rows, slots * BLK)
    partial_value = jnp.einsum(
        "brk,kbn->brn", grouped, up_chosen, preferred_element_type=jnp.float32
    )
    bias_chosen = jnp.take(up_bias.reshape(per_shard, BLK), flat, axis=0).reshape(
        block_rows, 1, slots * BLK
    )
    slot_iota = jnp.arange(slots, dtype=jnp.int32)
    live = (slot_iota[None, :] < active_counts[:, 0][:, None]).astype(jnp.float32)
    live = jnp.broadcast_to(live[:, :, None], (block_rows, slots, BLK)).reshape(
        block_rows, 1, slots * BLK
    )
    summed = lax.psum(partial_value.astype(jnp.bfloat16), "dp").astype(jnp.float32)
    hidden = finish(summed, bias_chosen, live)
    down_chosen = jnp.take(down_weight.reshape(per_shard, BLK, width_part), flat, axis=0)
    down_chosen = down_chosen.reshape(block_rows, slots * BLK, width_part)
    terms = jnp.einsum("brn,bnk->brk", hidden, down_chosen, preferred_element_type=jnp.float32)
    terms = terms.reshape(total_rows, width_part)
    owned = lax.psum_scatter(
        terms.astype(jnp.bfloat16), "tensor", scatter_dimension=0, tiled=True
    ).astype(jnp.float32)
    return owned + down_bias[None, :]


def solution(mesh):
    placed = (
        P(("parts", "tensor"), "dp"),
        P("dp", "tensor"),
        P("tensor"),
        P("tensor", "dp"),
        P("dp"),
        P("parts", "tensor", None),
        P("parts", "tensor"),
    )
    return jax.shard_map(
        shards, mesh=mesh, in_specs=placed, out_specs=P(("parts", "tensor"), "dp"), check_vma=False
    )
```

profile of v0, /device:TPU:12, one launch (start us, length us, event | category | flops | bytes accessed | tf_op | source)
XLA Modules:
  0.0 385.0 jit_solution(8436447665139304768)
XLA Ops:
  6.5 0.0 copy-start
  6.5 0.0 all-gather.2.cloned.1.call-start
  6.5 0.7 all-gather.2.cloned.1.call-update
  7.3 0.0 all-reduce.2.cloned.1.call-start
  7.3 0.7 compare_and_fusion
  8.0 0.1 sub.26
  8.1 42.3 %copy.14 = bf16[2048,8192]{0,1:T(8,128)(2,1)} copy(bf16[2048,8192]{1,0:T(8,128)(2,1)} %param.8) | data formatting | bytes 67108864 | tf_op args[1]
  50.4 44.4 %copy.15 = bf16[2048,64,128]{2,0,1:T(8,128)(2,1)} copy(bf16[2048,64,128]{0,2,1:T(8,128)(2,1)} %bitcast.36) | data formatting | bytes 67108864 | tf_op jit(solution)/shard_map/reshape | solution.py:22
  94.8 22.7 %gather_fusion = bf16[64,2048,128]{2,1,0:T(8,128)(2,1)} fusion(bf16[2048,64,128]{2,0,1:T(8,128)(2,1)} %copy.15, s32[1024]{0:T(1024)S(1)} %pad_clamp_fusion), kind=kCustom, calls=%fused_computation | custom fusion | bytes 67109120 | tf_op jit(solution)/shard_map/jit(_take)/gather | solution.py:22
  117.5 44.6 %copy.16 = bf16[2048,64,128]{0,2,1:T(8,128)(2,1)} copy(bf16[2048,64,128]{2,0,1:T(8,128)(2,1)} %bitcast.34) | data formatting | bytes 67108864 | tf_op jit(solution)/shard_map/jit(_take)/gather | solution.py:22
  162.0 0.1 copy.13
  162.1 0.0 copy-start.2
  162.1 22.6 %gather_fusion.2 = bf16[64,128,2048]{2,1,0:T(8,128)(2,1)} fusion(bf16[64,128,2048]{2,1,0:T(8,128)(2,1)} %bitcast.37, s32[1024]{0:T(1024)S(1)} %pad_clamp_fusion), kind=kCustom, calls=%fused_computation.2 | custom fusion | bytes 67109120 | tf_op jit(solution)/shard_map/jit(_take)/gather | solution.py:37
  184.7 0.0 copy-done
  184.7 0.6 gather_fusion.1
  185.4 0.0 copy-done.2
  185.4 0.1 broadcast_bitcast_fusion.1
  185.4 0.1 broadcast_bitcast_fusion
  185.5 0.1 broadcast_select_fusion
  185.6 22.9 %bitcast_select_fusion.1 = bf16[2048,8,1024]{0,2,1:T(8,128)(2,1)} fusion(pred[8,1024]{1,0:T(8,128)(4,1)S(1)} %broadcast_bitcast_fusion.1, bf16[2048,8,1024]{0,2,1:T(8,128)(2,1)} %bitcast.35), kind=kLoop, calls=%fused_computation.4 | loop fusion | flops 16777216 | bytes 67117056 | tf_op jit(solution)/shard_map/jit(_take)/select_n | solution.py:22
  208.5 0.0 all-gather.2.cloned.1.call-done
  208.5 17.3 %convert_bitcast_fusion = bf16[8,128,1024]{1,2,0:T(8,128)(2,1)} fusion(bf16[2048,8,1024]{0,2,1:T(8,128)(2,1)} %bitcast_select_fusion.1, bf16[8,128,2048]{2,1,0:T(8,128)(2,1)} %bitcast.41), kind=kOutput, calls=%fused_computation.11 | convolution fusion | flops 4296015872 | bytes 39845888 | tf_op jit(solution)/shard_map/brk,kbn->brn/dot_general | solution.py:24
  225.8 0.0 all-reduce.2.cloned.1.call-update
  225.8 0.0 reduce-scatter.2.cloned.1.call-start
  225.9 23.1 %bitcast_select_fusion = bf16[8,1024,2048]{2,1,0:T(8,128)(2,1)} fusion(pred[8,1024]{1,0:T(8,128)(4,1)S(1)} %broadcast_bitcast_fusion.1, bf16[8,1024,2048]{2,1,0:T(8,128)(2,1)} %bitcast.33), kind=kLoop, calls=%fused_computation.3 | loop fusion | flops 16777216 | bytes 67117056 | tf_op jit(solution)/shard_map/jit(_take)/select_n | solution.py:37
  249.0 0.0 copy-start.1
  249.0 65.6 %all-reduce.2.cloned.1.call-done = bf16[8,128,1024]{1,2,0:T(8,128)(2,1)} async-done(((bf16[8,128,1024]{1,2,0:T(8,128)(2,1)}), bf16[8,128,1024]{1,2,0:T(8,128)(2,1)}) %all-reduce.2.cloned.1.call-update) | async-done | bytes 2097168 | tf_op jit(solution)/shard_map/psum | solution.py:35
  314.6 16.0 %convolution_convert_fusion = bf16[8,128,2048]{2,1,0:T(8,128)(2,1)} fusion(bf16[8,1024,2048]{2,1,0:T(8,128)(2,1)} %bitcast_select_fusion, bf16[8,128,1024]{1,2,0:T(8,128)(2,1)} %all-reduce.2.cloned.1.call-done, f32[8,1024]{1,0:T(8,128)S(1)} %broadcast_bitcast_fusion, f32[8,1024]{1,0:T(8,128)S(1)} %broadcast_select_fusion), kind=kOutput, calls=%fused_computation.6 | convolution fusion | flops 4302307328 | bytes 39911424 | tf_op jit(solution)/shard_map/brn,bnk->brk/dot_general | solution.py:39
  330.6 0.0 reduce-scatter.2.cloned.1.call-update
  330.6 45.0 %reduce-scatter.2.cloned.1.call-done = bf16[256,2048]{1,0:T(8,128)(2,1)} async-done(((bf16[1024,2048]{1,0:T(8,128)(2,1)}), bf16[256,2048]{1,0:T(8,128)(2,1)}) %reduce-scatter.2.cloned.1.call-update) | async-done | bytes 1048592 | tf_op jit(solution)/shard_map/reduce_scatter | solution.py:41
  375.6 0.0 copy-done.1
  375.6 2.8 convert_add_fusion
  (4 shorter events, 0.0 us)
Async XLA Ops:
  6.5 178.2 %copy-start = (f32[8192]{0:T(1024)S(1)}, f32[8192]{0:T(1024)}, u32[]{:S(2)}) copy-start(f32[8192]{0:T(1024)} %param.9) | copy-start | bytes 98308
  6.5 202.0 %all-gather.2.cloned.1.call-start = ((), (), s32[]{:S(2)}) async-start(), calls=%async_computation.1 | async-start | bytes 5242880 | tf_op jit(solution)/shard_map/all_gather | solution.py:14
  7.3 307.3 %all-reduce.2.cloned.1.call-start = ((), (), s32[]{:S(2)}) async-start(), calls=%async_computation.2 | async-start | bytes 4194304 | tf_op jit(solution)/shard_map/psum | solution.py:35
  162.1 23.2 %copy-start.2 = (s32[8,1]{0,1:T(1,128)S(1)}, s32[8,1]{0,1:T(1,128)}, u32[]{:S(2)}) copy-start(s32[8,1]{0,1:T(1,128)} %param.13) | copy-start | bytes 100
  225.8 149.8 %reduce-scatter.2.cloned.1.call-start = ((), (), s32[]{:S(2)}) async-start(), calls=%async_computation.3 | async-start | bytes 5242880 | tf_op jit(solution)/shard_map/reduce_scatter | solution.py:41
  249.0 126.7 %copy-start.1 = (f32[2048]{0:T(1024)S(1)}, f32[2048]{0:T(1024)}, u32[]{:S(2)}) copy-start(f32[2048]{0:T(1024)} %param.11) | copy-start | bytes 24580
Sparse Core Ops, SparseCore 0:
  8.9 35.5 all-gather.1
  226.0 88.5 all-reduce.1
  330.8 44.8 reduce-scatter.1
where the time goes:
time: 390 us; the launch traced here: 385 us
  local copies, waits for them, and re-layouts  177 us (45%)
  waiting for transfers between devices  111 us (28%)
  other arithmetic  49.6 us (13%)
  matrix products  33.3 us (9%)
  between operations  13.1 us (3%)
    gather x2, local copies, waits for them, and re-layouts, shards(): jnp.take(up_weight.reshape(width_part, per_shard, BLK), flat, axis=1)  67.3 us
    psum x1, waiting for transfers between devices, shards(): lax.psum(partial_value.astype(jnp.bfloat16), 'dp').astype(jnp.float32)  65.6 us
    reduce_scatter x1, waiting for transfers between devices, shards(): lax.psum_scatter(terms.astype(jnp.bfloat16), 'tensor', scatter_dimension=...  45 us
    reshape x1, local copies, waits for them, and re-layouts, shards(): up_weight.reshape(width_part, per_shard, BLK)  44.4 us
    unnamed x7, local copies, waits for them, and re-layouts  42.3 us
    select_n x1, other arithmetic, shards(): jnp.take(down_weight.reshape(per_shard, BLK, width_part), flat, axis=0)  23.1 us
    select_n x2, other arithmetic, shards(): jnp.take(up_weight.reshape(width_part, per_shard, BLK), flat, axis=1)  22.9 us
    gather x1, local copies, waits for them, and re-layouts, shards(): jnp.take(down_weight.reshape(per_shard, BLK, width_part), flat, axis=0)  22.6 us
  transfers between devices with their start and end apart: 3, of which 2 were waited for; matrix products, arithmetic and copies ran while one was open for 58% of the time, Pallas kernels for 0%

commit v1 on v0

v1 whole, which is shorter than its diff:
```python
import functools

import jax
import jax.numpy as jnp
from jax import lax
from jax.experimental import pallas as pl
from jax.experimental.pallas import tpu as pltpu
from jax.sharding import PartitionSpec as P

BLK = 128
ANY = pl.BlockSpec(memory_space=pl.ANY)
SMEM = pl.BlockSpec(memory_space=pltpu.SMEM)
VMEM = pl.BlockSpec(memory_space=pltpu.VMEM)
VMEM_LIMIT = 40 * 1024 * 1024


def place(flip, step, per_owner):
    if flip is None:
        return step
    return (lax.axis_index("tensor") ^ flip) * per_owner + step


def up_kernel(which, row0, ids, counts, rows, weight, out, x_buf, w_buf, sems):
    slots = ids.shape[2]
    per_shard = weight.shape[1] // BLK
    b = place(*which)
    count = counts[b, 0]

    def slab(s):
        block = lax.rem(ids[b, 0, s], per_shard)
        return pltpu.make_async_copy(
            weight.at[:, pl.ds(pl.multiple_of(block * BLK, BLK), BLK)],
            w_buf.at[:, pl.ds(s * BLK, BLK)],
            sems.at[s],
        )

    fetch = pltpu.make_async_copy(rows.at[pl.ds(row0, BLK)], x_buf, sems.at[slots])
    fetch.start()
    for s in range(slots):
        pl.when(s < count)(lambda s=s: slab(s).start())
    fetch.wait()
    for s in range(0, slots, 2):
        span = pl.ds(s * BLK, 2 * BLK)

        @pl.when(s < count)
        def _(s=s, span=span):
            slab(s).wait()
            pl.when(s + 1 < count)(lambda: slab(s + 1).wait())
            value = jnp.dot(x_buf[...], w_buf[:, span], preferred_element_type=jnp.float32)
            column = lax.broadcasted_iota(jnp.int32, value.shape, 1)
            live = (column < BLK) | (s + 1 < count)
            out[:, span] = jnp.where(live, value, 0.0).astype(out.dtype)

        @pl.when(s >= count)
        def _(span=span):
            out[:, span] = jnp.zeros((BLK, 2 * BLK), out.dtype)


def up(which, row0, ids, counts, rows, weight):
    slots = ids.shape[2]
    width = weight.shape[0]
    return pl.pallas_call(
        functools.partial(up_kernel, which, row0),
        out_shape=jax.ShapeDtypeStruct((BLK, slots * BLK), jnp.bfloat16),
        in_specs=[SMEM, SMEM, ANY, ANY],
        out_specs=VMEM,
        scratch_shapes=[
            pltpu.VMEM((BLK, width), jnp.bfloat16),
            pltpu.VMEM((width, slots * BLK), jnp.bfloat16),
            pltpu.SemaphoreType.DMA((slots + 1,)),
        ],
        compiler_params=pltpu.CompilerParams(vmem_limit_bytes=VMEM_LIMIT),
        cost_estimate=pl.CostEstimate(
            flops=2 * BLK * width * slots * BLK, bytes_accessed=2 * width * slots * BLK, transcendentals=0
        ),
        name="up",
    )(ids, counts, rows, weight)


def act_kernel(which, ids, counts, own, other, bias, out):
    slots = ids.shape[2]
    b = place(*which)
    count = counts[b, 0]
    per_shard = bias.shape[0]
    for s in range(slots):
        span = pl.ds(s * BLK, BLK)
        block = lax.rem(ids[b, 0, s], per_shard)
        value = own[:, span].astype(jnp.float32)
        if other is not None:
            value = value + other[:, span].astype(jnp.float32)
        value = jnp.maximum(value + bias[pl.ds(block, 1), :], 0.0)
        out[:, span] = jnp.where(s < count, value, 0.0).astype(out.dtype)


def activate(which, ids, counts, own, other, bias):
    body = act_kernel
    if other is None:
        body = lambda which, ids, counts, own, bias, out: act_kernel(which, ids, counts, own, None, bias, out)
    operands = [own] if other is None else [own, other]
    return pl.pallas_call(
        functools.partial(body, which),
        out_shape=jax.ShapeDtypeStruct(own.shape, jnp.bfloat16),
        in_specs=[SMEM, SMEM] + [VMEM] * len(operands) + [VMEM],
        out_specs=VMEM,
        cost_estimate=pl.CostEstimate(flops=own.size, bytes_accessed=6 * own.size, transcendentals=0),
        name="act",
    )(ids, counts, *operands, bias)


def down_kernel(which, row0, n_init, has_bias, has_base, two, ids, counts, *refs):
    refs = list(refs)
    hidden = refs.pop(0)
    other = refs.pop(0) if two else None
    weight = refs.pop(0)
    inits = [refs.pop(0) for _ in range(n_init)]
    bias = refs.pop(0) if has_bias else None
    if has_base:
        refs.pop(0)
    out, h_buf, w_buf, acc, out_buf, sems = refs
    slots = ids.shape[2]
    per_shard = weight.shape[0] // BLK
    b = place(*which)
    count = counts[b, 0]

    def slab(s):
        block = lax.rem(ids[b, 0, s], per_shard)
        return pltpu.make_async_copy(
            weight.at[pl.ds(pl.multiple_of(block * BLK, BLK), BLK)],
            w_buf.at[pl.ds(s * BLK, BLK)],
            sems.at[s],
        )

    def fetch(source):
        return pltpu.make_async_copy(source, h_buf, sems.at[slots])

    if two:
        z = lax.axis_index("dp")
        edge = (z != lax.axis_size("dp") // 2) & (z != lax.axis_size("dp") // 2 - 1)
        pl.when(edge)(lambda: fetch(other).start())
        pl.when(jnp.logical_not(edge))(lambda: fetch(hidden).start())
    else:
        fetch(hidden).start()
    for s in range(slots):
        pl.when(s < count)(lambda s=s: slab(s).start())
    start = jnp.zeros(acc.shape, jnp.float32)
    for init in inits:
        start = start + init[...].astype(jnp.float32)
    if bias is not None:
        start = start + bias[...]
    acc[...] = start
    fetch(hidden).wait()
    for s in range(0, slots, 2):

        @pl.when(s < count)
        def _(s=s):
            slab(s).wait()
            pl.when(s + 1 < count)(lambda: slab(s + 1).wait())

            @pl.when(s + 1 >= count)
            def _():
                w_buf[pl.ds((s + 1) * BLK, BLK), :] = jnp.zeros((BLK, w_buf.shape[1]), w_buf.dtype)

            acc[...] += jnp.dot(
                h_buf[:, pl.ds(s * BLK, 2 * BLK)],
                w_buf[pl.ds(s * BLK, 2 * BLK), :],
                preferred_element_type=jnp.float32,
            )

    out_buf[...] = acc[...].astype(out_buf.dtype)
    put = pltpu.make_async_copy(out_buf, out.at[pl.ds(row0, BLK)], sems.at[slots])
    put.start()
    put.wait()


def down(which, ids, counts, hidden, other, weight, inits=(), bias=None, base=None, rows=BLK, row0=0, dtype=jnp.bfloat16):
    slots = ids.shape[2]
    width = weight.shape[1]
    two = other is not None
    operands = [hidden] + ([other] if two else []) + [weight]
    specs = [ANY] * len(operands)
    operands += list(inits)
    specs += [VMEM] * len(inits)
    if bias is not None:
        operands.append(bias)
        specs.append(VMEM)
    aliases = {}
    if base is not None:
        operands.append(base)
        specs.append(ANY)
        aliases = {2 + len(operands) - 1: 0}
    return pl.pallas_call(
        functools.partial(down_kernel, which, row0, len(inits), bias is not None, base is not None, two),
        out_shape=jax.ShapeDtypeStruct((rows, width), dtype),
        in_specs=[SMEM, SMEM] + specs,
        out_specs=ANY,
        scratch_shapes=[
            pltpu.VMEM((BLK, slots * BLK), jnp.bfloat16),
            pltpu.VMEM((slots * BLK, width), jnp.bfloat16),
            pltpu.VMEM((BLK, width), jnp.float32),
            pltpu.VMEM((BLK, width), dtype),
            pltpu.SemaphoreType.DMA((slots + 1,)),
        ],
        input_output_aliases=aliases,
        compiler_params=pltpu.CompilerParams(vmem_limit_bytes=VMEM_LIMIT),
        cost_estimate=pl.CostEstimate(
            flops=2 * BLK * width * slots * BLK, bytes_accessed=2 * width * slots * BLK, transcendentals=0
        ),
        name="down",
    )(ids, counts, *operands)


def plain(rows_in, up_weight, up_bias, down_weight, down_bias, active_ids, active_counts):
    gathered = lax.all_gather(rows_in, "tensor", axis=0, tiled=True)
    blocks = gathered.shape[0] // BLK
    terms = []
    for b in range(blocks):
        which = (None, b, 1)
        part = up(which, b * BLK, active_ids, active_counts, gathered, up_weight)
        summed = lax.psum(part, "dp")
        hidden = activate(which, active_ids, active_counts, summed, None, up_bias.reshape(-1, BLK))
        terms.append(down(which, active_ids, active_counts, hidden, None, down_weight))
    terms = jnp.concatenate(terms, axis=0)
    owned = lax.psum_scatter(terms, "tensor", scatter_dimension=0, tiled=True).astype(jnp.float32)
    return owned + down_bias[None, :]


def staged(rows_in, up_weight, up_bias, down_weight, down_bias, active_ids, active_counts):
    per_owner = rows_in.shape[0] // BLK
    depth = lax.axis_size("dp")
    half = depth // 2
    bias_blocks = up_bias.reshape(-1, BLK)

    def swap(value, flip):
        return lax.ppermute(value, "tensor", [(t, t ^ flip) for t in range(4)])

    def hidden_of(which, row0, rows):
        value = up(which, row0, active_ids, active_counts, rows, up_weight)
        for hop in range(half - 1):
            moved = lax.ppermute(value, "dp", [(hop, hop + 1), (depth - 1 - hop, depth - 2 - hop)])
            value = (value.astype(jnp.float32) + moved.astype(jnp.float32)).astype(jnp.bfloat16)
        moved = lax.ppermute(value, "dp", [(half - 1, half), (half, half - 1)])
        hidden = activate(which, active_ids, active_counts, value, moved, bias_blocks)
        back = hidden
        for hop in range(half - 1, 0, -1):
            back = lax.ppermute(back, "dp", [(hop, hop - 1), (depth - 1 - hop, depth - hop)])
        return hidden, back

    def terms_of(which, pair, **more):
        return down(which, active_ids, active_counts, *pair, down_weight, **more)

    beside = swap(rows_in, 1)
    across = [swap(rows_in[j * BLK : (j + 1) * BLK], 3) for j in range(per_owner)]
    relayed = [swap(a, 1) for a in across]

    own = {}
    sums = {}
    near = {}
    far = {}
    base = None
    for j in range(per_owner):
        own[j] = hidden_of((0, j, per_owner), j * BLK, rows_in)
    for j in range(per_owner):
        pair3 = hidden_of((3, j, per_owner), 0, across[j])
        pair2 = hidden_of((2, j, per_owner), 0, relayed[j])
        sent = swap(terms_of((3, j, per_owner), pair3), 1)
        far[j] = swap(terms_of((2, j, per_owner), pair2, inits=[sent]), 2)
    for j in range(per_owner):
        pair1 = hidden_of((1, j, per_owner), j * BLK, beside)
        near[j] = swap(terms_of((1, j, per_owner), pair1), 1)
    for j in range(per_owner):
        base = terms_of(
            (0, j, per_owner),
            own[j],
            inits=[near[j], far[j]],
            bias=down_bias[None, :],
            base=base,
            rows=per_owner * BLK,
            row0=j * BLK,
            dtype=jnp.float32,
        )
    return base


def solution(mesh):
    placed = (
        P(("parts", "tensor"), "dp"),
        P("dp", "tensor"),
        P("tensor"),
        P("tensor", "dp"),
        P("dp"),
        P("parts", "tensor", None),
        P("parts", "tensor"),
    )

    def run(rows_in, *rest):
        whole_blocks = rows_in.shape[0] % BLK == 0
        if mesh.shape["tensor"] == 4 and mesh.shape["dp"] % 2 == 0 and whole_blocks:
            return staged(rows_in, *rest)
        return plain(rows_in, *rest)

    return jax.shard_map(
        run, mesh=mesh, in_specs=placed, out_specs=P(("parts", "tensor"), "dp"), check_vma=False
    )
```

time: 390 us -> 181 us (0.46)
  local copies, waits for them, and re-layouts: 177 us -> 6.71 us
  waiting for transfers between devices: 111 us -> 39 us
  Pallas kernels: 0 us -> 65 us
  starting transfers between devices: 0.08 us -> 59.4 us
  other arithmetic: 49.6 us -> 6.22 us
  matrix products: 33.3 us -> 0 us
  between operations: 13.1 us -> 0.83 us
    gather x5 -> x0, local copies, waits for them, and re-layouts: 90.5 us -> none  [the longest x2 67.3 us: shards(): jnp.take(up_weight.reshape(width_part, per_shard, BLK), flat, axis=1)]
    psum x1 -> x0, waiting for transfers between devices: 65.6 us -> none  [shards(): lax.psum(partial_value.astype(jnp.bfloat16), 'dp').astype(jnp.float32)]
    pallas_call x0 -> x24, Pallas kernels: none -> 65 us  [the longest x8 26.6 us: down(): pl.pallas_call(functools.partial(down_kernel, which, row0, len(inits), bi...]
    ppermute x0 -> x35, starting transfers between devices: none -> 59.4 us  [the longest x8 24.2 us: hidden_of(): moved = lax.ppermute(value, 'dp', [(half - 1, half), (half, half - 1)])]
    select_n x4 -> x0, other arithmetic: 46.1 us -> none  [the longest x1 23.1 us: shards(): jnp.take(down_weight.reshape(per_shard, BLK, width_part), flat, axis=0)]
    reduce_scatter x1 -> x0, waiting for transfers between devices: 45 us -> none  [shards(): lax.psum_scatter(terms.astype(jnp.bfloat16), 'tensor', scatter_dimension=...]
    reshape x1 -> x0, local copies, waits for them, and re-layouts: 44.4 us -> none  [shards(): up_weight.reshape(width_part, per_shard, BLK)]
    ppermute x0 -> x35, waiting for transfers between devices: none -> 39 us  [the longest x11 25 us: swap(): return lax.ppermute(value, 'tensor', [(t, t ^ flip) for t in range(4)])]
  transfers between devices with their start and end apart: 3 -> 35, of which waited for: 2 -> 9; matrix products, arithmetic and copies ran while one was open for 58% -> 4% of each run, Pallas kernels for 0% -> 34%
where the time goes in v1:
time: 181 us; the launch traced here: 177 us
  Pallas kernels  65 us (36%)
  starting transfers between devices  59.4 us (33%)
  waiting for transfers between devices  39 us (22%)
  local copies, waits for them, and re-layouts  6.71 us (4%)
  other arithmetic  6.22 us (3%)
    pallas_call x8, Pallas kernels, down(): pl.pallas_call(functools.partial(down_kernel, which, row0, len(inits), bi...  26.6 us
    ppermute x11, waiting for transfers between devices, swap(): return lax.ppermute(value, 'tensor', [(t, t ^ flip) for t in range(4)])  25 us
    ppermute x8, starting transfers between devices, hidden_of(): moved = lax.ppermute(value, 'dp', [(half - 1, half), (half, half - 1)])  24.2 us
    pallas_call x8, Pallas kernels, up(): pl.pallas_call(functools.partial(up_kernel, which, row0), out_shape=jax.S...  23.2 us
    ppermute x8, starting transfers between devices, hidden_of(): lax.ppermute(back, 'dp', [(hop, hop - 1), (depth - 1 - hop, depth - hop)])  18.8 us
    pallas_call x8, Pallas kernels, activate(): pl.pallas_call(functools.partial(body, which), out_shape=jax.ShapeDtypeSt...  15.1 us
    ppermute x8, starting transfers between devices, hidden_of(): lax.ppermute(value, 'dp', [(hop, hop + 1), (depth - 1 - hop, depth - 2 -...  10.6 us
    ppermute x8, waiting for transfers between devices, hidden_of(): lax.ppermute(value, 'dp', [(hop, hop + 1), (depth - 1 - hop, depth - 2 -...  7.78 us
  transfers between devices with their start and end apart: 35, of which 9 were waited for; matrix products, arithmetic and copies ran while one was open for 4% of the time, Pallas kernels for 34%

profile of v1, /device:TPU:12, one launch (start us, length us, event | category | flops | bytes accessed | tf_op | source)
XLA Modules:
  0.0 177.1 jit_solution(14413884074027291887)
XLA Ops:
  0.0 2.2 %fusion = (bf16[128,2048]{1,0:T(8,128)(2,1)S(1)}, bf16[128,2048]{1,0:T(8,128)(2,1)}) fusion(bf16[256,2048]{1,0:T(8,128)(2,1)} %rows.3), kind=kLoop, calls=%fused_computation.8 | loop fusion | bytes 2097152 | tf_op jit(solution)/shard_map/slice | solution.py:252
  4.7 11.7 %collective-permute-done.25.rows = bf16[128,2048]{1,0:T(8,128)(2,1)S(1)} collective-permute-done((bf16[128,2048]{1,0:T(8,128)(2,1)S(1)}, bf16[128,2048]{1,0:T(8,128)(2,1)S(1)}, u32[]{:S(2)}, u32[]{:S(2)}) %collective-permute-start.25) | collective-permute-done | bytes 524320 | tf_op jit(solution)/shard_map/ppermute | solution.py:234
  17.0 2.7 %up.15 = bf16[128,1024]{1,0:T(8,128)(2,1)S(1)} custom-call(s32[8,1,8]{2,1,0:T(1,128)S(1)} %copy-done.5, s32[8,1]{1,0:T(8,128)S(1)} %copy.32.counts, bf16[128,2048]{1,0:T(8,128)(2,1)S(1)} %collective-permute-done.25.rows, bf16[2048,8192]{1,0:T(8,128)(2,1)} %weight.15), custom_call_target="tpu_custom_call" | custom-call | flops 536870912 | bytes 4194304 | tf_op jit(solution)/shard_map/up/pallas_call | solution.py:62
  21.3 6.3 %collective-permute-done.8.rows = bf16[128,2048]{1,0:T(8,128)(2,1)S(1)} collective-permute-done((bf16[128,2048]{1,0:T(8,128)(2,1)}, bf16[128,2048]{1,0:T(8,128)(2,1)S(1)}, u32[]{:S(2)}, u32[]{:S(2)}) %collective-permute-start.8) | collective-permute-done | bytes 524320 | tf_op jit(solution)/shard_map/ppermute | solution.py:234
  27.6 3.4 %up.11 = bf16[128,1024]{1,0:T(8,128)(2,1)S(1)} custom-call(s32[8,1,8]{2,1,0:T(1,128)S(1)} %copy-done.5, s32[8,1]{1,0:T(8,128)S(1)} %copy.32.counts, bf16[128,2048]{1,0:T(8,128)(2,1)S(1)} %collective-permute-done.8.rows, bf16[2048,8192]{1,0:T(8,128)(2,1)} %weight.15), custom_call_target="tpu_custom_call" | custom-call | flops 536870912 | bytes 4194304 | tf_op jit(solution)/shard_map/up/pallas_call | solution.py:62
  32.9 3.5 %collective-permute-start.31 = (bf16[128,1024]{1,0:T(8,128)(2,1)S(1)}, bf16[128,1024]{1,0:T(8,128)(2,1)S(1)}, u32[]{:S(2)}, u32[]{:S(2)}) collective-permute-start(bf16[128,1024]{1,0:T(8,128)(2,1)S(1)} %add_convert_fusion.own), channel_id=1, source_target_pairs={{1,2},{2,1},{5,6},{6,5},{9,10},{10,9},{13,14},{14,13},{17,18},{18,... | collective-permute-start | bytes 786440 | tf_op jit(solution)/shard_map/ppermute | solution.py:241
  36.4 3.8 %collective-permute-done.13 = bf16[128,1024]{1,0:T(8,128)(2,1)S(1)} collective-permute-done((bf16[128,1024]{1,0:T(8,128)(2,1)S(1)}, bf16[128,1024]{1,0:T(8,128)(2,1)S(1)}, u32[]{:S(2)}, u32[]{:S(2)}) %collective-permute-start.13) | collective-permute-done | bytes 262176 | tf_op jit(solution)/shard_map/ppermute | solution.py:239
  41.0 3.5 %collective-permute-start.14 = (bf16[128,1024]{1,0:T(8,128)(2,1)}, bf16[128,1024]{1,0:T(8,128)(2,1)}, u32[]{:S(2)}, u32[]{:S(2)}) collective-permute-start(bf16[128,1024]{1,0:T(8,128)(2,1)} %add_convert_fusion.4.own), channel_id=1, source_target_pairs={{1,2},{2,1},{5,6},{6,5},{9,10},{10,9},{13,14},{14,13},{17,18},{18,... | collective-permute-start | bytes 786440 | tf_op jit(solution)/shard_map/ppermute | solution.py:241
  44.5 3.4 %up.14 = bf16[128,1024]{1,0:T(8,128)(2,1)S(1)} custom-call(s32[8,1,8]{2,1,0:T(1,128)S(1)} %copy-done.5, s32[8,1]{1,0:T(8,128)S(1)} %copy.32.counts, bf16[128,2048]{1,0:T(8,128)(2,1)S(1)} %collective-permute-done.26.rows, bf16[2048,8192]{1,0:T(8,128)(2,1)} %weight.15), custom_call_target="tpu_custom_call" | custom-call | flops 536870912 | bytes 4194304 | tf_op jit(solution)/shard_map/up/pallas_call | solution.py:62
  49.2 2.7 %up.12 = bf16[128,1024]{1,0:T(8,128)(2,1)S(1)} custom-call(s32[8,1,8]{2,1,0:T(1,128)S(1)} %copy-done.5, s32[8,1]{1,0:T(8,128)S(1)} %copy.32.counts, bf16[256,2048]{1,0:T(8,128)(2,1)S(1)} %copy-done, bf16[2048,8192]{1,0:T(8,128)(2,1)} %weight.15), custom_call_target="tpu_custom_call" | custom-call | flops 536870912 | bytes 4194304 | tf_op jit(solution)/shard_map/up/pallas_call | solution.py:62
  51.9 2.7 %up.8 = bf16[128,1024]{1,0:T(8,128)(2,1)S(1)} custom-call(s32[8,1,8]{2,1,0:T(1,128)S(1)} %copy-done.5, s32[8,1]{1,0:T(8,128)S(1)} %copy.32.counts, bf16[256,2048]{1,0:T(8,128)(2,1)S(1)} %copy-done, bf16[2048,8192]{1,0:T(8,128)(2,1)} %weight.15), custom_call_target="tpu_custom_call" | custom-call | flops 536870912 | bytes 4194304 | tf_op jit(solution)/shard_map/up/pallas_call | solution.py:62
  56.6 1.9 %act.15.refs_0_ = bf16[128,1024]{1,0:T(8,128)(2,1)} custom-call(s32[8,1,8]{2,1,0:T(1,128)} %ids.47, s32[8,1]{1,0:T(8,128)} %copy-done.1, bf16[128,1024]{1,0:T(8,128)(2,1)} %copy-done.21, bf16[128,1024]{1,0:T(8,128)(2,1)} %copy-done.25, f32[64,128]{1,0:T(8,128)} %bitcast.4), custom_call_target="tpu_custom_call" | custom-call | flops 131072 | bytes 786432 | tf_op jit(solution)/shard_map/act/pallas_call | solution.py:100
  58.5 6.7 %collective-permute-start.32 = (bf16[128,1024]{1,0:T(8,128)(2,1)}, bf16[128,1024]{1,0:T(8,128)(2,1)}, u32[]{:S(2)}, u32[]{:S(2)}) collective-permute-start(bf16[128,1024]{1,0:T(8,128)(2,1)} %act.15.refs_0_), channel_id=1, source_target_pairs={{1,0},{2,3},{5,4},{6,7},{9,8},{10,11},{13,12},{14,15},{17,16},{18,... | collective-permute-start | bytes 786440 | tf_op jit(solution)/shard_map/ppermute | solution.py:245
  65.2 1.9 %act.11.refs_0_ = bf16[128,1024]{1,0:T(8,128)(2,1)} custom-call(s32[8,1,8]{2,1,0:T(1,128)} %ids.47, s32[8,1]{1,0:T(8,128)} %copy-done.1, bf16[128,1024]{1,0:T(8,128)(2,1)} %add_convert_fusion.4.own, bf16[128,1024]{1,0:T(8,128)(2,1)} %collective-permute-done.14.other, f32[64,128]{1,0:T(8,128)} %bitcast.5), custom_call_target="tpu_custom_call" | custom-call | flops 131072 | bytes 786432 | tf_op jit(solution)/shard_map/act/pallas_call | solution.py:100
  69.0 2.8 %up.10 = bf16[128,1024]{1,0:T(8,128)(2,1)S(1)} custom-call(s32[8,1,8]{2,1,0:T(1,128)S(1)} %copy-done.6, s32[8,1]{1,0:T(8,128)S(1)} %copy-done.2, bf16[128,2048]{1,0:T(8,128)(2,1)} %collective-permute-done.9.rows, bf16[2048,8192]{1,0:T(8,128)(2,1)} %weight.15), custom_call_target="tpu_custom_call" | custom-call | flops 536870912 | bytes 4194304 | tf_op jit(solution)/shard_map/up/pallas_call | solution.py:62
  73.3 2.2 %up.13 = bf16[128,1024]{1,0:T(8,128)(2,1)S(1)} custom-call(s32[8,1,8]{2,1,0:T(1,128)S(1)} %copy-done.6, s32[8,1]{1,0:T(8,128)S(1)} %copy-done.2, bf16[256,2048]{1,0:T(8,128)(2,1)S(1)} %collective-permute-done.3.rows, bf16[2048,8192]{1,0:T(8,128)(2,1)} %weight.15), custom_call_target="tpu_custom_call" | custom-call | flops 536870912 | bytes 4194304 | tf_op jit(solution)/shard_map/up/pallas_call | solution.py:62
  75.5 3.4 %up.9 = bf16[128,1024]{1,0:T(8,128)(2,1)S(1)} custom-call(s32[8,1,8]{2,1,0:T(1,128)S(1)} %copy-done.6, s32[8,1]{1,0:T(8,128)S(1)} %copy-done.2, bf16[256,2048]{1,0:T(8,128)(2,1)S(1)} %collective-permute-done.3.rows, bf16[2048,8192]{1,0:T(8,128)(2,1)} %weight.15), custom_call_target="tpu_custom_call" | custom-call | flops 536870912 | bytes 4194304 | tf_op jit(solution)/shard_map/up/pallas_call | solution.py:62
  82.7 2.7 %down.12 = bf16[128,2048]{1,0:T(8,128)(2,1)S(1)} custom-call(s32[8,1,8]{2,1,0:T(1,128)S(1)} %copy-done.6, s32[8,1]{1,0:T(8,128)S(1)} %copy-done.2, bf16[128,1024]{1,0:T(8,128)(2,1)S(1)} %copy-done.15, bf16[128,1024]{1,0:T(8,128)(2,1)} %collective-permute-done.32.refs_1_, bf16[8192,2048]{1,0:T(8,128)(2,1)} %refs_2_.15), custom_call_target="tpu_custom_call" | custom-call | flops 536870912 | bytes 4194304 | tf_op jit(solution)/shard_map/down/pallas_call | solution.py:191
  85.6 4.0 %collective-permute-done.4 = bf16[128,1024]{1,0:T(8,128)(2,1)S(1)} collective-permute-done((bf16[128,1024]{1,0:T(8,128)(2,1)S(1)}, bf16[128,1024]{1,0:T(8,128)(2,1)S(1)}, u32[]{:S(2)}, u32[]{:S(2)}) %collective-permute-start.4) | collective-permute-done | bytes 262176 | tf_op jit(solution)/shard_map/ppermute | solution.py:239
  89.6 2.3 %collective-permute-start.28 = (bf16[128,1024]{1,0:T(8,128)(2,1)S(1)}, bf16[128,1024]{1,0:T(8,128)(2,1)S(1)}, u32[]{:S(2)}, u32[]{:S(2)}) collective-permute-start(bf16[128,1024]{1,0:T(8,128)(2,1)S(1)} %add_convert_fusion.1.own), channel_id=1, source_target_pairs={{1,2},{2,1},{5,6},{6,5},{9,10},{10,9},{13,14},{14,13},{17,18},{18,... | collective-permute-start | bytes 786440 | tf_op jit(solution)/shard_map/ppermute | solution.py:241
  92.7 3.7 %collective-permute-start.11 = (bf16[128,1024]{1,0:T(8,128)(2,1)S(1)}, bf16[128,1024]{1,0:T(8,128)(2,1)S(1)}, u32[]{:S(2)}, u32[]{:S(2)}) collective-permute-start(bf16[128,1024]{1,0:T(8,128)(2,1)S(1)} %add_convert_fusion.5.own), channel_id=1, source_target_pairs={{1,2},{2,1},{5,6},{6,5},{9,10},{10,9},{13,14},{14,13},{17,18},{18,... | collective-permute-start | bytes 786440 | tf_op jit(solution)/shard_map/ppermute | solution.py:241
  96.5 2.3 %collective-permute-start.5 = (bf16[128,1024]{1,0:T(8,128)(2,1)}, bf16[128,1024]{1,0:T(8,128)(2,1)S(1)}, u32[]{:S(2)}, u32[]{:S(2)}) collective-permute-start(bf16[128,1024]{1,0:T(8,128)(2,1)} %add_convert_fusion.6.own), channel_id=1, source_target_pairs={{1,2},{2,1},{5,6},{6,5},{9,10},{10,9},{13,14},{14,13},{17,18},{18,... | collective-permute-start | bytes 786440 | tf_op jit(solution)/shard_map/ppermute | solution.py:241
  98.9 3.5 %collective-permute-start.22 = (bf16[128,1024]{1,0:T(8,128)(2,1)S(1)}, bf16[128,1024]{1,0:T(8,128)(2,1)S(1)}, u32[]{:S(2)}, u32[]{:S(2)}) collective-permute-start(bf16[128,1024]{1,0:T(8,128)(2,1)S(1)} %add_convert_fusion.2.own), channel_id=1, source_target_pairs={{1,2},{2,1},{5,6},{6,5},{9,10},{10,9},{13,14},{14,13},{17,18},{18,... | collective-permute-start | bytes 786440 | tf_op jit(solution)/shard_map/ppermute | solution.py:241
  102.4 1.7 add_convert_fusion.3.own
  106.3 2.2 %collective-permute-start.19 = (bf16[128,1024]{1,0:T(8,128)(2,1)}, bf16[128,1024]{1,0:T(8,128)(2,1)}, u32[]{:S(2)}, u32[]{:S(2)}) collective-permute-start(bf16[128,1024]{1,0:T(8,128)(2,1)} %add_convert_fusion.3.own), channel_id=1, source_target_pairs={{1,2},{2,1},{5,6},{6,5},{9,10},{10,9},{13,14},{14,13},{17,18},{18,... | collective-permute-start | bytes 786440 | tf_op jit(solution)/shard_map/ppermute | solution.py:241
  108.6 3.3 %down.9 = bf16[128,2048]{1,0:T(8,128)(2,1)S(1)} custom-call(s32[8,1,8]{2,1,0:T(1,128)S(1)} %copy-done.6, s32[8,1]{1,0:T(8,128)S(1)} %copy-done.2, bf16[128,1024]{1,0:T(8,128)(2,1)S(1)} %copy-done.9, bf16[128,1024]{1,0:T(8,128)(2,1)S(1)} %collective-permute-done.15.refs_1_, bf16[8192,2048]{1,0:T(8,128)(2,1)} %refs_2_.15), custom_call_target="tpu_custom_call" | custom-call | flops 536870912 | bytes 4194304 | tf_op jit(solution)/shard_map/down/pallas_call | solution.py:191
  111.9 4.3 %collective-permute-done.22.other = bf16[128,1024]{1,0:T(8,128)(2,1)S(1)} collective-permute-done((bf16[128,1024]{1,0:T(8,128)(2,1)S(1)}, bf16[128,1024]{1,0:T(8,128)(2,1)S(1)}, u32[]{:S(2)}, u32[]{:S(2)}) %collective-permute-start.22) | collective-permute-done | bytes 262176 | tf_op jit(solution)/shard_map/ppermute | solution.py:241
  116.9 1.9 %act.13.refs_0_ = bf16[128,1024]{1,0:T(8,128)(2,1)} custom-call(s32[8,1,8]{2,1,0:T(1,128)} %ids.47, s32[8,1]{1,0:T(8,128)} %copy-done.1, bf16[128,1024]{1,0:T(8,128)(2,1)} %copy-done.20, bf16[128,1024]{1,0:T(8,128)(2,1)} %copy-done.26, f32[64,128]{1,0:T(8,128)} %bitcast.6), custom_call_target="tpu_custom_call" | custom-call | flops 131072 | bytes 786432 | tf_op jit(solution)/shard_map/act/pallas_call | solution.py:100
  120.1 1.9 %act.14.refs_0_ = bf16[128,1024]{1,0:T(8,128)(2,1)} custom-call(s32[8,1,8]{2,1,0:T(1,128)} %ids.47, s32[8,1]{1,0:T(8,128)} %copy-done.1, bf16[128,1024]{1,0:T(8,128)(2,1)} %copy-done.18, bf16[128,1024]{1,0:T(8,128)(2,1)} %copy-done.22, f32[64,128]{1,0:T(8,128)} %bitcast.7), custom_call_target="tpu_custom_call" | custom-call | flops 131072 | bytes 786432 | tf_op jit(solution)/shard_map/act/pallas_call | solution.py:100
  122.0 1.9 %act.10.refs_0_ = bf16[128,1024]{1,0:T(8,128)(2,1)} custom-call(s32[8,1,8]{2,1,0:T(1,128)} %ids.47, s32[8,1]{1,0:T(8,128)} %copy-done.1, bf16[128,1024]{1,0:T(8,128)(2,1)} %copy-done.19, bf16[128,1024]{1,0:T(8,128)(2,1)} %copy-done.23, f32[64,128]{1,0:T(8,128)} %bitcast.8), custom_call_target="tpu_custom_call" | custom-call | flops 131072 | bytes 786432 | tf_op jit(solution)/shard_map/act/pallas_call | solution.py:100
  124.0 1.9 %act.9.refs_0_ = bf16[128,1024]{1,0:T(8,128)(2,1)} custom-call(s32[8,1,8]{2,1,0:T(1,128)} %ids.47, s32[8,1]{1,0:T(8,128)} %copy-done.1, bf16[128,1024]{1,0:T(8,128)(2,1)} %add_convert_fusion.6.own, bf16[128,1024]{1,0:T(8,128)(2,1)} %copy-done.24, f32[64,128]{1,0:T(8,128)} %bitcast.9), custom_call_target="tpu_custom_call" | custom-call | flops 131072 | bytes 786432 | tf_op jit(solution)/shard_map/act/pallas_call | solution.py:100
  125.9 2.0 %collective-permute-start.29 = (bf16[128,1024]{1,0:T(8,128)(2,1)}, bf16[128,1024]{1,0:T(8,128)(2,1)}, u32[]{:S(2)}, u32[]{:S(2)}) collective-permute-start(bf16[128,1024]{1,0:T(8,128)(2,1)} %act.14.refs_0_), channel_id=1, source_target_pairs={{1,0},{2,3},{5,4},{6,7},{9,8},{10,11},{13,12},{14,15},{17,16},{18,... | collective-permute-start | bytes 786440 | tf_op jit(solution)/shard_map/ppermute | solution.py:245
  127.9 2.0 %collective-permute-start.12 = (bf16[128,1024]{1,0:T(8,128)(2,1)}, bf16[128,1024]{1,0:T(8,128)(2,1)}, u32[]{:S(2)}, u32[]{:S(2)}) collective-permute-start(bf16[128,1024]{1,0:T(8,128)(2,1)} %act.10.refs_0_), channel_id=1, source_target_pairs={{1,0},{2,3},{5,4},{6,7},{9,8},{10,11},{13,12},{14,15},{17,16},{18,... | collective-permute-start | bytes 786440 | tf_op jit(solution)/shard_map/ppermute | solution.py:245
  129.9 2.0 %collective-permute-start.6 = (bf16[128,1024]{1,0:T(8,128)(2,1)}, bf16[128,1024]{1,0:T(8,128)(2,1)}, u32[]{:S(2)}, u32[]{:S(2)}) collective-permute-start(bf16[128,1024]{1,0:T(8,128)(2,1)} %act.9.refs_0_), channel_id=1, source_target_pairs={{1,0},{2,3},{5,4},{6,7},{9,8},{10,11},{13,12},{14,15},{17,16},{18,... | collective-permute-start | bytes 786440 | tf_op jit(solution)/shard_map/ppermute | solution.py:245
  131.9 1.7 add_convert_fusion.7.own
  133.6 3.2 %collective-permute-start.1 = (bf16[128,1024]{1,0:T(8,128)(2,1)}, bf16[128,1024]{1,0:T(8,128)(2,1)}, u32[]{:S(2)}, u32[]{:S(2)}) collective-permute-start(bf16[128,1024]{1,0:T(8,128)(2,1)} %add_convert_fusion.7.own), channel_id=1, source_target_pairs={{1,2},{2,1},{5,6},{6,5},{9,10},{10,9},{13,14},{14,13},{17,18},{18,... | collective-permute-start | bytes 786440 | tf_op jit(solution)/shard_map/ppermute | solution.py:241
  136.8 1.9 %act.12.refs_0_ = bf16[128,1024]{1,0:T(8,128)(2,1)} custom-call(s32[8,1,8]{2,1,0:T(1,128)} %ids.47, s32[8,1]{1,0:T(8,128)} %copy-done.1, bf16[128,1024]{1,0:T(8,128)(2,1)} %add_convert_fusion.3.own, bf16[128,1024]{1,0:T(8,128)(2,1)} %collective-permute-done.19.other, f32[64,128]{1,0:T(8,128)} %bitcast.10), custom_call_target="tpu_custom_call" | custom-call | flops 131072 | bytes 786432 | tf_op jit(solution)/shard_map/act/pallas_call | solution.py:100
  139.7 2.3 %down.11 = bf16[128,2048]{1,0:T(8,128)(2,1)S(1)} custom-call(s32[8,1,8]{2,1,0:T(1,128)S(1)} %copy-done.7, s32[8,1]{1,0:T(8,128)S(1)} %copy-done.3, bf16[128,1024]{1,0:T(8,128)(2,1)S(1)} %copy-done.14, bf16[128,1024]{1,0:T(8,128)(2,1)S(1)} %collective-permute-done.23.refs_1_, bf16[8192,2048]{1,0:T(8,128)(2,1)} %refs_2_.15), custom_call_target="tpu_custom_call" | custom-call | flops 536870912 | bytes 4194304 | tf_op jit(solution)/shard_map/down/pallas_call | solution.py:191
  142.0 2.1 %collective-permute-start.20 = (bf16[128,1024]{1,0:T(8,128)(2,1)S(1)}, bf16[128,1024]{1,0:T(8,128)(2,1)}, u32[]{:S(2)}, u32[]{:S(2)}) collective-permute-start(bf16[128,1024]{1,0:T(8,128)(2,1)S(1)} %copy-done.12), channel_id=1, source_target_pairs={{1,0},{2,3},{5,4},{6,7},{9,8},{10,11},{13,12},{14,15},{17,16},{18,... | collective-permute-start | bytes 786440 | tf_op jit(solution)/shard_map/ppermute | solution.py:245
  144.1 3.3 %down.13 = bf16[128,2048]{1,0:T(8,128)(2,1)S(1)} custom-call(s32[8,1,8]{2,1,0:T(1,128)S(1)} %copy-done.7, s32[8,1]{1,0:T(8,128)S(1)} %copy-done.3, bf16[128,1024]{1,0:T(8,128)(2,1)S(1)} %copy-done.13, bf16[128,1024]{1,0:T(8,128)(2,1)} %collective-permute-done.29.refs_1_, bf16[8192,2048]{1,0:T(8,128)(2,1)} %refs_2_.15, ...), custom_call_target="tpu_custom_call" | custom-call | flops 536870912 | bytes 4194304 | tf_op jit(solution)/shard_map/down/pallas_call | solution.py:191
  147.5 2.2 %collective-permute-start.34 = (bf16[128,2048]{1,0:T(8,128)(2,1)S(1)}, bf16[128,2048]{1,0:T(8,128)(2,1)S(1)}, u32[]{:S(2)}, u32[]{:S(2)}) collective-permute-start(bf16[128,2048]{1,0:T(8,128)(2,1)S(1)} %down.13), channel_id=1, source_target_pairs={{0,8},{4,12},{8,0},{12,4},{1,9},{5,13},{9,1},{13,5},{2,10},{6,14},... | collective-permute-start | bytes 1572872 | tf_op jit(solution)/shard_map/ppermute | solution.py:234
  149.7 2.7 %down.10 = bf16[128,2048]{1,0:T(8,128)(2,1)S(1)} custom-call(s32[8,1,8]{2,1,0:T(1,128)S(1)} %copy-done.7, s32[8,1]{1,0:T(8,128)S(1)} %copy-done.3, bf16[128,1024]{1,0:T(8,128)(2,1)S(1)} %copy-done.11, bf16[128,1024]{1,0:T(8,128)(2,1)} %collective-permute-done.12.refs_1_, bf16[8192,2048]{1,0:T(8,128)(2,1)} %refs_2_.15, ...), custom_call_target="tpu_custom_call" | custom-call | flops 536870912 | bytes 4194304 | tf_op jit(solution)/shard_map/down/pallas_call | solution.py:191
  153.2 4.1 %down.8 = bf16[128,2048]{1,0:T(8,128)(2,1)} custom-call(s32[8,1,8]{2,1,0:T(1,128)S(1)} %copy-done.7, s32[8,1]{1,0:T(8,128)S(1)} %copy-done.3, bf16[128,1024]{1,0:T(8,128)(2,1)S(1)} %copy-done.10, bf16[128,1024]{1,0:T(8,128)(2,1)} %collective-permute-done.6.refs_1_, bf16[8192,2048]{1,0:T(8,128)(2,1)} %refs_2_.15), custom_call_target="tpu_custom_call" | custom-call | flops 536870912 | bytes 4194304 | tf_op jit(solution)/shard_map/down/pallas_call | solution.py:191
  157.4 1.9 %act.8.refs_0_ = bf16[128,1024]{1,0:T(8,128)(2,1)} custom-call(s32[8,1,8]{2,1,0:T(1,128)} %ids.47, s32[8,1]{1,0:T(8,128)} %copy-done.1, bf16[128,1024]{1,0:T(8,128)(2,1)} %add_convert_fusion.7.own, bf16[128,1024]{1,0:T(8,128)(2,1)} %collective-permute-done.1.other, f32[64,128]{1,0:T(8,128)} %bitcast.11), custom_call_target="tpu_custom_call" | custom-call | flops 131072 | bytes 786432 | tf_op jit(solution)/shard_map/act/pallas_call | solution.py:100
  160.8 1.7 collective-permute-done.34.refs_4_
  162.5 4.1 %down.14.refs_6_ = f32[256,2048]{1,0:T(8,128)} custom-call(s32[8,1,8]{2,1,0:T(1,128)S(1)} %copy-done.8, s32[8,1]{1,0:T(8,128)S(1)} %copy-done.4, bf16[128,1024]{1,0:T(8,128)(2,1)S(1)} %copy-done.12, bf16[128,1024]{1,0:T(8,128)(2,1)} %collective-permute-done.20.refs_1_, bf16[8192,2048]{1,0:T(8,128)(2,1)} %refs_2_.15, ...), custom_call_target="tpu_custom_call" | custom-call | flops 536870912 | bytes 4194304 | tf_op jit(solution)/shard_map/down/pallas_call | solution.py:191
  167.6 5.3 %collective-permute-done.17.refs_4_ = bf16[128,2048]{1,0:T(8,128)(2,1)S(1)} collective-permute-done((bf16[128,2048]{1,0:T(8,128)(2,1)S(1)}, bf16[128,2048]{1,0:T(8,128)(2,1)S(1)}, u32[]{:S(2)}, u32[]{:S(2)}) %collective-permute-start.17) | collective-permute-done | bytes 524320 | tf_op jit(solution)/shard_map/ppermute | solution.py:234
  172.9 4.1 %down.15 = f32[256,2048]{1,0:T(8,128)} custom-call(s32[8,1,8]{2,1,0:T(1,128)S(1)} %copy-done.8, s32[8,1]{1,0:T(8,128)S(1)} %copy-done.4, bf16[128,1024]{1,0:T(8,128)(2,1)S(1)} %copy-done.16, bf16[128,1024]{1,0:T(8,128)(2,1)S(1)} %collective-permute-done.2.refs_1_, bf16[8192,2048]{1,0:T(8,128)(2,1)} %refs_2_.15, ...), custom_call_target="tpu_custom_call", output_to_operand_aliasing={{}: (8, {})} | custom-call | flops 536870912 | bytes 4194304 | tf_op jit(solution)/shard_map/down/pallas_call | solution.py:191
  (110 shorter events, 27.4 us)
Async XLA Ops:
  0.0 21.0 %copy-start = (bf16[256,2048]{1,0:T(8,128)(2,1)S(1)}, bf16[256,2048]{1,0:T(8,128)(2,1)}, u32[]{:S(2)}) copy-start(bf16[256,2048]{1,0:T(8,128)(2,1)} %rows.3) | copy-start | bytes 3145732
  2.2 14.2 %collective-permute-start.25 = (bf16[128,2048]{1,0:T(8,128)(2,1)S(1)}, bf16[128,2048]{1,0:T(8,128)(2,1)S(1)}, u32[]{:S(2)}, u32[]{:S(2)}) collective-permute-start(bf16[128,2048]{1,0:T(8,128)(2,1)S(1)} %get-tuple-element.5), channel_id=1, source_target_pairs={{0,12},{4,8},{8,4},{12,0},{1,13},{5,9},{9,5},{13,1},{2,14},{6,10},... | collective-permute-start | bytes 1572872 | tf_op jit(solution)/shard_map/ppermute | solution.py:234
  3.1 24.5 %collective-permute-start.8 = (bf16[128,2048]{1,0:T(8,128)(2,1)}, bf16[128,2048]{1,0:T(8,128)(2,1)S(1)}, u32[]{:S(2)}, u32[]{:S(2)}) collective-permute-start(bf16[128,2048]{1,0:T(8,128)(2,1)} %get-tuple-element.6), channel_id=1, source_target_pairs={{0,12},{4,8},{8,4},{12,0},{1,13},{5,9},{9,5},{13,1},{2,14},{6,10},... | collective-permute-start | bytes 1572872 | tf_op jit(solution)/shard_map/ppermute | solution.py:234
  4.7 47.2 %copy-start.1 = (s32[8,1]{1,0:T(8,128)}, s32[8,1]{1,0:T(8,128)S(1)}, u32[]{:S(2)}) copy-start(s32[8,1]{1,0:T(8,128)S(1)} %copy.32.counts) | copy-start | bytes 100
  19.7 13.1 %collective-permute-start.30 = (bf16[128,1024]{1,0:T(8,128)(2,1)S(1)}, bf16[128,1024]{1,0:T(8,128)(2,1)S(1)}, u32[]{:S(2)}, u32[]{:S(2)}) collective-permute-start(bf16[128,1024]{1,0:T(8,128)(2,1)S(1)} %up.15), channel_id=1, source_target_pairs={{0,1},{3,2},{4,5},{7,6},{8,9},{11,10},{12,13},{15,14},{16,17},{19,... | collective-permute-start | bytes 786440 | tf_op jit(solution)/shard_map/ppermute | solution.py:239
  21.0 50.8 %collective-permute-start.3 = (bf16[256,2048]{1,0:T(8,128)(2,1)S(1)}, bf16[256,2048]{1,0:T(8,128)(2,1)S(1)}, u32[]{:S(2)}, u32[]{:S(2)}) collective-permute-start(bf16[256,2048]{1,0:T(8,128)(2,1)S(1)} %copy-done), channel_id=1, source_target_pairs={{0,4},{4,0},{8,12},{12,8},{1,5},{5,1},{9,13},{13,9},{2,6},{6,2},{1... | collective-permute-start | bytes 3145736 | tf_op jit(solution)/shard_map/ppermute | solution.py:234
  31.0 9.3 %collective-permute-start.13 = (bf16[128,1024]{1,0:T(8,128)(2,1)S(1)}, bf16[128,1024]{1,0:T(8,128)(2,1)S(1)}, u32[]{:S(2)}, u32[]{:S(2)}) collective-permute-start(bf16[128,1024]{1,0:T(8,128)(2,1)S(1)} %up.11), channel_id=1, source_target_pairs={{0,1},{3,2},{4,5},{7,6},{8,9},{11,10},{12,13},{15,14},{16,17},{19,... | collective-permute-start | bytes 786440 | tf_op jit(solution)/shard_map/ppermute | solution.py:239
  32.3 12.2 %collective-permute-start.26 = (bf16[128,2048]{1,0:T(8,128)(2,1)S(1)}, bf16[128,2048]{1,0:T(8,128)(2,1)S(1)}, u32[]{:S(2)}, u32[]{:S(2)}) collective-permute-start(bf16[128,2048]{1,0:T(8,128)(2,1)S(1)} %collective-permute-done.25.rows), channel_id=1, source_target_pairs={{0,4},{4,0},{8,12},{12,8},{1,5},{5,1},{9,13},{13,9},{2,6},{6,2},{1... | collective-permute-start | bytes 1572872 | tf_op jit(solution)/shard_map/ppermute | solution.py:234
  32.3 34.7 %collective-permute-start.9 = (bf16[128,2048]{1,0:T(8,128)(2,1)S(1)}, bf16[128,2048]{1,0:T(8,128)(2,1)}, u32[]{:S(2)}, u32[]{:S(2)}) collective-permute-start(bf16[128,2048]{1,0:T(8,128)(2,1)S(1)} %collective-permute-done.8.rows), channel_id=1, source_target_pairs={{0,4},{4,0},{8,12},{12,8},{1,5},{5,1},{9,13},{13,9},{2,6},{6,2},{1... | collective-permute-start | bytes 1572872 | tf_op jit(solution)/shard_map/ppermute | solution.py:234
  32.9 19.0 %copy-start.21 = (bf16[128,1024]{1,0:T(8,128)(2,1)}, bf16[128,1024]{1,0:T(8,128)(2,1)S(1)}, u32[]{:S(2)}) copy-start(bf16[128,1024]{1,0:T(8,128)(2,1)S(1)} %add_convert_fusion.own) | copy-start | bytes 786436
  32.9 21.7 %collective-permute-start.31 = (bf16[128,1024]{1,0:T(8,128)(2,1)S(1)}, bf16[128,1024]{1,0:T(8,128)(2,1)S(1)}, u32[]{:S(2)}, u32[]{:S(2)}) collective-permute-start(bf16[128,1024]{1,0:T(8,128)(2,1)S(1)} %add_convert_fusion.own), channel_id=1, source_target_pairs={{1,2},{2,1},{5,6},{6,5},{9,10},{10,9},{13,14},{14,13},{17,18},{18,... | collective-permute-start | bytes 786440 | tf_op jit(solution)/shard_map/ppermute | solution.py:241
  41.0 17.5 %collective-permute-start.14 = (bf16[128,1024]{1,0:T(8,128)(2,1)}, bf16[128,1024]{1,0:T(8,128)(2,1)}, u32[]{:S(2)}, u32[]{:S(2)}) collective-permute-start(bf16[128,1024]{1,0:T(8,128)(2,1)} %add_convert_fusion.4.own), channel_id=1, source_target_pairs={{1,2},{2,1},{5,6},{6,5},{9,10},{10,9},{13,14},{14,13},{17,18},{18,... | collective-permute-start | bytes 786440 | tf_op jit(solution)/shard_map/ppermute | solution.py:241
  47.9 20.5 %copy-start.6 = (s32[8,1,8]{2,1,0:T(1,128)S(1)}, s32[8,1,8]{2,1,0:T(1,128)}, u32[]{:S(2)}) copy-start(s32[8,1,8]{2,1,0:T(1,128)} %ids.47) | copy-start | bytes 772
  47.9 31.0 %collective-permute-start.27 = (bf16[128,1024]{1,0:T(8,128)(2,1)S(1)}, bf16[128,1024]{1,0:T(8,128)(2,1)}, u32[]{:S(2)}, u32[]{:S(2)}) collective-permute-start(bf16[128,1024]{1,0:T(8,128)(2,1)S(1)} %up.14), channel_id=1, source_target_pairs={{0,1},{3,2},{4,5},{7,6},{8,9},{11,10},{12,13},{15,14},{16,17},{19,... | collective-permute-start | bytes 786440 | tf_op jit(solution)/shard_map/ppermute | solution.py:239
  55.3 41.2 %collective-permute-start.18 = (bf16[128,1024]{1,0:T(8,128)(2,1)S(1)}, bf16[128,1024]{1,0:T(8,128)(2,1)}, u32[]{:S(2)}, u32[]{:S(2)}) collective-permute-start(bf16[128,1024]{1,0:T(8,128)(2,1)S(1)} %up.12), channel_id=1, source_target_pairs={{0,1},{3,2},{4,5},{7,6},{8,9},{11,10},{12,13},{15,14},{16,17},{19,... | collective-permute-start | bytes 786440 | tf_op jit(solution)/shard_map/ppermute | solution.py:239
  58.5 22.8 %collective-permute-start.32 = (bf16[128,1024]{1,0:T(8,128)(2,1)}, bf16[128,1024]{1,0:T(8,128)(2,1)}, u32[]{:S(2)}, u32[]{:S(2)}) collective-permute-start(bf16[128,1024]{1,0:T(8,128)(2,1)} %act.15.refs_0_), channel_id=1, source_target_pairs={{1,0},{2,3},{5,4},{6,7},{9,8},{10,11},{13,12},{14,15},{17,16},{18,... | collective-permute-start | bytes 786440 | tf_op jit(solution)/shard_map/ppermute | solution.py:245
  67.1 31.8 %collective-permute-start.15 = (bf16[128,1024]{1,0:T(8,128)(2,1)}, bf16[128,1024]{1,0:T(8,128)(2,1)S(1)}, u32[]{:S(2)}, u32[]{:S(2)}) collective-permute-start(bf16[128,1024]{1,0:T(8,128)(2,1)} %act.11.refs_0_), channel_id=1, source_target_pairs={{1,0},{2,3},{5,4},{6,7},{9,8},{10,11},{13,12},{14,15},{17,16},{18,... | collective-permute-start | bytes 786440 | tf_op jit(solution)/shard_map/ppermute | solution.py:245
  71.9 13.6 %collective-permute-start.10 = (bf16[128,1024]{1,0:T(8,128)(2,1)S(1)}, bf16[128,1024]{1,0:T(8,128)(2,1)S(1)}, u32[]{:S(2)}, u32[]{:S(2)}) collective-permute-start(bf16[128,1024]{1,0:T(8,128)(2,1)S(1)} %up.10), channel_id=1, source_target_pairs={{0,1},{3,2},{4,5},{7,6},{8,9},{11,10},{12,13},{15,14},{16,17},{19,... | collective-permute-start | bytes 786440 | tf_op jit(solution)/shard_map/ppermute | solution.py:239
  75.5 33.0 %copy-start.9 = (bf16[128,1024]{1,0:T(8,128)(2,1)S(1)}, bf16[128,1024]{1,0:T(8,128)(2,1)}, u32[]{:S(2)}) copy-start(bf16[128,1024]{1,0:T(8,128)(2,1)} %act.11.refs_0_) | copy-start | bytes 786436
  78.9 10.7 %collective-permute-start.4 = (bf16[128,1024]{1,0:T(8,128)(2,1)S(1)}, bf16[128,1024]{1,0:T(8,128)(2,1)S(1)}, u32[]{:S(2)}, u32[]{:S(2)}) collective-permute-start(bf16[128,1024]{1,0:T(8,128)(2,1)S(1)} %up.9), channel_id=1, source_target_pairs={{0,1},{3,2},{4,5},{7,6},{8,9},{11,10},{12,13},{15,14},{16,17},{19,... | collective-permute-start | bytes 786440 | tf_op jit(solution)/shard_map/ppermute | solution.py:239
  81.2 30.7 %copy-start.18 = (bf16[128,1024]{1,0:T(8,128)(2,1)}, bf16[128,1024]{1,0:T(8,128)(2,1)S(1)}, u32[]{:S(2)}) copy-start(bf16[128,1024]{1,0:T(8,128)(2,1)S(1)} %add_convert_fusion.1.own) | copy-start | bytes 786436
  81.3 57.5 %copy-start.3 = (s32[8,1]{1,0:T(8,128)S(1)}, s32[8,1]{1,0:T(8,128)}, u32[]{:S(2)}) copy-start(s32[8,1]{1,0:T(8,128)} %copy-done.1) | copy-start | bytes 100
  81.3 57.5 %copy-start.7 = (s32[8,1,8]{2,1,0:T(1,128)S(1)}, s32[8,1,8]{2,1,0:T(1,128)}, u32[]{:S(2)}) copy-start(s32[8,1,8]{2,1,0:T(1,128)} %ids.47) | copy-start | bytes 772
  81.3 11.4 %collective-permute-start.21 = (bf16[128,1024]{1,0:T(8,128)(2,1)S(1)}, bf16[128,1024]{1,0:T(8,128)(2,1)S(1)}, u32[]{:S(2)}, u32[]{:S(2)}) collective-permute-start(bf16[128,1024]{1,0:T(8,128)(2,1)S(1)} %up.13), channel_id=1, source_target_pairs={{0,1},{3,2},{4,5},{7,6},{8,9},{11,10},{12,13},{15,14},{16,17},{19,... | collective-permute-start | bytes 786440 | tf_op jit(solution)/shard_map/ppermute | solution.py:239
  85.5 44.4 %collective-permute-start.33 = (bf16[128,2048]{1,0:T(8,128)(2,1)S(1)}, bf16[128,2048]{1,0:T(8,128)(2,1)S(1)}, u32[]{:S(2)}, u32[]{:S(2)}) collective-permute-start(bf16[128,2048]{1,0:T(8,128)(2,1)S(1)} %down.12), channel_id=1, source_target_pairs={{0,4},{4,0},{8,12},{12,8},{1,5},{5,1},{9,13},{13,9},{2,6},{6,2},{1... | collective-permute-start | bytes 1572872 | tf_op jit(solution)/shard_map/ppermute | solution.py:234
  85.6 33.2 %copy-start.19 = (bf16[128,1024]{1,0:T(8,128)(2,1)}, bf16[128,1024]{1,0:T(8,128)(2,1)S(1)}, u32[]{:S(2)}) copy-start(bf16[128,1024]{1,0:T(8,128)(2,1)S(1)} %add_convert_fusion.5.own) | copy-start | bytes 786436
  89.6 14.5 %collective-permute-start.28 = (bf16[128,1024]{1,0:T(8,128)(2,1)S(1)}, bf16[128,1024]{1,0:T(8,128)(2,1)S(1)}, u32[]{:S(2)}, u32[]{:S(2)}) collective-permute-start(bf16[128,1024]{1,0:T(8,128)(2,1)S(1)} %add_convert_fusion.1.own), channel_id=1, source_target_pairs={{1,2},{2,1},{5,6},{6,5},{9,10},{10,9},{13,14},{14,13},{17,18},{18,... | collective-permute-start | bytes 786440 | tf_op jit(solution)/shard_map/ppermute | solution.py:241
  92.7 13.6 %collective-permute-start.11 = (bf16[128,1024]{1,0:T(8,128)(2,1)S(1)}, bf16[128,1024]{1,0:T(8,128)(2,1)S(1)}, u32[]{:S(2)}, u32[]{:S(2)}) collective-permute-start(bf16[128,1024]{1,0:T(8,128)(2,1)S(1)} %add_convert_fusion.5.own), channel_id=1, source_target_pairs={{1,2},{2,1},{5,6},{6,5},{9,10},{10,9},{13,14},{14,13},{17,18},{18,... | collective-permute-start | bytes 786440 | tf_op jit(solution)/shard_map/ppermute | solution.py:241
  96.5 15.5 %copy-start.20 = (bf16[128,1024]{1,0:T(8,128)(2,1)}, bf16[128,1024]{1,0:T(8,128)(2,1)S(1)}, u32[]{:S(2)}) copy-start(bf16[128,1024]{1,0:T(8,128)(2,1)S(1)} %add_convert_fusion.2.own) | copy-start | bytes 786436
  96.5 22.3 %collective-permute-start.5 = (bf16[128,1024]{1,0:T(8,128)(2,1)}, bf16[128,1024]{1,0:T(8,128)(2,1)S(1)}, u32[]{:S(2)}, u32[]{:S(2)}) collective-permute-start(bf16[128,1024]{1,0:T(8,128)(2,1)} %add_convert_fusion.6.own), channel_id=1, source_target_pairs={{1,2},{2,1},{5,6},{6,5},{9,10},{10,9},{13,14},{14,13},{17,18},{18,... | collective-permute-start | bytes 786440 | tf_op jit(solution)/shard_map/ppermute | solution.py:241
  98.9 17.3 %collective-permute-start.22 = (bf16[128,1024]{1,0:T(8,128)(2,1)S(1)}, bf16[128,1024]{1,0:T(8,128)(2,1)S(1)}, u32[]{:S(2)}, u32[]{:S(2)}) collective-permute-start(bf16[128,1024]{1,0:T(8,128)(2,1)S(1)} %add_convert_fusion.2.own), channel_id=1, source_target_pairs={{1,2},{2,1},{5,6},{6,5},{9,10},{10,9},{13,14},{14,13},{17,18},{18,... | collective-permute-start | bytes 786440 | tf_op jit(solution)/shard_map/ppermute | solution.py:241
  104.1 21.8 %collective-permute-start = (bf16[128,1024]{1,0:T(8,128)(2,1)S(1)}, bf16[128,1024]{1,0:T(8,128)(2,1)}, u32[]{:S(2)}, u32[]{:S(2)}) collective-permute-start(bf16[128,1024]{1,0:T(8,128)(2,1)S(1)} %up.8), channel_id=1, source_target_pairs={{0,1},{3,2},{4,5},{7,6},{8,9},{11,10},{12,13},{15,14},{16,17},{19,... | collective-permute-start | bytes 786440 | tf_op jit(solution)/shard_map/ppermute | solution.py:239
  106.3 21.5 %collective-permute-start.19 = (bf16[128,1024]{1,0:T(8,128)(2,1)}, bf16[128,1024]{1,0:T(8,128)(2,1)}, u32[]{:S(2)}, u32[]{:S(2)}) collective-permute-start(bf16[128,1024]{1,0:T(8,128)(2,1)} %add_convert_fusion.3.own), channel_id=1, source_target_pairs={{1,2},{2,1},{5,6},{6,5},{9,10},{10,9},{13,14},{14,13},{17,18},{18,... | collective-permute-start | bytes 786440 | tf_op jit(solution)/shard_map/ppermute | solution.py:241
  116.9 30.6 %collective-permute-start.16 = (bf16[128,2048]{1,0:T(8,128)(2,1)S(1)}, bf16[128,2048]{1,0:T(8,128)(2,1)S(1)}, u32[]{:S(2)}, u32[]{:S(2)}) collective-permute-start(bf16[128,2048]{1,0:T(8,128)(2,1)S(1)} %down.9), channel_id=1, source_target_pairs={{0,4},{4,0},{8,12},{12,8},{1,5},{5,1},{9,13},{13,9},{2,6},{6,2},{1... | collective-permute-start | bytes 1572872 | tf_op jit(solution)/shard_map/ppermute | solution.py:234
  118.8 14.8 %collective-permute-start.23 = (bf16[128,1024]{1,0:T(8,128)(2,1)}, bf16[128,1024]{1,0:T(8,128)(2,1)S(1)}, u32[]{:S(2)}, u32[]{:S(2)}) collective-permute-start(bf16[128,1024]{1,0:T(8,128)(2,1)} %act.13.refs_0_), channel_id=1, source_target_pairs={{1,0},{2,3},{5,4},{6,7},{9,8},{10,11},{13,12},{14,15},{17,16},{18,... | collective-permute-start | bytes 786440 | tf_op jit(solution)/shard_map/ppermute | solution.py:245
  122.0 22.1 %copy-start.13 = (bf16[128,1024]{1,0:T(8,128)(2,1)S(1)}, bf16[128,1024]{1,0:T(8,128)(2,1)}, u32[]{:S(2)}) copy-start(bf16[128,1024]{1,0:T(8,128)(2,1)} %act.14.refs_0_) | copy-start | bytes 786436
  125.9 16.1 %collective-permute-start.29 = (bf16[128,1024]{1,0:T(8,128)(2,1)}, bf16[128,1024]{1,0:T(8,128)(2,1)}, u32[]{:S(2)}, u32[]{:S(2)}) collective-permute-start(bf16[128,1024]{1,0:T(8,128)(2,1)} %act.14.refs_0_), channel_id=1, source_target_pairs={{1,0},{2,3},{5,4},{6,7},{9,8},{10,11},{13,12},{14,15},{17,16},{18,... | collective-permute-start | bytes 786440 | tf_op jit(solution)/shard_map/ppermute | solution.py:245
  127.9 21.8 %collective-permute-start.12 = (bf16[128,1024]{1,0:T(8,128)(2,1)}, bf16[128,1024]{1,0:T(8,128)(2,1)}, u32[]{:S(2)}, u32[]{:S(2)}) collective-permute-start(bf16[128,1024]{1,0:T(8,128)(2,1)} %act.10.refs_0_), channel_id=1, source_target_pairs={{1,0},{2,3},{5,4},{6,7},{9,8},{10,11},{13,12},{14,15},{17,16},{18,... | collective-permute-start | bytes 786440 | tf_op jit(solution)/shard_map/ppermute | solution.py:245
  129.9 22.6 %collective-permute-start.6 = (bf16[128,1024]{1,0:T(8,128)(2,1)}, bf16[128,1024]{1,0:T(8,128)(2,1)}, u32[]{:S(2)}, u32[]{:S(2)}) collective-permute-start(bf16[128,1024]{1,0:T(8,128)(2,1)} %act.9.refs_0_), channel_id=1, source_target_pairs={{1,0},{2,3},{5,4},{6,7},{9,8},{10,11},{13,12},{14,15},{17,16},{18,... | collective-permute-start | bytes 786440 | tf_op jit(solution)/shard_map/ppermute | solution.py:245
  133.6 23.7 %collective-permute-start.1 = (bf16[128,1024]{1,0:T(8,128)(2,1)}, bf16[128,1024]{1,0:T(8,128)(2,1)}, u32[]{:S(2)}, u32[]{:S(2)}) collective-permute-start(bf16[128,1024]{1,0:T(8,128)(2,1)} %add_convert_fusion.7.own), channel_id=1, source_target_pairs={{1,2},{2,1},{5,6},{6,5},{9,10},{10,9},{13,14},{14,13},{17,18},{18,... | collective-permute-start | bytes 786440 | tf_op jit(solution)/shard_map/ppermute | solution.py:241
  142.0 17.4 %collective-permute-start.20 = (bf16[128,1024]{1,0:T(8,128)(2,1)S(1)}, bf16[128,1024]{1,0:T(8,128)(2,1)}, u32[]{:S(2)}, u32[]{:S(2)}) collective-permute-start(bf16[128,1024]{1,0:T(8,128)(2,1)S(1)} %copy-done.12), channel_id=1, source_target_pairs={{1,0},{2,3},{5,4},{6,7},{9,8},{10,11},{13,12},{14,15},{17,16},{18,... | collective-permute-start | bytes 786440 | tf_op jit(solution)/shard_map/ppermute | solution.py:245
  147.5 15.0 %copy-start.4 = (s32[8,1]{1,0:T(8,128)S(1)}, s32[8,1]{1,0:T(8,128)}, u32[]{:S(2)}) copy-start(s32[8,1]{1,0:T(8,128)} %copy-done.1) | copy-start | bytes 100
  147.5 15.0 %copy-start.8 = (s32[8,1,8]{2,1,0:T(1,128)S(1)}, s32[8,1,8]{2,1,0:T(1,128)}, u32[]{:S(2)}) copy-start(s32[8,1,8]{2,1,0:T(1,128)} %ids.47) | copy-start | bytes 772
  147.5 14.9 %collective-permute-start.34 = (bf16[128,2048]{1,0:T(8,128)(2,1)S(1)}, bf16[128,2048]{1,0:T(8,128)(2,1)S(1)}, u32[]{:S(2)}, u32[]{:S(2)}) collective-permute-start(bf16[128,2048]{1,0:T(8,128)(2,1)S(1)} %down.13), channel_id=1, source_target_pairs={{0,8},{4,12},{8,0},{12,4},{1,9},{5,13},{9,1},{13,5},{2,10},{6,14},... | collective-permute-start | bytes 1572872 | tf_op jit(solution)/shard_map/ppermute | solution.py:234
  149.7 12.8 %collective-permute-start.24 = (bf16[128,2048]{1,0:T(8,128)(2,1)S(1)}, bf16[128,2048]{1,0:T(8,128)(2,1)}, u32[]{:S(2)}, u32[]{:S(2)}) collective-permute-start(bf16[128,2048]{1,0:T(8,128)(2,1)S(1)} %down.11), channel_id=1, source_target_pairs={{0,4},{4,0},{8,12},{12,8},{1,5},{5,1},{9,13},{13,9},{2,6},{6,2},{1... | collective-permute-start | bytes 1572872 | tf_op jit(solution)/shard_map/ppermute | solution.py:234
  152.4 20.4 %collective-permute-start.17 = (bf16[128,2048]{1,0:T(8,128)(2,1)S(1)}, bf16[128,2048]{1,0:T(8,128)(2,1)S(1)}, u32[]{:S(2)}, u32[]{:S(2)}) collective-permute-start(bf16[128,2048]{1,0:T(8,128)(2,1)S(1)} %down.10), channel_id=1, source_target_pairs={{0,8},{4,12},{8,0},{12,4},{1,9},{5,13},{9,1},{13,5},{2,10},{6,14},... | collective-permute-start | bytes 1572872 | tf_op jit(solution)/shard_map/ppermute | solution.py:234
  157.4 15.5 %collective-permute-start.7 = (bf16[128,2048]{1,0:T(8,128)(2,1)}, bf16[128,2048]{1,0:T(8,128)(2,1)}, u32[]{:S(2)}, u32[]{:S(2)}) collective-permute-start(bf16[128,2048]{1,0:T(8,128)(2,1)} %down.8), channel_id=1, source_target_pairs={{0,4},{4,0},{8,12},{12,8},{1,5},{5,1},{9,13},{13,9},{2,6},{6,2},{1... | collective-permute-start | bytes 1572872 | tf_op jit(solution)/shard_map/ppermute | solution.py:234
  159.3 8.2 %collective-permute-start.2 = (bf16[128,1024]{1,0:T(8,128)(2,1)}, bf16[128,1024]{1,0:T(8,128)(2,1)S(1)}, u32[]{:S(2)}, u32[]{:S(2)}) collective-permute-start(bf16[128,1024]{1,0:T(8,128)(2,1)} %act.8.refs_0_), channel_id=1, source_target_pairs={{1,0},{2,3},{5,4},{6,7},{9,8},{10,11},{13,12},{14,15},{17,16},{18,... | collective-permute-start | bytes 786440 | tf_op jit(solution)/shard_map/ppermute | solution.py:245
  (14 other events, 90.0 us)

commit v2 on v1

--- a/solution.py
+++ b/solution.py
@@ -11,7 +11,8 @@
 ANY = pl.BlockSpec(memory_space=pl.ANY)
 SMEM = pl.BlockSpec(memory_space=pltpu.SMEM)
 VMEM = pl.BlockSpec(memory_space=pltpu.VMEM)
-VMEM_LIMIT = 40 * 1024 * 1024
+MIB = 1024 * 1024
+VMEM_LIMIT = 36 * MIB
 
 
 def place(flip, step, per_owner):
@@ -77,34 +78,27 @@
     )(ids, counts, rows, weight)
 
 
-def act_kernel(which, ids, counts, own, other, bias, out):
-    slots = ids.shape[2]
-    b = place(*which)
-    count = counts[b, 0]
+def bias_kernel(order, ids, counts, bias, out):
+    slots = ids.shape[2]
     per_shard = bias.shape[0]
-    for s in range(slots):
-        span = pl.ds(s * BLK, BLK)
-        block = lax.rem(ids[b, 0, s], per_shard)
-        value = own[:, span].astype(jnp.float32)
-        if other is not None:
-            value = value + other[:, span].astype(jnp.float32)
-        value = jnp.maximum(value + bias[pl.ds(block, 1), :], 0.0)
-        out[:, span] = jnp.where(s < count, value, 0.0).astype(out.dtype)
-
-
-def activate(which, ids, counts, own, other, bias):
-    body = act_kernel
-    if other is None:
-        body = lambda which, ids, counts, own, bias, out: act_kernel(which, ids, counts, own, None, bias, out)
-    operands = [own] if other is None else [own, other]
+    for c, which in enumerate(order):
+        b = place(*which)
+        for s in range(slots):
+            row = bias[pl.ds(lax.rem(ids[b, 0, s], per_shard), 1), :]
+            out[pl.ds(c, 1), pl.ds(s * BLK, BLK)] = jnp.where(s < counts[b, 0], row, 0.0)
+
+
+def bias_table(order, ids, counts, bias):
+    slots = ids.shape[2]
     return pl.pallas_call(
-        functools.partial(body, which),
-        out_shape=jax.ShapeDtypeStruct(own.shape, jnp.bfloat16),
-        in_specs=[SMEM, SMEM] + [VMEM] * len(operands) + [VMEM],
+        functools.partial(bias_kernel, order),
+        out_shape=jax.ShapeDtypeStruct((len(order), slots * BLK), jnp.float32),
+        in_specs=[SMEM, SMEM, VMEM],
         out_specs=VMEM,
-        cost_estimate=pl.CostEstimate(flops=own.size, bytes_accessed=6 * own.size, transcendentals=0),
-        name="act",
-    )(ids, counts, *operands, bias)
+        compiler_params=pltpu.CompilerParams(vmem_limit_bytes=MIB),
+        cost_estimate=pl.CostEstimate(flops=bias.size, bytes_accessed=8 * bias.size, transcendentals=0),
+        name="bias_table",
+    )(ids, counts, bias)
 
 
 def down_kernel(which, row0, n_init, has_bias, has_base, two, ids, counts, *refs):
@@ -209,15 +203,19 @@
     )(ids, counts, *operands)
 
 
+def active(total, bias):
+    return jnp.maximum(total + bias, 0.0).astype(jnp.bfloat16)
+
+
 def plain(rows_in, up_weight, up_bias, down_weight, down_bias, active_ids, active_counts):
     gathered = lax.all_gather(rows_in, "tensor", axis=0, tiled=True)
-    blocks = gathered.shape[0] // BLK
+    order = [(None, b, 1) for b in range(gathered.shape[0] // BLK)]
+    table = bias_table(order, active_ids, active_counts, up_bias.reshape(-1, BLK))
     terms = []
-    for b in range(blocks):
-        which = (None, b, 1)
+    for b, which in enumerate(order):
         part = up(which, b * BLK, active_ids, active_counts, gathered, up_weight)
-        summed = lax.psum(part, "dp")
-        hidden = activate(which, active_ids, active_counts, summed, None, up_bias.reshape(-1, BLK))
+        summed = lax.psum(part, "dp").astype(jnp.float32)
+        hidden = active(summed, table[b : b + 1])
         terms.append(down(which, active_ids, active_counts, hidden, None, down_weight))
     terms = jnp.concatenate(terms, axis=0)
     owned = lax.psum_scatter(terms, "tensor", scatter_dimension=0, tiled=True).astype(jnp.float32)
@@ -225,59 +223,69 @@
 
 
 def staged(rows_in, up_weight, up_bias, down_weight, down_bias, active_ids, active_counts):
-    per_owner = rows_in.shape[0] // BLK
-    depth = lax.axis_size("dp")
-    half = depth // 2
-    bias_blocks = up_bias.reshape(-1, BLK)
+    f32 = jnp.float32
+    order = [(0, 0, 2), (1, 0, 2), (3, 0, 2), (2, 0, 2), (3, 1, 2), (2, 1, 2), (1, 1, 2), (0, 1, 2)]
+    steps = len(order)
+    lag = 3
+    position = lax.axis_index("dp")
+    edge = (position == 0) | (position == 3)
 
     def swap(value, flip):
         return lax.ppermute(value, "tensor", [(t, t ^ flip) for t in range(4)])
 
-    def hidden_of(which, row0, rows):
-        value = up(which, row0, active_ids, active_counts, rows, up_weight)
-        for hop in range(half - 1):
-            moved = lax.ppermute(value, "dp", [(hop, hop + 1), (depth - 1 - hop, depth - 2 - hop)])
-            value = (value.astype(jnp.float32) + moved.astype(jnp.float32)).astype(jnp.bfloat16)
-        moved = lax.ppermute(value, "dp", [(half - 1, half), (half, half - 1)])
-        hidden = activate(which, active_ids, active_counts, value, moved, bias_blocks)
-        back = hidden
-        for hop in range(half - 1, 0, -1):
-            back = lax.ppermute(back, "dp", [(hop, hop - 1), (depth - 1 - hop, depth - hop)])
-        return hidden, back
-
-    def terms_of(which, pair, **more):
-        return down(which, active_ids, active_counts, *pair, down_weight, **more)
-
+    across = [swap(rows_in[:BLK], 3), swap(rows_in[BLK:], 3)]
     beside = swap(rows_in, 1)
-    across = [swap(rows_in[j * BLK : (j + 1) * BLK], 3) for j in range(per_owner)]
     relayed = [swap(a, 1) for a in across]
-
-    own = {}
-    sums = {}
-    near = {}
-    far = {}
+    table = bias_table(order, active_ids, active_counts, up_bias.reshape(-1, BLK))
+    source = {0: (rows_in, BLK), 1: (beside, BLK), 2: (relayed, 0), 3: (across, 0)}
+
+    def up_step(i):
+        flip, j, _ = order[i]
+        rows, stride = source[flip]
+        rows = rows[j] if stride == 0 else rows
+        return up(order[i], j * stride, active_ids, active_counts, rows, up_weight)
+
+    def down_step(i, pair, **more):
+        return down(order[i], active_ids, active_counts, *pair, down_weight, **more)
+
+    hidden, terms, near, far = {}, {}, {}, {}
     base = None
-    for j in range(per_owner):
-        own[j] = hidden_of((0, j, per_owner), j * BLK, rows_in)
-    for j in range(per_owner):
-        pair3 = hidden_of((3, j, per_owner), 0, across[j])
-        pair2 = hidden_of((2, j, per_owner), 0, relayed[j])
-        sent = swap(terms_of((3, j, per_owner), pair3), 1)
-        far[j] = swap(terms_of((2, j, per_owner), pair2, inits=[sent]), 2)
-    for j in range(per_owner):
-        pair1 = hidden_of((1, j, per_owner), j * BLK, beside)
-        near[j] = swap(terms_of((1, j, per_owner), pair1), 1)
-    for j in range(per_owner):
-        base = terms_of(
-            (0, j, per_owner),
-            own[j],
-            inits=[near[j], far[j]],
-            bias=down_bias[None, :],
-            base=base,
-            rows=per_owner * BLK,
-            row0=j * BLK,
-            dtype=jnp.float32,
-        )
+    for i in range(steps + lag):
+        back = i - lag
+        part = up_step(i) if i < steps else None
+        if part is None:
+            sent = hidden[back]
+        elif back < 0:
+            sent = part
+        else:
+            sent = jnp.where(edge, part, hidden[back])
+        got = lax.ppermute(sent, "dp", [(0, 1), (1, 0), (2, 3), (3, 2)])
+        if part is not None:
+            folded = (part.astype(f32) + got.astype(f32)).astype(jnp.bfloat16)
+            other = lax.ppermute(folded, "dp", [(1, 2), (2, 1)])
+            hidden[i] = active(folded.astype(f32) + other.astype(f32), table[i : i + 1])
+        if back >= 0:
+            flip, j, _ = order[back]
+            pair = (hidden[back], got)
+            if flip == 1:
+                near[j] = swap(down_step(back, pair), 1)
+            elif flip == 3:
+                terms[j] = swap(down_step(back, pair), 1)
+            elif flip == 2:
+                far[j] = swap(down_step(back, pair, inits=[terms[j]]), 2)
+            else:
+                terms[j, "own"] = (back, pair)
+            if j == 1 and flip == 0:
+                for row in range(2):
+                    base = down_step(
+                        *terms[row, "own"],
+                        inits=[near[row], far[row]],
+                        bias=down_bias[None, :],
+                        base=base,
+                        rows=2 * BLK,
+                        row0=row * BLK,
+                        dtype=f32,
+                    )
     return base
 
 
@@ -293,8 +301,7 @@
     )
 
     def run(rows_in, *rest):
-        whole_blocks = rows_in.shape[0] % BLK == 0
-        if mesh.shape["tensor"] == 4 and mesh.shape["dp"] % 2 == 0 and whole_blocks:
+        if mesh.shape["tensor"] == 4 and mesh.shape["dp"] == 4 and rows_in.shape[0] == 2 * BLK:
             return staged(rows_in, *rest)
         return plain(rows_in, *rest)
 

time: 181 us -> 128 us (0.71)
  starting transfers between devices: 59.4 us -> 33.7 us
  Pallas kernels: 65 us -> 46.6 us
  other arithmetic: 6.22 us -> 1.66 us
  local copies, waits for them, and re-layouts: 6.71 us -> 4.75 us
    ppermute x24 -> x19, starting transfers between devices: 53.7 us -> 28.3 us  [the longest x8 23.8 us: staged(): other = lax.ppermute(folded, 'dp', [(1, 2), (2, 1)])]
    pallas_call x8 -> x1, Pallas kernels: 15.1 us -> 0.9 us  [bias_table(): pl.pallas_call(functools.partial(bias_kernel, order), out_shape=jax.Shape...]
    convert_element_type x8 -> x11, other arithmetic: 6.22 us -> 0.84 us  [the longest x8 0.53 us: staged(): folded = (part.astype(f32) + got.astype(f32)).astype(jnp.bfloat16)]
    ppermute x11, waiting for transfers between devices: 25 us -> 20.1 us  [swap(): return lax.ppermute(value, 'tensor', [(t, t ^ flip) for t in range(4)])]
    ppermute x24 -> x19, waiting for transfers between devices: 14 us -> 18 us  [the longest x8 10.4 us: staged(): other = lax.ppermute(folded, 'dp', [(1, 2), (2, 1)])]
    pallas_call x8, Pallas kernels: 26.6 us -> 24 us  [down(): pl.pallas_call(functools.partial(down_kernel, which, row0, len(inits), bi...]
    unnamed x55 -> x11, local copies, waits for them, and re-layouts: 4.54 us -> 2.65 us
  transfers between devices with their start and end apart: 35 -> 30, of which waited for: 9 -> 10; matrix products, arithmetic and copies ran while one was open for 4% -> 2% of each run, Pallas kernels for 34% -> 34%
where the time goes in v2:
time: 128 us; the launch traced here: 126 us
  Pallas kernels  46.6 us (36%)
  waiting for transfers between devices  38 us (30%)
  starting transfers between devices  33.7 us (26%)
  local copies, waits for them, and re-layouts  4.75 us (4%)
  other arithmetic  1.66 us (1%)
    pallas_call x8, Pallas kernels, down(): pl.pallas_call(functools.partial(down_kernel, which, row0, len(inits), bi...  24 us
    ppermute x8, starting transfers between devices, staged(): other = lax.ppermute(folded, 'dp', [(1, 2), (2, 1)])  23.8 us
    pallas_call x8, Pallas kernels, up(): pl.pallas_call(functools.partial(up_kernel, which, row0), out_shape=jax.S...  21.8 us
    ppermute x11, waiting for transfers between devices, swap(): return lax.ppermute(value, 'tensor', [(t, t ^ flip) for t in range(4)])  20.1 us
    ppermute x8, waiting for transfers between devices, staged(): other = lax.ppermute(folded, 'dp', [(1, 2), (2, 1)])  10.4 us
    ppermute x11, waiting for transfers between devices, staged(): got = lax.ppermute(sent, 'dp', [(0, 1), (1, 0), (2, 3), (3, 2)])  7.56 us
    ppermute x11, starting transfers between devices, swap(): return lax.ppermute(value, 'tensor', [(t, t ^ flip) for t in range(4)])  5.42 us
    ppermute x11, starting transfers between devices, staged(): got = lax.ppermute(sent, 'dp', [(0, 1), (1, 0), (2, 3), (3, 2)])  4.51 us
  transfers between devices with their start and end apart: 30, of which 10 were waited for; matrix products, arithmetic and copies ran while one was open for 2% of the time, Pallas kernels for 34%

profile of v2, /device:TPU:12, one launch (start us, length us, event | category | flops | bytes accessed | tf_op | source)
XLA Modules:
  0.0 125.5 jit_solution(15640299663820570994)
XLA Ops:
  0.0 2.1 %fusion = (bf16[128,2048]{1,0:T(8,128)(2,1)}, bf16[128,2048]{1,0:T(8,128)(2,1)S(1)}) fusion(bf16[256,2048]{1,0:T(8,128)(2,1)} %rows.3), kind=kLoop, calls=%fused_computation.21 | loop fusion | bytes 2097152 | tf_op jit(solution)/shard_map/slice | solution.py:236
  2.1 0.9 collective-permute-start.9
  3.0 0.7 collective-permute-start.1
  3.7 0.7 copy.25.counts
  4.4 1.2 copy-done
  5.6 0.7 copy-done.1
  6.3 2.2 %up.13 = bf16[128,1024]{1,0:T(8,128)(2,1)S(1)} custom-call(s32[8,1,8]{2,1,0:T(1,128)S(1)} %copy-done.1, s32[8,1]{1,0:T(8,128)S(1)} %copy.25.counts, bf16[256,2048]{1,0:T(8,128)(2,1)S(1)} %copy-done, bf16[2048,8192]{1,0:T(8,128)(2,1)} %weight.15), custom_call_target="tpu_custom_call" | custom-call | flops 536870912 | bytes 4194304 | tf_op jit(solution)/shard_map/up/pallas_call | solution.py:63
  8.5 0.5 collective-permute-start.11
  9.4 2.7 %up.8 = bf16[128,1024]{1,0:T(8,128)(2,1)S(1)} custom-call(s32[8,1,8]{2,1,0:T(1,128)S(1)} %copy-done.1, s32[8,1]{1,0:T(8,128)S(1)} %copy.25.counts, bf16[256,2048]{1,0:T(8,128)(2,1)S(1)} %copy-done, bf16[2048,8192]{1,0:T(8,128)(2,1)} %weight.15), custom_call_target="tpu_custom_call" | custom-call | flops 536870912 | bytes 4194304 | tf_op jit(solution)/shard_map/up/pallas_call | solution.py:63
  12.1 0.9 bias_table.1
  13.1 3.4 %collective-permute-done.9.rows = bf16[128,2048]{1,0:T(8,128)(2,1)S(1)} collective-permute-done((bf16[128,2048]{1,0:T(8,128)(2,1)}, bf16[128,2048]{1,0:T(8,128)(2,1)S(1)}, u32[]{:S(2)}, u32[]{:S(2)}) %collective-permute-start.9) | collective-permute-done | bytes 524320 | tf_op jit(solution)/shard_map/ppermute | solution.py:234
  16.5 3.4 %up.15 = bf16[128,1024]{1,0:T(8,128)(2,1)S(1)} custom-call(s32[8,1,8]{2,1,0:T(1,128)S(1)} %copy-done.2, s32[8,1]{1,0:T(8,128)S(1)} %copy.25.counts, bf16[128,2048]{1,0:T(8,128)(2,1)S(1)} %collective-permute-done.9.rows, bf16[2048,8192]{1,0:T(8,128)(2,1)} %weight.15), custom_call_target="tpu_custom_call" | custom-call | flops 536870912 | bytes 4194304 | tf_op jit(solution)/shard_map/up/pallas_call | solution.py:63
  19.9 0.5 collective-permute-start.20
  20.4 4.6 %collective-permute-start.12 = (bf16[128,1024]{1,0:T(8,128)(2,1)S(1)}, bf16[128,1024]{1,0:T(8,128)(2,1)S(1)}, u32[]{:S(2)}, u32[]{:S(2)}) collective-permute-start(bf16[128,1024]{1,0:T(8,128)(2,1)S(1)} %add_convert_fusion.4), channel_id=1, source_target_pairs={{1,2},{2,1},{5,6},{6,5},{9,10},{10,9},{13,14},{14,13},{17,18},{18,... | collective-permute-start | bytes 786440 | tf_op jit(solution)/shard_map/ppermute | solution.py:265
  25.1 2.6 %collective-permute-done.rows = bf16[128,2048]{1,0:T(8,128)(2,1)S(1)} collective-permute-done((bf16[128,2048]{1,0:T(8,128)(2,1)S(1)}, bf16[128,2048]{1,0:T(8,128)(2,1)S(1)}, u32[]{:S(2)}, u32[]{:S(2)}) %collective-permute-start) | collective-permute-done | bytes 524320 | tf_op jit(solution)/shard_map/ppermute | solution.py:234
  27.9 2.7 %up.9 = bf16[128,1024]{1,0:T(8,128)(2,1)S(1)} custom-call(s32[8,1,8]{2,1,0:T(1,128)S(1)} %copy-done.2, s32[8,1]{1,0:T(8,128)S(1)} %copy.25.counts, bf16[128,2048]{1,0:T(8,128)(2,1)S(1)} %collective-permute-done.rows, bf16[2048,8192]{1,0:T(8,128)(2,1)} %weight.15), custom_call_target="tpu_custom_call" | custom-call | flops 536870912 | bytes 4194304 | tf_op jit(solution)/shard_map/up/pallas_call | solution.py:63
  30.6 3.5 %collective-permute-start.21 = (bf16[128,1024]{1,0:T(8,128)(2,1)S(1)}, bf16[128,1024]{1,0:T(8,128)(2,1)S(1)}, u32[]{:S(2)}, u32[]{:S(2)}) collective-permute-start(bf16[128,1024]{1,0:T(8,128)(2,1)S(1)} %add_convert_fusion.1), channel_id=1, source_target_pairs={{1,2},{2,1},{5,6},{6,5},{9,10},{10,9},{13,14},{14,13},{17,18},{18,... | collective-permute-start | bytes 786440 | tf_op jit(solution)/shard_map/ppermute | solution.py:265
  34.1 2.7 %up.10 = bf16[128,1024]{1,0:T(8,128)(2,1)S(1)} custom-call(s32[8,1,8]{2,1,0:T(1,128)S(1)} %copy-done.2, s32[8,1]{1,0:T(8,128)S(1)} %copy.25.counts, bf16[256,2048]{1,0:T(8,128)(2,1)S(1)} %collective-permute-done.1.rows, bf16[2048,8192]{1,0:T(8,128)(2,1)} %weight.15), custom_call_target="tpu_custom_call" | custom-call | flops 536870912 | bytes 4194304 | tf_op jit(solution)/shard_map/up/pallas_call | solution.py:63
  37.0 2.7 %up.12 = bf16[128,1024]{1,0:T(8,128)(2,1)S(1)} custom-call(s32[8,1,8]{2,1,0:T(1,128)S(1)} %copy-done.2, s32[8,1]{1,0:T(8,128)S(1)} %copy.25.counts, bf16[128,2048]{1,0:T(8,128)(2,1)S(1)} %collective-permute-done.10.rows, bf16[2048,8192]{1,0:T(8,128)(2,1)} %weight.15), custom_call_target="tpu_custom_call" | custom-call | flops 536870912 | bytes 4194304 | tf_op jit(solution)/shard_map/up/pallas_call | solution.py:63
  39.9 2.1 %collective-permute-start.13 = (bf16[128,1024]{1,0:T(8,128)(2,1)S(1)}, bf16[128,1024]{1,0:T(8,128)(2,1)S(1)}, u32[]{:S(2)}, u32[]{:S(2)}) collective-permute-start(bf16[128,1024]{1,0:T(8,128)(2,1)S(1)} %get-tuple-element.9), channel_id=1, source_target_pairs={{0,1},{1,0},{2,3},{3,2},{4,5},{5,4},{6,7},{7,6},{8,9},{9,8},{10,11... | collective-permute-start | bytes 786440 | tf_op jit(solution)/shard_map/ppermute | solution.py:262
  41.9 2.7 %up.14 = bf16[128,1024]{1,0:T(8,128)(2,1)S(1)} custom-call(s32[8,1,8]{2,1,0:T(1,128)S(1)} %copy-done.2, s32[8,1]{1,0:T(8,128)S(1)} %copy.25.counts, bf16[128,2048]{1,0:T(8,128)(2,1)S(1)} %collective-permute-done.19.rows, bf16[2048,8192]{1,0:T(8,128)(2,1)} %weight.15), custom_call_target="tpu_custom_call" | custom-call | flops 536870912 | bytes 4194304 | tf_op jit(solution)/shard_map/up/pallas_call | solution.py:63
  44.6 1.4 %collective-permute-done.2 = bf16[128,1024]{1,0:T(8,128)(2,1)S(1)} collective-permute-done((bf16[128,1024]{1,0:T(8,128)(2,1)S(1)}, bf16[128,1024]{1,0:T(8,128)(2,1)S(1)}, u32[]{:S(2)}, u32[]{:S(2)}) %collective-permute-start.2) | collective-permute-done | bytes 262176 | tf_op jit(solution)/shard_map/ppermute | solution.py:262
  46.1 2.3 %collective-permute-start.3 = (bf16[128,1024]{1,0:T(8,128)(2,1)S(1)}, bf16[128,1024]{1,0:T(8,128)(2,1)S(1)}, u32[]{:S(2)}, u32[]{:S(2)}) collective-permute-start(bf16[128,1024]{1,0:T(8,128)(2,1)S(1)} %add_convert_fusion.7), channel_id=1, source_target_pairs={{1,2},{2,1},{5,6},{6,5},{9,10},{10,9},{13,14},{14,13},{17,18},{18,... | collective-permute-start | bytes 786440 | tf_op jit(solution)/shard_map/ppermute | solution.py:265
  48.7 2.7 %up.11 = bf16[128,1024]{1,0:T(8,128)(2,1)S(1)} custom-call(s32[8,1,8]{2,1,0:T(1,128)S(1)} %copy-done.2, s32[8,1]{1,0:T(8,128)S(1)} %copy.25.counts, bf16[256,2048]{1,0:T(8,128)(2,1)S(1)} %collective-permute-done.1.rows, bf16[2048,8192]{1,0:T(8,128)(2,1)} %weight.15), custom_call_target="tpu_custom_call" | custom-call | flops 536870912 | bytes 4194304 | tf_op jit(solution)/shard_map/up/pallas_call | solution.py:63
  51.4 4.0 %collective-permute-done.3 = bf16[128,1024]{1,0:T(8,128)(2,1)S(1)} collective-permute-done((bf16[128,1024]{1,0:T(8,128)(2,1)S(1)}, bf16[128,1024]{1,0:T(8,128)(2,1)S(1)}, u32[]{:S(2)}, u32[]{:S(2)}) %collective-permute-start.3) | collective-permute-done | bytes 262176 | tf_op jit(solution)/shard_map/ppermute | solution.py:265
  55.7 2.4 %collective-permute-start.14 = (bf16[128,1024]{1,0:T(8,128)(2,1)S(1)}, bf16[128,1024]{1,0:T(8,128)(2,1)S(1)}, u32[]{:S(2)}, u32[]{:S(2)}) collective-permute-start(bf16[128,1024]{1,0:T(8,128)(2,1)S(1)} %add_convert_fusion.3), channel_id=1, source_target_pairs={{1,2},{2,1},{5,6},{6,5},{9,10},{10,9},{13,14},{14,13},{17,18},{18,... | collective-permute-start | bytes 786440 | tf_op jit(solution)/shard_map/ppermute | solution.py:265
  58.2 3.5 %collective-permute-start.23 = (bf16[128,1024]{1,0:T(8,128)(2,1)S(1)}, bf16[128,1024]{1,0:T(8,128)(2,1)S(1)}, u32[]{:S(2)}, u32[]{:S(2)}) collective-permute-start(bf16[128,1024]{1,0:T(8,128)(2,1)S(1)} %add_convert_fusion), channel_id=1, source_target_pairs={{1,2},{2,1},{5,6},{6,5},{9,10},{10,9},{13,14},{14,13},{17,18},{18,... | collective-permute-start | bytes 786440 | tf_op jit(solution)/shard_map/ppermute | solution.py:265
  61.7 0.8 collective-permute-done.4.refs_1_
  62.5 2.5 %collective-permute-start.5 = (bf16[128,1024]{1,0:T(8,128)(2,1)S(1)}, bf16[128,1024]{1,0:T(8,128)(2,1)S(1)}, u32[]{:S(2)}, u32[]{:S(2)}) collective-permute-start(bf16[128,1024]{1,0:T(8,128)(2,1)S(1)} %add_convert_fusion.6), channel_id=1, source_target_pairs={{1,2},{2,1},{5,6},{6,5},{9,10},{10,9},{13,14},{14,13},{17,18},{18,... | collective-permute-start | bytes 786440 | tf_op jit(solution)/shard_map/ppermute | solution.py:265
  65.0 1.8 %collective-permute-done.14 = bf16[128,1024]{1,0:T(8,128)(2,1)S(1)} collective-permute-done((bf16[128,1024]{1,0:T(8,128)(2,1)S(1)}, bf16[128,1024]{1,0:T(8,128)(2,1)S(1)}, u32[]{:S(2)}, u32[]{:S(2)}) %collective-permute-start.14) | collective-permute-done | bytes 262176 | tf_op jit(solution)/shard_map/ppermute | solution.py:265
  67.1 3.5 %down.12 = bf16[128,2048]{1,0:T(8,128)(2,1)S(1)} custom-call(s32[8,1,8]{2,1,0:T(1,128)S(1)} %copy-done.2, s32[8,1]{1,0:T(8,128)S(1)} %copy.25.counts, bf16[128,1024]{1,0:T(8,128)(2,1)S(1)} %get-tuple-element.6.refs_0_, bf16[128,1024]{1,0:T(8,128)(2,1)S(1)} %collective-permute-done.22.refs_1_, bf16[8192,2048]{1,0:T(8,128)(2,1)} %refs_2_.15), custom_call_target="tpu_custom_call" | custom-call | flops 536870912 | bytes 4194304 | tf_op jit(solution)/shard_map/down/pallas_call | solution.py:185
  70.7 4.6 %collective-permute-done.5 = bf16[128,1024]{1,0:T(8,128)(2,1)S(1)} collective-permute-done((bf16[128,1024]{1,0:T(8,128)(2,1)S(1)}, bf16[128,1024]{1,0:T(8,128)(2,1)S(1)}, u32[]{:S(2)}, u32[]{:S(2)}) %collective-permute-start.5) | collective-permute-done | bytes 262176 | tf_op jit(solution)/shard_map/ppermute | solution.py:265
  75.7 2.4 %collective-permute-start.16 = (bf16[128,1024]{1,0:T(8,128)(2,1)S(1)}, bf16[128,1024]{1,0:T(8,128)(2,1)S(1)}, u32[]{:S(2)}, u32[]{:S(2)}) collective-permute-start(bf16[128,1024]{1,0:T(8,128)(2,1)S(1)} %add_convert_fusion.2), channel_id=1, source_target_pairs={{1,2},{2,1},{5,6},{6,5},{9,10},{10,9},{13,14},{14,13},{17,18},{18,... | collective-permute-start | bytes 786440 | tf_op jit(solution)/shard_map/ppermute | solution.py:265
  78.5 5.4 %collective-permute-done.6.refs_1_ = bf16[128,1024]{1,0:T(8,128)(2,1)S(1)} collective-permute-done((bf16[128,1024]{1,0:T(8,128)(2,1)S(1)}, bf16[128,1024]{1,0:T(8,128)(2,1)S(1)}, u32[]{:S(2)}, u32[]{:S(2)}) %collective-permute-start.6) | collective-permute-done | bytes 262176 | tf_op jit(solution)/shard_map/ppermute | solution.py:262
  83.9 2.7 %down.9 = bf16[128,2048]{1,0:T(8,128)(2,1)S(1)} custom-call(s32[8,1,8]{2,1,0:T(1,128)S(1)} %copy-done.2, s32[8,1]{1,0:T(8,128)S(1)} %copy.25.counts, bf16[128,1024]{1,0:T(8,128)(2,1)S(1)} %get-tuple-element.12.refs_0_, bf16[128,1024]{1,0:T(8,128)(2,1)S(1)} %collective-permute-done.6.refs_1_, bf16[8192,2048]{1,0:T(8,128)(2,1)} %refs_2_.15), custom_call_target="tpu_custom_call" | custom-call | flops 536870912 | bytes 4194304 | tf_op jit(solution)/shard_map/down/pallas_call | solution.py:185
  86.9 0.6 collective-permute-start.17
  87.6 2.6 %collective-permute-start.7 = (bf16[128,1024]{1,0:T(8,128)(2,1)S(1)}, bf16[128,1024]{1,0:T(8,128)(2,1)S(1)}, u32[]{:S(2)}, u32[]{:S(2)}) collective-permute-start(bf16[128,1024]{1,0:T(8,128)(2,1)S(1)} %add_convert_fusion.5), channel_id=1, source_target_pairs={{1,2},{2,1},{5,6},{6,5},{9,10},{10,9},{13,14},{14,13},{17,18},{18,... | collective-permute-start | bytes 786440 | tf_op jit(solution)/shard_map/ppermute | solution.py:265
  90.2 2.7 %down.11 = bf16[128,2048]{1,0:T(8,128)(2,1)S(1)} custom-call(s32[8,1,8]{2,1,0:T(1,128)S(1)} %copy-done.2, s32[8,1]{1,0:T(8,128)S(1)} %copy.25.counts, bf16[128,1024]{1,0:T(8,128)(2,1)S(1)} %get-tuple-element.14.refs_0_, bf16[128,1024]{1,0:T(8,128)(2,1)S(1)} %collective-permute-done.4.refs_1_, bf16[8192,2048]{1,0:T(8,128)(2,1)} %refs_2_.15), custom_call_target="tpu_custom_call" | custom-call | flops 536870912 | bytes 4194304 | tf_op jit(solution)/shard_map/down/pallas_call | solution.py:185
  92.9 0.9 collective-permute-start.27
  93.8 2.7 %down.13 = bf16[128,2048]{1,0:T(8,128)(2,1)S(1)} custom-call(s32[8,1,8]{2,1,0:T(1,128)S(1)} %copy-done.2, s32[8,1]{1,0:T(8,128)S(1)} %copy.25.counts, bf16[128,1024]{1,0:T(8,128)(2,1)S(1)} %get-tuple-element.8.refs_0_, bf16[128,1024]{1,0:T(8,128)(2,1)S(1)} %collective-permute-done.15.refs_1_, bf16[8192,2048]{1,0:T(8,128)(2,1)} %refs_2_.15, ...), custom_call_target="tpu_custom_call" | custom-call | flops 536870912 | bytes 4194304 | tf_op jit(solution)/shard_map/down/pallas_call | solution.py:185
  96.9 2.7 %down.8 = bf16[128,2048]{1,0:T(8,128)(2,1)S(1)} custom-call(s32[8,1,8]{2,1,0:T(1,128)S(1)} %copy-done.2, s32[8,1]{1,0:T(8,128)S(1)} %copy.25.counts, bf16[128,1024]{1,0:T(8,128)(2,1)S(1)} %maximum_convert_fusion.2.refs_0_, bf16[128,1024]{1,0:T(8,128)(2,1)S(1)} %collective-permute-done.17.refs_1_, bf16[8192,2048]{1,0:T(8,128)(2,1)} %refs_2_.15), custom_call_target="tpu_custom_call" | custom-call | flops 536870912 | bytes 4194304 | tf_op jit(solution)/shard_map/down/pallas_call | solution.py:185
  99.6 0.6 collective-permute-start.18
  100.2 2.7 %down.10 = bf16[128,2048]{1,0:T(8,128)(2,1)S(1)} custom-call(s32[8,1,8]{2,1,0:T(1,128)S(1)} %copy-done.2, s32[8,1]{1,0:T(8,128)S(1)} %copy.25.counts, bf16[128,1024]{1,0:T(8,128)(2,1)S(1)} %maximum_convert_fusion.refs_0_, bf16[128,1024]{1,0:T(8,128)(2,1)S(1)} %collective-permute-done.24.refs_1_, bf16[8192,2048]{1,0:T(8,128)(2,1)} %refs_2_.15, ...), custom_call_target="tpu_custom_call" | custom-call | flops 536870912 | bytes 4194304 | tf_op jit(solution)/shard_map/down/pallas_call | solution.py:185
  102.9 1.4 %collective-permute-start.26 = (bf16[128,2048]{1,0:T(8,128)(2,1)S(1)}, bf16[128,2048]{1,0:T(8,128)(2,1)S(1)}, u32[]{:S(2)}, u32[]{:S(2)}) collective-permute-start(bf16[128,2048]{1,0:T(8,128)(2,1)S(1)} %down.10), channel_id=1, source_target_pairs={{0,8},{4,12},{8,0},{12,4},{1,9},{5,13},{9,1},{13,5},{2,10},{6,14},... | collective-permute-start | bytes 1572872 | tf_op jit(solution)/shard_map/ppermute | solution.py:234
  104.5 7.0 %collective-permute-done.29.refs_4_ = bf16[128,2048]{1,0:T(8,128)(2,1)S(1)} collective-permute-done((bf16[128,2048]{1,0:T(8,128)(2,1)S(1)}, bf16[128,2048]{1,0:T(8,128)(2,1)S(1)}, u32[]{:S(2)}, u32[]{:S(2)}) %collective-permute-start.29) | collective-permute-done | bytes 524320 | tf_op jit(solution)/shard_map/ppermute | solution.py:234
  111.4 3.2 %down.14.refs_6_ = f32[256,2048]{1,0:T(8,128)} custom-call(s32[8,1,8]{2,1,0:T(1,128)S(1)} %copy-done.2, s32[8,1]{1,0:T(8,128)S(1)} %copy.25.counts, bf16[128,1024]{1,0:T(8,128)(2,1)S(1)} %get-tuple-element.10.refs_0_, bf16[128,1024]{1,0:T(8,128)(2,1)S(1)} %collective-permute-done.13.refs_1_, bf16[8192,2048]{1,0:T(8,128)(2,1)} %refs_2_.15, ...), custom_call_target="tpu_custom_call" | custom-call | flops 536870912 | bytes 4194304 | tf_op jit(solution)/shard_map/down/pallas_call | solution.py:185
  114.7 7.1 %collective-permute-done.26.refs_4_ = bf16[128,2048]{1,0:T(8,128)(2,1)S(1)} collective-permute-done((bf16[128,2048]{1,0:T(8,128)(2,1)S(1)}, bf16[128,2048]{1,0:T(8,128)(2,1)S(1)}, u32[]{:S(2)}, u32[]{:S(2)}) %collective-permute-start.26) | collective-permute-done | bytes 524320 | tf_op jit(solution)/shard_map/ppermute | solution.py:234
  121.7 3.6 %down.15 = f32[256,2048]{1,0:T(8,128)} custom-call(s32[8,1,8]{2,1,0:T(1,128)S(1)} %copy-done.2, s32[8,1]{1,0:T(8,128)S(1)} %copy.25.counts, bf16[128,1024]{1,0:T(8,128)(2,1)S(1)} %maximum_convert_fusion.5.refs_0_, bf16[128,1024]{1,0:T(8,128)(2,1)S(1)} %collective-permute-done.8.refs_1_, bf16[8192,2048]{1,0:T(8,128)(2,1)} %refs_2_.15, ...), custom_call_target="tpu_custom_call", output_to_operand_aliasing={{}: (8, {})} | custom-call | flops 536870912 | bytes 4194304 | tf_op jit(solution)/shard_map/down/pallas_call | solution.py:185
  (58 shorter events, 3.5 us)
Async XLA Ops:
  2.1 14.4 %collective-permute-start.9 = (bf16[128,2048]{1,0:T(8,128)(2,1)}, bf16[128,2048]{1,0:T(8,128)(2,1)S(1)}, u32[]{:S(2)}, u32[]{:S(2)}) collective-permute-start(bf16[128,2048]{1,0:T(8,128)(2,1)} %get-tuple-element.15), channel_id=1, source_target_pairs={{0,12},{4,8},{8,4},{12,0},{1,13},{5,9},{9,5},{13,1},{2,14},{6,10},... | collective-permute-start | bytes 1572872 | tf_op jit(solution)/shard_map/ppermute | solution.py:234
  3.0 31.1 %collective-permute-start.1 = (bf16[256,2048]{1,0:T(8,128)(2,1)}, bf16[256,2048]{1,0:T(8,128)(2,1)S(1)}, u32[]{:S(2)}, u32[]{:S(2)}) collective-permute-start(bf16[256,2048]{1,0:T(8,128)(2,1)} %rows.3), channel_id=1, source_target_pairs={{0,4},{4,0},{8,12},{12,8},{1,5},{5,1},{9,13},{13,9},{2,6},{6,2},{1... | collective-permute-start | bytes 3145736 | tf_op jit(solution)/shard_map/ppermute | solution.py:234
  4.4 1.2 copy-start
  5.6 0.7 copy-start.1
  6.3 5.8 %copy-start.3 = (f32[8192]{0:T(1024)S(1)}, f32[8192]{0:T(1024)}, u32[]{:S(2)}) copy-start(f32[8192]{0:T(1024)} %param.9) | copy-start | bytes 98308
  6.3 10.1 %copy-start.2 = (s32[8,1,8]{2,1,0:T(1,128)S(1)}, s32[8,1,8]{2,1,0:T(1,128)}, u32[]{:S(2)}) copy-start(s32[8,1,8]{2,1,0:T(1,128)} %ids.33) | copy-start | bytes 772
  8.5 11.8 %collective-permute-start.11 = (bf16[128,1024]{1,0:T(8,128)(2,1)S(1)}, bf16[128,1024]{1,0:T(8,128)(2,1)S(1)}, u32[]{:S(2)}, u32[]{:S(2)}) collective-permute-start(bf16[128,1024]{1,0:T(8,128)(2,1)S(1)} %up.13), channel_id=1, source_target_pairs={{0,1},{1,0},{2,3},{3,2},{4,5},{5,4},{6,7},{7,6},{8,9},{9,8},{10,11... | collective-permute-start | bytes 786440 | tf_op jit(solution)/shard_map/ppermute | solution.py:262
  9.0 18.7 %collective-permute-start = (bf16[128,2048]{1,0:T(8,128)(2,1)S(1)}, bf16[128,2048]{1,0:T(8,128)(2,1)S(1)}, u32[]{:S(2)}, u32[]{:S(2)}) collective-permute-start(bf16[128,2048]{1,0:T(8,128)(2,1)S(1)} %get-tuple-element.16), channel_id=1, source_target_pairs={{0,12},{4,8},{8,4},{12,0},{1,13},{5,9},{9,5},{13,1},{2,14},{6,10},... | collective-permute-start | bytes 1572872 | tf_op jit(solution)/shard_map/ppermute | solution.py:234
  19.9 10.7 %collective-permute-start.20 = (bf16[128,1024]{1,0:T(8,128)(2,1)S(1)}, bf16[128,1024]{1,0:T(8,128)(2,1)S(1)}, u32[]{:S(2)}, u32[]{:S(2)}) collective-permute-start(bf16[128,1024]{1,0:T(8,128)(2,1)S(1)} %up.15), channel_id=1, source_target_pairs={{0,1},{1,0},{2,3},{3,2},{4,5},{5,4},{6,7},{7,6},{8,9},{9,8},{10,11... | collective-permute-start | bytes 786440 | tf_op jit(solution)/shard_map/ppermute | solution.py:262
  20.4 16.6 %collective-permute-start.10 = (bf16[128,2048]{1,0:T(8,128)(2,1)S(1)}, bf16[128,2048]{1,0:T(8,128)(2,1)S(1)}, u32[]{:S(2)}, u32[]{:S(2)}) collective-permute-start(bf16[128,2048]{1,0:T(8,128)(2,1)S(1)} %collective-permute-done.9.rows), channel_id=1, source_target_pairs={{0,4},{4,0},{8,12},{12,8},{1,5},{5,1},{9,13},{13,9},{2,6},{6,2},{1... | collective-permute-start | bytes 1572872 | tf_op jit(solution)/shard_map/ppermute | solution.py:234
  20.4 19.2 %collective-permute-start.12 = (bf16[128,1024]{1,0:T(8,128)(2,1)S(1)}, bf16[128,1024]{1,0:T(8,128)(2,1)S(1)}, u32[]{:S(2)}, u32[]{:S(2)}) collective-permute-start(bf16[128,1024]{1,0:T(8,128)(2,1)S(1)} %add_convert_fusion.4), channel_id=1, source_target_pairs={{1,2},{2,1},{5,6},{6,5},{9,10},{10,9},{13,14},{14,13},{17,18},{18,... | collective-permute-start | bytes 786440 | tf_op jit(solution)/shard_map/ppermute | solution.py:265
  27.7 14.2 %collective-permute-start.19 = (bf16[128,2048]{1,0:T(8,128)(2,1)S(1)}, bf16[128,2048]{1,0:T(8,128)(2,1)S(1)}, u32[]{:S(2)}, u32[]{:S(2)}) collective-permute-start(bf16[128,2048]{1,0:T(8,128)(2,1)S(1)} %collective-permute-done.rows), channel_id=1, source_target_pairs={{0,4},{4,0},{8,12},{12,8},{1,5},{5,1},{9,13},{13,9},{2,6},{6,2},{1... | collective-permute-start | bytes 1572872 | tf_op jit(solution)/shard_map/ppermute | solution.py:234
  30.6 17.8 %collective-permute-start.21 = (bf16[128,1024]{1,0:T(8,128)(2,1)S(1)}, bf16[128,1024]{1,0:T(8,128)(2,1)S(1)}, u32[]{:S(2)}, u32[]{:S(2)}) collective-permute-start(bf16[128,1024]{1,0:T(8,128)(2,1)S(1)} %add_convert_fusion.1), channel_id=1, source_target_pairs={{1,2},{2,1},{5,6},{6,5},{9,10},{10,9},{13,14},{14,13},{17,18},{18,... | collective-permute-start | bytes 786440 | tf_op jit(solution)/shard_map/ppermute | solution.py:265
  36.9 9.2 %collective-permute-start.2 = (bf16[128,1024]{1,0:T(8,128)(2,1)S(1)}, bf16[128,1024]{1,0:T(8,128)(2,1)S(1)}, u32[]{:S(2)}, u32[]{:S(2)}) collective-permute-start(bf16[128,1024]{1,0:T(8,128)(2,1)S(1)} %up.10), channel_id=1, source_target_pairs={{0,1},{1,0},{2,3},{3,2},{4,5},{5,4},{6,7},{7,6},{8,9},{9,8},{10,11... | collective-permute-start | bytes 786440 | tf_op jit(solution)/shard_map/ppermute | solution.py:262
  39.9 15.8 %collective-permute-start.13 = (bf16[128,1024]{1,0:T(8,128)(2,1)S(1)}, bf16[128,1024]{1,0:T(8,128)(2,1)S(1)}, u32[]{:S(2)}, u32[]{:S(2)}) collective-permute-start(bf16[128,1024]{1,0:T(8,128)(2,1)S(1)} %get-tuple-element.9), channel_id=1, source_target_pairs={{0,1},{1,0},{2,3},{3,2},{4,5},{5,4},{6,7},{7,6},{8,9},{9,8},{10,11... | collective-permute-start | bytes 786440 | tf_op jit(solution)/shard_map/ppermute | solution.py:262
  46.1 9.3 %collective-permute-start.3 = (bf16[128,1024]{1,0:T(8,128)(2,1)S(1)}, bf16[128,1024]{1,0:T(8,128)(2,1)S(1)}, u32[]{:S(2)}, u32[]{:S(2)}) collective-permute-start(bf16[128,1024]{1,0:T(8,128)(2,1)S(1)} %add_convert_fusion.7), channel_id=1, source_target_pairs={{1,2},{2,1},{5,6},{6,5},{9,10},{10,9},{13,14},{14,13},{17,18},{18,... | collective-permute-start | bytes 786440 | tf_op jit(solution)/shard_map/ppermute | solution.py:265
  48.6 9.5 %collective-permute-start.22 = (bf16[128,1024]{1,0:T(8,128)(2,1)S(1)}, bf16[128,1024]{1,0:T(8,128)(2,1)S(1)}, u32[]{:S(2)}, u32[]{:S(2)}) collective-permute-start(bf16[128,1024]{1,0:T(8,128)(2,1)S(1)} %get-tuple-element.5), channel_id=1, source_target_pairs={{0,1},{1,0},{2,3},{3,2},{4,5},{5,4},{6,7},{7,6},{8,9},{9,8},{10,11... | collective-permute-start | bytes 786440 | tf_op jit(solution)/shard_map/ppermute | solution.py:262
  55.6 6.9 %collective-permute-start.4 = (bf16[128,1024]{1,0:T(8,128)(2,1)S(1)}, bf16[128,1024]{1,0:T(8,128)(2,1)S(1)}, u32[]{:S(2)}, u32[]{:S(2)}) collective-permute-start(bf16[128,1024]{1,0:T(8,128)(2,1)S(1)} %get-tuple-element.13), channel_id=1, source_target_pairs={{0,1},{1,0},{2,3},{3,2},{4,5},{5,4},{6,7},{7,6},{8,9},{9,8},{10,11... | collective-permute-start | bytes 786440 | tf_op jit(solution)/shard_map/ppermute | solution.py:262
  55.7 11.1 %collective-permute-start.14 = (bf16[128,1024]{1,0:T(8,128)(2,1)S(1)}, bf16[128,1024]{1,0:T(8,128)(2,1)S(1)}, u32[]{:S(2)}, u32[]{:S(2)}) collective-permute-start(bf16[128,1024]{1,0:T(8,128)(2,1)S(1)} %add_convert_fusion.3), channel_id=1, source_target_pairs={{1,2},{2,1},{5,6},{6,5},{9,10},{10,9},{13,14},{14,13},{17,18},{18,... | collective-permute-start | bytes 786440 | tf_op jit(solution)/shard_map/ppermute | solution.py:265
  58.2 19.9 %collective-permute-start.23 = (bf16[128,1024]{1,0:T(8,128)(2,1)S(1)}, bf16[128,1024]{1,0:T(8,128)(2,1)S(1)}, u32[]{:S(2)}, u32[]{:S(2)}) collective-permute-start(bf16[128,1024]{1,0:T(8,128)(2,1)S(1)} %add_convert_fusion), channel_id=1, source_target_pairs={{1,2},{2,1},{5,6},{6,5},{9,10},{10,9},{13,14},{14,13},{17,18},{18,... | collective-permute-start | bytes 786440 | tf_op jit(solution)/shard_map/ppermute | solution.py:265
  62.5 12.8 %collective-permute-start.5 = (bf16[128,1024]{1,0:T(8,128)(2,1)S(1)}, bf16[128,1024]{1,0:T(8,128)(2,1)S(1)}, u32[]{:S(2)}, u32[]{:S(2)}) collective-permute-start(bf16[128,1024]{1,0:T(8,128)(2,1)S(1)} %add_convert_fusion.6), channel_id=1, source_target_pairs={{1,2},{2,1},{5,6},{6,5},{9,10},{10,9},{13,14},{14,13},{17,18},{18,... | collective-permute-start | bytes 786440 | tf_op jit(solution)/shard_map/ppermute | solution.py:265
  67.0 8.5 %collective-permute-start.15 = (bf16[128,1024]{1,0:T(8,128)(2,1)S(1)}, bf16[128,1024]{1,0:T(8,128)(2,1)S(1)}, u32[]{:S(2)}, u32[]{:S(2)}) collective-permute-start(bf16[128,1024]{1,0:T(8,128)(2,1)S(1)} %get-tuple-element.7), channel_id=1, source_target_pairs={{0,1},{1,0},{2,3},{3,2},{4,5},{5,4},{6,7},{7,6},{8,9},{9,8},{10,11... | collective-permute-start | bytes 786440 | tf_op jit(solution)/shard_map/ppermute | solution.py:262
  70.7 22.3 %collective-permute-start.28 = (bf16[128,2048]{1,0:T(8,128)(2,1)S(1)}, bf16[128,2048]{1,0:T(8,128)(2,1)S(1)}, u32[]{:S(2)}, u32[]{:S(2)}) collective-permute-start(bf16[128,2048]{1,0:T(8,128)(2,1)S(1)} %down.12), channel_id=1, source_target_pairs={{0,4},{4,0},{8,12},{12,8},{1,5},{5,1},{9,13},{13,9},{2,6},{6,2},{1... | collective-permute-start | bytes 1572872 | tf_op jit(solution)/shard_map/ppermute | solution.py:234
  75.5 8.4 %collective-permute-start.6 = (bf16[128,1024]{1,0:T(8,128)(2,1)S(1)}, bf16[128,1024]{1,0:T(8,128)(2,1)S(1)}, u32[]{:S(2)}, u32[]{:S(2)}) collective-permute-start(bf16[128,1024]{1,0:T(8,128)(2,1)S(1)} %get-tuple-element.11), channel_id=1, source_target_pairs={{0,1},{1,0},{2,3},{3,2},{4,5},{5,4},{6,7},{7,6},{8,9},{9,8},{10,11... | collective-permute-start | bytes 786440 | tf_op jit(solution)/shard_map/ppermute | solution.py:262
  75.7 11.1 %collective-permute-start.16 = (bf16[128,1024]{1,0:T(8,128)(2,1)S(1)}, bf16[128,1024]{1,0:T(8,128)(2,1)S(1)}, u32[]{:S(2)}, u32[]{:S(2)}) collective-permute-start(bf16[128,1024]{1,0:T(8,128)(2,1)S(1)} %add_convert_fusion.2), channel_id=1, source_target_pairs={{1,2},{2,1},{5,6},{6,5},{9,10},{10,9},{13,14},{14,13},{17,18},{18,... | collective-permute-start | bytes 786440 | tf_op jit(solution)/shard_map/ppermute | solution.py:265
  78.2 21.4 %collective-permute-start.24 = (bf16[128,1024]{1,0:T(8,128)(2,1)S(1)}, bf16[128,1024]{1,0:T(8,128)(2,1)S(1)}, u32[]{:S(2)}, u32[]{:S(2)}) collective-permute-start(bf16[128,1024]{1,0:T(8,128)(2,1)S(1)} %maximum_convert_fusion.refs_0_), channel_id=1, source_target_pairs={{0,1},{1,0},{2,3},{3,2},{4,5},{5,4},{6,7},{7,6},{8,9},{9,8},{10,11... | collective-permute-start | bytes 786440 | tf_op jit(solution)/shard_map/ppermute | solution.py:262
  86.7 13.5 %collective-permute-start.25 = (bf16[128,2048]{1,0:T(8,128)(2,1)S(1)}, bf16[128,2048]{1,0:T(8,128)(2,1)S(1)}, u32[]{:S(2)}, u32[]{:S(2)}) collective-permute-start(bf16[128,2048]{1,0:T(8,128)(2,1)S(1)} %down.9), channel_id=1, source_target_pairs={{0,4},{4,0},{8,12},{12,8},{1,5},{5,1},{9,13},{13,9},{2,6},{6,2},{1... | collective-permute-start | bytes 1572872 | tf_op jit(solution)/shard_map/ppermute | solution.py:234
  86.9 9.7 %collective-permute-start.17 = (bf16[128,1024]{1,0:T(8,128)(2,1)S(1)}, bf16[128,1024]{1,0:T(8,128)(2,1)S(1)}, u32[]{:S(2)}, u32[]{:S(2)}) collective-permute-start(bf16[128,1024]{1,0:T(8,128)(2,1)S(1)} %maximum_convert_fusion.2.refs_0_), channel_id=1, source_target_pairs={{0,1},{1,0},{2,3},{3,2},{4,5},{5,4},{6,7},{7,6},{8,9},{9,8},{10,11... | collective-permute-start | bytes 786440 | tf_op jit(solution)/shard_map/ppermute | solution.py:262
  87.6 16.7 %collective-permute-start.7 = (bf16[128,1024]{1,0:T(8,128)(2,1)S(1)}, bf16[128,1024]{1,0:T(8,128)(2,1)S(1)}, u32[]{:S(2)}, u32[]{:S(2)}) collective-permute-start(bf16[128,1024]{1,0:T(8,128)(2,1)S(1)} %add_convert_fusion.5), channel_id=1, source_target_pairs={{1,2},{2,1},{5,6},{6,5},{9,10},{10,9},{13,14},{14,13},{17,18},{18,... | collective-permute-start | bytes 786440 | tf_op jit(solution)/shard_map/ppermute | solution.py:265
  92.9 11.5 %collective-permute-start.27 = (bf16[128,2048]{1,0:T(8,128)(2,1)S(1)}, bf16[128,2048]{1,0:T(8,128)(2,1)S(1)}, u32[]{:S(2)}, u32[]{:S(2)}) collective-permute-start(bf16[128,2048]{1,0:T(8,128)(2,1)S(1)} %down.11), channel_id=1, source_target_pairs={{0,4},{4,0},{8,12},{12,8},{1,5},{5,1},{9,13},{13,9},{2,6},{6,2},{1... | collective-permute-start | bytes 1572872 | tf_op jit(solution)/shard_map/ppermute | solution.py:234
  96.5 14.9 %copy-start.4 = (f32[2048]{0:T(1024)S(1)}, f32[2048]{0:T(1024)}, u32[]{:S(2)}) copy-start(f32[2048]{0:T(1024)} %param.11) | copy-start | bytes 24580
  96.6 14.9 %collective-permute-start.29 = (bf16[128,2048]{1,0:T(8,128)(2,1)S(1)}, bf16[128,2048]{1,0:T(8,128)(2,1)S(1)}, u32[]{:S(2)}, u32[]{:S(2)}) collective-permute-start(bf16[128,2048]{1,0:T(8,128)(2,1)S(1)} %down.13), channel_id=1, source_target_pairs={{0,8},{4,12},{8,0},{12,4},{1,9},{5,13},{9,1},{13,5},{2,10},{6,14},... | collective-permute-start | bytes 1572872 | tf_op jit(solution)/shard_map/ppermute | solution.py:234
  99.6 15.1 %collective-permute-start.18 = (bf16[128,2048]{1,0:T(8,128)(2,1)S(1)}, bf16[128,2048]{1,0:T(8,128)(2,1)S(1)}, u32[]{:S(2)}, u32[]{:S(2)}) collective-permute-start(bf16[128,2048]{1,0:T(8,128)(2,1)S(1)} %down.8), channel_id=1, source_target_pairs={{0,4},{4,0},{8,12},{12,8},{1,5},{5,1},{9,13},{13,9},{2,6},{6,2},{1... | collective-permute-start | bytes 1572872 | tf_op jit(solution)/shard_map/ppermute | solution.py:234
  102.9 18.9 %collective-permute-start.26 = (bf16[128,2048]{1,0:T(8,128)(2,1)S(1)}, bf16[128,2048]{1,0:T(8,128)(2,1)S(1)}, u32[]{:S(2)}, u32[]{:S(2)}) collective-permute-start(bf16[128,2048]{1,0:T(8,128)(2,1)S(1)} %down.10), channel_id=1, source_target_pairs={{0,8},{4,12},{8,0},{12,4},{1,9},{5,13},{9,1},{13,5},{2,10},{6,14},... | collective-permute-start | bytes 1572872 | tf_op jit(solution)/shard_map/ppermute | solution.py:234
  104.4 10.3 %collective-permute-start.8 = (bf16[128,1024]{1,0:T(8,128)(2,1)S(1)}, bf16[128,1024]{1,0:T(8,128)(2,1)S(1)}, u32[]{:S(2)}, u32[]{:S(2)}) collective-permute-start(bf16[128,1024]{1,0:T(8,128)(2,1)S(1)} %maximum_convert_fusion.5.refs_0_), channel_id=1, source_target_pairs={{0,1},{1,0},{2,3},{3,2},{4,5},{5,4},{6,7},{7,6},{8,9},{9,8},{10,11... | collective-permute-start | bytes 786440 | tf_op jit(solution)/shard_map/ppermute | solution.py:262

commit v3 on v0

v3 whole, which is shorter than its diff:
```python
import functools

import jax
import jax.numpy as jnp
from jax import lax
from jax.experimental import pallas as pl
from jax.experimental.pallas import tpu as pltpu
from jax.sharding import PartitionSpec as P

BLK = 128
ANY = pl.BlockSpec(memory_space=pl.ANY)
SMEM = pl.BlockSpec(memory_space=pltpu.SMEM)
VMEM = pl.BlockSpec(memory_space=pltpu.VMEM)
MIB = 1024 * 1024
COST = 1
VMEM_LIMIT = 36 * MIB


def place(flip, step, per_owner):
    if flip is None:
        return step
    return (lax.axis_index("tensor") ^ flip) * per_owner + step


def projection(b, ids, counts, weight, x_buf, out, w_buf, sem):
    slots = ids.shape[2]
    per_shard = weight.shape[1] // BLK
    count = counts[0, b]

    def slab(s):
        block = lax.rem(ids[b, 0, s], per_shard)
        return pltpu.make_async_copy(
            weight.at[:, pl.ds(pl.multiple_of(block * BLK, BLK), BLK)],
            w_buf.at[:, pl.ds(s * BLK, BLK)],
            sem(s),
        )

    def start():
        for s in range(slots):
            pl.when(s < count)(lambda s=s: slab(s).start())

    def finish():
        for s in range(0, slots, 2):
            span = pl.ds(s * BLK, 2 * BLK)

            @pl.when(s < count)
            def _(s=s, span=span):
                slab(s).wait()
                pl.when(s + 1 < count)(lambda: slab(s + 1).wait())
                value = jnp.dot(x_buf[...], w_buf[:, span], preferred_element_type=jnp.float32)
                column = lax.broadcasted_iota(jnp.int32, value.shape, 1)
                live = (column < BLK) | (s + 1 < count)
                out[:, span] = jnp.where(live, value, 0.0).astype(out.dtype)

            @pl.when(s >= count)
            def _(span=span):
                out[:, span] = jnp.zeros((BLK, 2 * BLK), out.dtype)

    return start, finish


def fill_table(order, ids, counts, bias, out):
    slots = ids.shape[2]
    per_shard = bias.shape[0]
    for c, which in enumerate(order):
        b = place(*which)
        for s in range(slots):
            row = bias[pl.ds(lax.rem(ids[b, 0, s], per_shard), 1), :]
            out[pl.ds(c, 1), pl.ds(s * BLK, BLK)] = jnp.where(s < counts[0, b], row, 0.0)


def head_kernel(order, ids, counts, rows, weight, bias, out, low, high, table, w_buf, sems):
    slots = ids.shape[2]
    halves = [
        pltpu.make_async_copy(rows.at[pl.ds(j * BLK, BLK)], half, sems.at[slots + j])
        for j, half in enumerate((low, high))
    ]

    start, finish = projection(
        place(*order[0]), ids, counts, weight, low, out, w_buf, lambda s: sems.at[s]
    )
    for half in halves:
        half.start()
    start()
    fill_table(order, ids, counts, bias, table)
    for half in halves:
        half.wait()
    finish()


def head(order, ids, counts, rows, weight, bias):
    slots = ids.shape[2]
    width = weight.shape[0]
    return pl.pallas_call(
        functools.partial(head_kernel, order),
        out_shape=[
            jax.ShapeDtypeStruct((BLK, slots * BLK), jnp.bfloat16),
            jax.ShapeDtypeStruct((BLK, width), jnp.bfloat16),
            jax.ShapeDtypeStruct((BLK, width), jnp.bfloat16),
            jax.ShapeDtypeStruct((len(order), slots * BLK), jnp.float32),
        ],
        in_specs=[SMEM, SMEM, ANY, ANY, VMEM],
        out_specs=[VMEM] * 4,
        scratch_shapes=[
            pltpu.VMEM((width, slots * BLK), jnp.bfloat16),
            pltpu.SemaphoreType.DMA((slots + 2,)),
        ],
        compiler_params=pltpu.CompilerParams(vmem_limit_bytes=62 * MIB),
        cost_estimate=pl.CostEstimate(flops=COST, bytes_accessed=COST, transcendentals=0),
        name="head",
    )(ids, counts, rows, weight, bias)


def up_kernel(blocks, n_after, n_keep, ids, counts, weight, *refs):
    n_rows = [n for _, n in blocks]
    rows, refs = refs[: sum(n_rows)], refs[sum(n_rows) + n_after :]
    outs, kept = refs[: len(blocks)], refs[len(blocks) : len(blocks) + n_keep]
    x_buf, w_buf, sems, row_sems = refs[len(blocks) + n_keep :]
    fetches, steps = [], []
    for k, (which, n) in enumerate(blocks):
        height = BLK // n
        for part in range(n):
            at = len(fetches)
            fetches.append(
                pltpu.make_async_copy(
                    rows[at], x_buf.at[k, pl.ds(part * height, height)], row_sems.at[at]
                )
            )
        steps.append(
            projection(
                place(*which),
                ids,
                counts,
                weight,
                x_buf.at[k],
                outs[k],
                w_buf.at[k],
                lambda s, k=k: sems.at[k, s],
            )
        )
    for fetch in fetches:
        fetch.start()
    for start, _ in steps:
        start()
    for fetch in fetches:
        fetch.wait()
    for k, part in enumerate(kept):
        part[...] = x_buf[0, pl.ds(k * part.shape[0], part.shape[0]), :]
    for _, finish in steps:
        finish()


def up(whiches, ids, counts, rows, weight, after=(), keep=0):
    slots = ids.shape[2]
    width = weight.shape[0]
    count = len(whiches)
    parts = [part for block in rows for part in block]
    return pl.pallas_call(
        functools.partial(up_kernel, [(w, len(r)) for w, r in zip(whiches, rows)], len(after), keep),
        out_shape=[jax.ShapeDtypeStruct((BLK, slots * BLK), jnp.bfloat16)] * count
        + [jax.ShapeDtypeStruct((BLK // max(keep, 1), width), jnp.bfloat16)] * keep,
        in_specs=[SMEM, SMEM] + [ANY] * (1 + len(parts) + len(after)),
        out_specs=[VMEM] * (count + keep),
        scratch_shapes=[
            pltpu.VMEM((count, BLK, width), jnp.bfloat16),
            pltpu.VMEM((count, width, slots * BLK), jnp.bfloat16),
            pltpu.SemaphoreType.DMA((count, slots)),
            pltpu.SemaphoreType.DMA((len(parts),)),
        ],
        compiler_params=pltpu.CompilerParams(vmem_limit_bytes=VMEM_LIMIT),
        cost_estimate=pl.CostEstimate(flops=COST, bytes_accessed=COST, transcendentals=0),
        name="up",
    )(ids, counts, weight, *parts, *after)


def bias_table(order, ids, counts, bias):
    slots = ids.shape[2]
    return pl.pallas_call(
        functools.partial(fill_table, order),
        out_shape=jax.ShapeDtypeStruct((len(order), slots * BLK), jnp.float32),
        in_specs=[SMEM, SMEM, VMEM],
        out_specs=VMEM,
        compiler_params=pltpu.CompilerParams(vmem_limit_bytes=MIB),
        cost_estimate=pl.CostEstimate(flops=COST, bytes_accessed=COST, transcendentals=0),
        name="bias_table",
    )(ids, counts, bias)


def down_kernel(whiches, n_init, has_bias, n_after, two, n_parts, ids, counts, *refs):
    refs = list(refs)

    def take(n):
        taken = refs[:n]
        del refs[:n]
        return taken

    pairs = [take(2 if two else 1) for _ in whiches]
    (weight,) = take(1)
    inits = take(n_init)
    bias = take(has_bias)
    take(n_after)
    outs = [take(n_parts) for _ in whiches]
    h_buf, w_buf, acc, sems = refs
    slots = ids.shape[2]
    per_shard = weight.shape[0] // BLK
    position = lax.axis_index("dp")
    edge = (position == 0) | (position == lax.axis_size("dp") - 1)

    def slab(k, s):
        block = lax.rem(ids[place(*whiches[k]), 0, s], per_shard)
        return pltpu.make_async_copy(
            weight.at[pl.ds(pl.multiple_of(block * BLK, BLK), BLK)],
            w_buf.at[k, pl.ds(s * BLK, BLK)],
            sems.at[k, s],
        )

    def fetch(k, source):
        return pltpu.make_async_copy(source, h_buf.at[k], sems.at[k, slots])

    for k, which in enumerate(whiches):
        if two:
            pl.when(edge)(lambda k=k: fetch(k, pairs[k][1]).start())
            pl.when(jnp.logical_not(edge))(lambda k=k: fetch(k, pairs[k][0]).start())
        else:
            fetch(k, pairs[k][0]).start()
        for s in range(slots):
            pl.when(s < counts[0, place(*which)])(lambda k=k, s=s: slab(k, s).start())
    for k in range(len(whiches)):
        if bias and whiches[k][0] == 0:
            acc[k] = jnp.broadcast_to(bias[0][...], acc.shape[1:])
        elif not inits:
            acc[k] = jnp.zeros(acc.shape[1:], jnp.float32)
    for at, init in enumerate(inits):
        acc[0, pl.ds(at * init.shape[0], init.shape[0]), :] = init[...].astype(jnp.float32)
    for k, which in enumerate(whiches):
        count = counts[0, place(*which)]
        fetch(k, pairs[k][0]).wait()
        for s in range(0, slots, 2):

            @pl.when(s < count)
            def _(k=k, s=s, count=count):
                slab(k, s).wait()
                pl.when(s + 1 < count)(lambda: slab(k, s + 1).wait())

                @pl.when(s + 1 >= count)
                def _():
                    w_buf[k, pl.ds((s + 1) * BLK, BLK), :] = jnp.zeros((BLK, w_buf.shape[2]), w_buf.dtype)

                acc[k] += jnp.dot(
                    h_buf[k, :, pl.ds(s * BLK, 2 * BLK)],
                    w_buf[k, pl.ds(s * BLK, 2 * BLK), :],
                    preferred_element_type=jnp.float32,
                )

        for at, out in enumerate(outs[k]):
            out[...] = acc[k, pl.ds(at * out.shape[0], out.shape[0]), :].astype(out.dtype)


def down(whiches, ids, counts, pairs, weight, inits=(), bias=None, after=(), dtypes=(jnp.bfloat16,), parts=1):
    slots = ids.shape[2]
    width = weight.shape[1]
    count = len(whiches)
    two = len(pairs[0]) == 2
    extra = list(inits) + ([] if bias is None else [bias])
    out = pl.pallas_call(
        functools.partial(down_kernel, whiches, len(inits), bias is not None, len(after), two, parts),
        out_shape=[jax.ShapeDtypeStruct((BLK // parts, width), dtype) for dtype in dtypes for _ in range(parts)],
        in_specs=[SMEM, SMEM] + [ANY] * (count * len(pairs[0]) + 1) + [VMEM] * len(extra) + [ANY] * len(after),
        out_specs=[VMEM] * (parts * count),
        scratch_shapes=[
            pltpu.VMEM((count, BLK, slots * BLK), jnp.bfloat16),
            pltpu.VMEM((count, slots * BLK, width), jnp.bfloat16),
            pltpu.VMEM((count, BLK, width), jnp.float32),
            pltpu.SemaphoreType.DMA((count, slots + 1)),
        ],
        compiler_params=pltpu.CompilerParams(vmem_limit_bytes=VMEM_LIMIT),
        cost_estimate=pl.CostEstimate(flops=COST, bytes_accessed=COST, transcendentals=0),
        name="down",
    )(ids, counts, *[x for pair in pairs for x in pair], weight, *extra, *after)
    return [out[k * parts : (k + 1) * parts] for k in range(count)]


def active(total, bias):
    return jnp.maximum(total + bias, 0.0).astype(jnp.bfloat16)


def small(body, name, outs, operands, after):
    def run(*refs):
        body(*refs[: len(operands)], *refs[len(operands) + len(after) :])

    return pl.pallas_call(
        run,
        out_shape=outs,
        in_specs=[VMEM] * len(operands) + [ANY] * len(after),
        out_specs=jax.tree.map(lambda _: VMEM, outs),
        compiler_params=pltpu.CompilerParams(vmem_limit_bytes=VMEM_LIMIT),
        cost_estimate=pl.CostEstimate(flops=COST, bytes_accessed=COST, transcendentals=0),
        name=name,
    )(*operands, *after)


def fold(part, got, after):
    def body(part, got, out):
        out[...] = (part[...].astype(jnp.float32) + got[...].astype(jnp.float32)).astype(out.dtype)

    return small(body, "fold", jax.ShapeDtypeStruct(part.shape, part.dtype), [part, got], after)


def mix(i, folded, other, table, part, after):
    shape = jax.ShapeDtypeStruct(folded.shape, folded.dtype)

    def body(folded, other, table, *refs):
        total = folded[...].astype(jnp.float32) + other[...].astype(jnp.float32)
        value = active(total, table[i : i + 1, :])
        refs[-1][...] = value
        if part is not None:
            position = lax.axis_index("dp")
            edge = (position == 0) | (position == lax.axis_size("dp") - 1)
            out = refs[1]

            @pl.when(edge)
            def _():
                out[...] = refs[0][...]

            @pl.when(jnp.logical_not(edge))
            def _():
                out[...] = value

    if part is None:
        value = small(body, "mix", shape, [folded, other, table], after)
        return value, value
    sent, value = small(body, "mix", [shape, shape], [folded, other, table, part], after)
    return value, sent


def plain(rows_in, up_weight, up_bias, down_weight, down_bias, active_ids, active_counts):
    gathered = lax.all_gather(rows_in, "tensor", axis=0, tiled=True)
    order = [(None, b, 1) for b in range(gathered.shape[0] // BLK)]
    table = bias_table(order, active_ids, active_counts, up_bias.reshape(-1, BLK))
    terms = []
    for b, which in enumerate(order):
        (part,) = up([which], active_ids, active_counts, [[gathered[b * BLK : (b + 1) * BLK]]], up_weight)
        summed = lax.psum(part, "dp").astype(jnp.float32)
        hidden = active(summed, table[b : b + 1])
        terms.append(down([which], active_ids, active_counts, [[hidden]], down_weight)[0][0])
    terms = jnp.concatenate(terms, axis=0)
    owned = lax.psum_scatter(terms, "tensor", scatter_dimension=0, tiled=True).astype(jnp.float32)
    return owned + down_bias[None, :]


def staged(rows_in, up_weight, up_bias, down_weight, down_bias, active_ids, active_counts):
    f32 = jnp.float32
    order = [(f, j, 2) for f, j in ((0, 0), (1, 0), (0, 1), (3, 0), (2, 0), (3, 1), (2, 1), (1, 1))]
    steps = len(order)
    lag = 3

    def swap(parts, flip):
        return [lax.ppermute(part, "tensor", [(t, t ^ flip) for t in range(4)]) for part in parts]

    first, low, high, table = head(
        order, active_ids, active_counts, rows_in, up_weight, up_bias.reshape(-1, BLK)
    )
    mine = [[low], [high]]
    across = [swap(block, 3) for block in mine]
    beside = [swap(block, 1) for block in mine]
    relayed = {}
    source = {0: mine, 1: beside, 2: relayed, 3: across}
    partial, folded, other, hidden, got, terms, near, far, own = {0: first}, {}, {}, {}, {}, {}, {}, {}, {}
    after = first
    line = []

    def do_up(some, after, keep=0):
        rows = [source[order[i][0]][order[i][1]] for i in some]
        out = up([order[i] for i in some], active_ids, active_counts, rows, up_weight, [after], keep)
        partial.update(zip(some, out))
        return out[len(some) :]

    def do_down(some, after, **more):
        pairs = [(hidden[i], got[i + lag]) for i in some]
        return down([order[i] for i in some], active_ids, active_counts, pairs, down_weight, after=after, **more)

    ups = {0: [(1, 2, 7)], 2: [(3,)], 3: [(4,)], 4: [(5,)], 5: [(6,)]}
    downs = {7: [(3,)], 8: [(4,)], 9: [(5,)], 10: [(6,)], 11: [(7,), (0, 1, 2)]}
    for i in range(steps + lag + 1):
        back = i - lag
        latest = after
        if i < steps + lag:
            sent = partial.get(i)
            if back >= 0:
                hidden[back], sent = mix(back, folded[back], other[back], table, partial.get(i), [])
                latest = sent
            got[i] = lax.ppermute(sent, "dp", [(0, 1), (1, 0), (2, 3), (3, 2)])
        for some in ups.get(i, ()):
            flip, j, _ = order[some[0]]
            rows = do_up(some, partial[some[0] - 1], 2 if flip == 3 else 0)
            latest = partial[some[0]]
            if flip == 3:
                relayed[j] = swap(rows, 1)
        if 0 <= i - 1 < steps:
            latest = folded[i - 1] = fold(partial[i - 1], got[i - 1], [])
            other[i - 1] = lax.ppermute(latest, "dp", [(1, 2), (2, 1)])
        for some in downs.get(i, ()):
            flip, j, _ = order[some[0]]
            if flip == 0:
                dtypes = [f32 if order[k][0] == 0 else jnp.bfloat16 for k in some]
                out = do_down(some, [latest] + line + far[0], bias=down_bias[None, :], dtypes=dtypes)
                for k, value in zip(some, out):
                    flip, j, _ = order[k]
                    if flip == 0:
                        own[j] = value[0]
                    else:
                        near[j] = swap(value, 1)
                latest = out[0][0]
                line = [latest]
                continue
            (out,) = do_down(some, [latest] + line, inits=terms[j] if flip == 2 else (), parts=2)
            latest = out[0]
            line = [latest]
            {1: near, 2: far, 3: terms}[flip][j] = swap(out, 2 if flip == 2 else 1)
        after = latest

    def joined(parts):
        return jnp.concatenate(parts, axis=0).astype(f32)

    return jnp.concatenate([own[j] + joined(near[j]) + joined(far[j]) for j in range(2)], axis=0)


def solution(mesh):
    placed = (
        P(("parts", "tensor"), "dp"),
        P("dp", "tensor"),
        P("tensor"),
        P("tensor", "dp"),
        P("dp"),
        P("parts", "tensor", None),
        P("parts", "tensor"),
    )

    def run(rows_in, up_weight, up_bias, down_weight, down_bias, active_ids, active_counts):
        rest = (up_weight, up_bias, down_weight, down_bias, active_ids, active_counts.T)
        if mesh.shape["tensor"] == 4 and mesh.shape["dp"] == 4 and rows_in.shape[0] == 2 * BLK:
            return staged(rows_in, *rest)
        return plain(rows_in, *rest)

    return jax.shard_map(
        run, mesh=mesh, in_specs=placed, out_specs=P(("parts", "tensor"), "dp"), check_vma=False
    )
```

time: 390 us -> 110 us (0.28)
  the two profiles are of different devices: /device:TPU:12 before, /device:TPU:0 now
where the time goes in v3:
time: 110 us; the launch traced here: 108 us
  starting transfers between devices  50 us (45%)
  Pallas kernels  39.5 us (36%)
  waiting for transfers between devices  14.6 us (13%)
  local copies, waits for them, and re-layouts  2.02 us (2%)
  other arithmetic  1.83 us (2%)
    ppermute x11, starting transfers between devices, staged(): got[i] = lax.ppermute(sent, 'dp', [(0, 1), (1, 0), (2, 3), (3, 2)])  31.6 us
    pallas_call x6, Pallas kernels, down(): pl.pallas_call(functools.partial(down_kernel, whiches, len(inits), bias i...  18.4 us
    pallas_call x5, Pallas kernels, up(): pl.pallas_call(functools.partial(up_kernel, [(w, len(r)) for w, r in zip(...  15.5 us
    ppermute x19, starting transfers between devices, swap(): lax.ppermute(part, 'tensor', [(t, t ^ flip) for t in range(4)])  13.1 us
    ppermute x19, waiting for transfers between devices, swap(): lax.ppermute(part, 'tensor', [(t, t ^ flip) for t in range(4)])  10.3 us
    ppermute x8, starting transfers between devices, staged(): other[i - 1] = lax.ppermute(latest, 'dp', [(1, 2), (2, 1)])  5.42 us
    ppermute x11, waiting for transfers between devices, staged(): got[i] = lax.ppermute(sent, 'dp', [(0, 1), (1, 0), (2, 3), (3, 2)])  4.3 us
    pallas_call x1, Pallas kernels, head(): pl.pallas_call(functools.partial(head_kernel, order), out_shape=[jax.Shap...  4.24 us
  transfers between devices with their start and end apart: 38, of which 5 were waited for; matrix products, arithmetic and copies ran while one was open for 0% of the time, Pallas kernels for 33%

profile of v3, /device:TPU:0, one launch (start us, length us, event | category | flops | bytes accessed | tf_op | source)
XLA Modules:
  0.0 108.5 jit_solution(7624059283989477983)
XLA Ops:
  0.0 4.2 %head.1 = (bf16[128,1024]{1,0:T(8,128)(2,1)}, bf16[128,2048]{1,0:T(8,128)(2,1)}, bf16[128,2048]{1,0:T(8,128)(2,1)}, f32[8,1024]{1,0:T(8,128)}) custom-call(s32[8,1,8]{2,1,0:T(1,128)} %ids.23, s32[1,8]{1,0:T(1,128)} %bitcast.3, bf16[256,2048]{1,0:T(8,128)(2,1)} %rows.1, bf16[2048,8192]{1,0:T(8,128)(2,1)} %weight.11, f32[64,128]{1,0:T(8,128)} %bitcast.16), custom_call_target="tpu_custom_call" | custom-call | flops 1 | bytes 1 | tf_op jit(solution)/shard_map/head/pallas_call | solution.py:94
  4.3 1.2 %collective-permute-start.4 = (bf16[128,2048]{1,0:T(8,128)(2,1)}, bf16[128,2048]{1,0:T(8,128)(2,1)S(1)}, u32[]{:S(2)}, u32[]{:S(2)}) collective-permute-start(bf16[128,2048]{1,0:T(8,128)(2,1)} %get-tuple-element.44.refs_1_), channel_id=1, source_target_pairs={{0,4},{4,0},{8,12},{12,8},{1,5},{5,1},{9,13},{13,9},{2,6},{6,2},{1... | collective-permute-start | bytes 1572872 | tf_op jit(solution)/shard_map/ppermute | solution.py:358
  5.5 2.4 %collective-permute-start.2 = (bf16[128,2048]{1,0:T(8,128)(2,1)}, bf16[128,2048]{1,0:T(8,128)(2,1)S(1)}, u32[]{:S(2)}, u32[]{:S(2)}) collective-permute-start(bf16[128,2048]{1,0:T(8,128)(2,1)} %get-tuple-element.43), channel_id=1, source_target_pairs={{0,12},{4,8},{8,4},{12,0},{1,13},{5,9},{9,5},{13,1},{2,14},{6,10},... | collective-permute-start | bytes 1572872 | tf_op jit(solution)/shard_map/ppermute | solution.py:358
  7.9 1.6 %collective-permute-start = (bf16[128,1024]{1,0:T(8,128)(2,1)}, bf16[128,1024]{1,0:T(8,128)(2,1)S(1)}, u32[]{:S(2)}, u32[]{:S(2)}) collective-permute-start(bf16[128,1024]{1,0:T(8,128)(2,1)} %get-tuple-element.41.refs_0_.refs_3_), channel_id=1, source_target_pairs={{0,1},{1,0},{2,3},{3,2},{4,5},{5,4},{6,7},{7,6},{8,9},{9,8},{10,11... | collective-permute-start | bytes 786440 | tf_op jit(solution)/shard_map/ppermute | solution.py:392
  9.5 1.0 copy-done.1
  10.5 1.0 copy-done.4
  11.5 3.9 %up.5 = (bf16[128,1024]{1,0:T(8,128)(2,1)S(1)}, bf16[128,1024]{1,0:T(8,128)(2,1)S(1)}, bf16[128,1024]{1,0:T(8,128)(2,1)S(1)}) custom-call(s32[8,1,8]{2,1,0:T(1,128)S(1)} %copy-done.3, s32[1,8]{1,0:T(1,128)S(1)} %bitcast.4, bf16[2048,8192]{1,0:T(8,128)(2,1)} %weight.11, bf16[128,2048]{1,0:T(8,128)(2,1)S(1)} %collective-permute-done.3.refs_0_, ...), custom_call_target="tpu_custom_call" | custom-call | flops 1 | bytes 1 | tf_op jit(solution)/shard_map/up/pallas_call | solution.py:158
  15.4 0.9 collective-permute-start.6
  16.5 0.7 collective-permute-start.1
  17.2 1.6 %collective-permute-start.13 = (bf16[128,2048]{1,0:T(8,128)(2,1)S(1)}, bf16[128,2048]{1,0:T(8,128)(2,1)S(1)}, u32[]{:S(2)}, u32[]{:S(2)}) collective-permute-start(bf16[128,2048]{1,0:T(8,128)(2,1)S(1)} %copy-done.5), channel_id=1, source_target_pairs={{0,12},{4,8},{8,4},{12,0},{1,13},{5,9},{9,5},{13,1},{2,14},{6,10},... | collective-permute-start | bytes 1572872 | tf_op jit(solution)/shard_map/ppermute | solution.py:358
  18.8 4.1 %collective-permute-start.11 = (bf16[128,1024]{1,0:T(8,128)(2,1)S(1)}, bf16[128,1024]{1,0:T(8,128)(2,1)S(1)}, u32[]{:S(2)}, u32[]{:S(2)}) collective-permute-start(bf16[128,1024]{1,0:T(8,128)(2,1)S(1)} %get-tuple-element.45.refs_1_.refs_0_), channel_id=1, source_target_pairs={{0,1},{1,0},{2,3},{3,2},{4,5},{5,4},{6,7},{7,6},{8,9},{9,8},{10,11... | collective-permute-start | bytes 786440 | tf_op jit(solution)/shard_map/ppermute | solution.py:392
  22.9 2.6 %up.6 = (bf16[128,1024]{1,0:T(8,128)(2,1)S(1)}, bf16[64,2048]{1,0:T(8,128)(2,1)S(1)}, bf16[64,2048]{1,0:T(8,128)(2,1)S(1)}) custom-call(s32[8,1,8]{2,1,0:T(1,128)S(1)} %copy-done.3, s32[1,8]{1,0:T(1,128)S(1)} %bitcast.5, bf16[2048,8192]{1,0:T(8,128)(2,1)} %weight.11, bf16[128,2048]{1,0:T(8,128)(2,1)S(1)} %collective-permute-done.2.refs_0_, ...), custom_call_target="tpu_custom_call" | custom-call | flops 1 | bytes 1 | tf_op jit(solution)/shard_map/up/pallas_call | solution.py:158
  25.5 0.8 collective-permute-start.8
  26.5 0.7 collective-permute-start.7
  27.3 2.4 %collective-permute-done.11.refs_1_ = bf16[128,1024]{1,0:T(8,128)(2,1)S(1)} collective-permute-done((bf16[128,1024]{1,0:T(8,128)(2,1)S(1)}, bf16[128,1024]{1,0:T(8,128)(2,1)S(1)}, u32[]{:S(2)}, u32[]{:S(2)}) %collective-permute-start.11) | collective-permute-done | bytes 262176 | tf_op jit(solution)/shard_map/ppermute | solution.py:392
  29.7 2.5 %collective-permute-start.5 = (bf16[128,1024]{1,0:T(8,128)(2,1)S(1)}, bf16[128,1024]{1,0:T(8,128)(2,1)S(1)}, u32[]{:S(2)}, u32[]{:S(2)}) collective-permute-start(bf16[128,1024]{1,0:T(8,128)(2,1)S(1)} %get-tuple-element.48), channel_id=1, source_target_pairs={{0,1},{1,0},{2,3},{3,2},{4,5},{5,4},{6,7},{7,6},{8,9},{9,8},{10,11... | collective-permute-start | bytes 786440 | tf_op jit(solution)/shard_map/ppermute | solution.py:392
  32.2 0.7 collective-permute-start.12
  32.9 2.6 %up.7.refs_3_.refs_1_.refs_0_ = bf16[128,1024]{1,0:T(8,128)(2,1)S(1)} custom-call(s32[8,1,8]{2,1,0:T(1,128)S(1)} %copy-done.3, s32[1,8]{1,0:T(1,128)S(1)} %bitcast.6, bf16[2048,8192]{1,0:T(8,128)(2,1)} %weight.11, bf16[64,2048]{1,0:T(8,128)(2,1)S(1)} %collective-permute-done.8.refs_0_, bf16[64,2048]{1,0:T(8,128)(2,1)S(1)} %collective-permute-done.9.refs_1_, ...), custom_call_target="tpu_custom_call" | custom-call | flops 1 | bytes 1 | tf_op jit(solution)/shard_map/up/pallas_call | solution.py:158
  35.7 3.8 %collective-permute-start.10 = (bf16[128,1024]{1,0:T(8,128)(2,1)S(1)}, bf16[128,1024]{1,0:T(8,128)(2,1)S(1)}, u32[]{:S(2)}, u32[]{:S(2)}) collective-permute-start(bf16[128,1024]{1,0:T(8,128)(2,1)S(1)} %get-tuple-element.53), channel_id=1, source_target_pairs={{0,1},{1,0},{2,3},{3,2},{4,5},{5,4},{6,7},{7,6},{8,9},{9,8},{10,11... | collective-permute-start | bytes 786440 | tf_op jit(solution)/shard_map/ppermute | solution.py:392
  39.5 3.0 %up.8 = (bf16[128,1024]{1,0:T(8,128)(2,1)S(1)}, bf16[64,2048]{1,0:T(8,128)(2,1)S(1)}, bf16[64,2048]{1,0:T(8,128)(2,1)S(1)}) custom-call(s32[8,1,8]{2,1,0:T(1,128)S(1)} %copy-done.3, s32[1,8]{1,0:T(1,128)S(1)} %bitcast.7, bf16[2048,8192]{1,0:T(8,128)(2,1)} %weight.11, bf16[128,2048]{1,0:T(8,128)(2,1)S(1)} %collective-permute-done.13.refs_0_, ...), custom_call_target="tpu_custom_call" | custom-call | flops 1 | bytes 1 | tf_op jit(solution)/shard_map/up/pallas_call | solution.py:158
  42.6 0.5 collective-permute-start.20
  43.1 0.7 collective-permute-start.21
  43.9 3.1 %collective-permute-start.14 = (bf16[128,1024]{1,0:T(8,128)(2,1)S(1)}, bf16[128,1024]{1,0:T(8,128)(2,1)S(1)}, u32[]{:S(2)}, u32[]{:S(2)}) collective-permute-start(bf16[128,1024]{1,0:T(8,128)(2,1)S(1)} %get-tuple-element.56), channel_id=1, source_target_pairs={{0,1},{1,0},{2,3},{3,2},{4,5},{5,4},{6,7},{7,6},{8,9},{9,8},{10,11... | collective-permute-start | bytes 786440 | tf_op jit(solution)/shard_map/ppermute | solution.py:392
  47.1 0.7 collective-permute-start.15
  47.8 3.3 %up.9.refs_3_.refs_0_ = bf16[128,1024]{1,0:T(8,128)(2,1)S(1)} custom-call(s32[8,1,8]{2,1,0:T(1,128)S(1)} %copy-done.3, s32[1,8]{1,0:T(1,128)S(1)} %bitcast.8, bf16[2048,8192]{1,0:T(8,128)(2,1)} %weight.11, bf16[64,2048]{1,0:T(8,128)(2,1)S(1)} %collective-permute-done.19.refs_0_, bf16[64,2048]{1,0:T(8,128)(2,1)S(1)} %collective-permute-done.20.refs_1_, ...), custom_call_target="tpu_custom_call" | custom-call | flops 1 | bytes 1 | tf_op jit(solution)/shard_map/up/pallas_call | solution.py:158
  51.2 3.1 %collective-permute-start.22 = (bf16[128,1024]{1,0:T(8,128)(2,1)S(1)}, bf16[128,1024]{1,0:T(8,128)(2,1)S(1)}, u32[]{:S(2)}, u32[]{:S(2)}) collective-permute-start(bf16[128,1024]{1,0:T(8,128)(2,1)S(1)} %get-tuple-element.61), channel_id=1, source_target_pairs={{0,1},{1,0},{2,3},{3,2},{4,5},{5,4},{6,7},{7,6},{8,9},{9,8},{10,11... | collective-permute-start | bytes 786440 | tf_op jit(solution)/shard_map/ppermute | solution.py:392
  54.5 0.7 collective-permute-start.25
  55.3 4.3 %collective-permute-start.16 = (bf16[128,1024]{1,0:T(8,128)(2,1)S(1)}, bf16[128,1024]{1,0:T(8,128)(2,1)S(1)}, u32[]{:S(2)}, u32[]{:S(2)}) collective-permute-start(bf16[128,1024]{1,0:T(8,128)(2,1)S(1)} %get-tuple-element.58), channel_id=1, source_target_pairs={{0,1},{1,0},{2,3},{3,2},{4,5},{5,4},{6,7},{7,6},{8,9},{9,8},{10,11... | collective-permute-start | bytes 786440 | tf_op jit(solution)/shard_map/ppermute | solution.py:392
  59.6 0.7 collective-permute-start.23
  60.3 2.8 %down.6 = (bf16[64,2048]{1,0:T(8,128)(2,1)S(1)}, bf16[64,2048]{1,0:T(8,128)(2,1)S(1)}) custom-call(s32[8,1,8]{2,1,0:T(1,128)S(1)} %copy-done.3, s32[1,8]{1,0:T(1,128)S(1)} %bitcast.9, bf16[128,1024]{1,0:T(8,128)(2,1)S(1)} %get-tuple-element.63.refs_0_, bf16[128,1024]{1,0:T(8,128)(2,1)S(1)} %collective-permute-done.22.refs_1_, bf16[8192,2048]{1,0:T(8,128)(2,1)} %refs_6_.1, ...), custom_call_target="tpu_custom_call" | custom-call | flops 1 | bytes 1 | tf_op jit(solution)/shard_map/down/pallas_call | solution.py:265
  63.2 0.5 collective-permute-start.28
  63.8 4.5 %collective-permute-start.26 = (bf16[128,1024]{1,0:T(8,128)(2,1)S(1)}, bf16[128,1024]{1,0:T(8,128)(2,1)S(1)}, u32[]{:S(2)}, u32[]{:S(2)}) collective-permute-start(bf16[128,1024]{1,0:T(8,128)(2,1)S(1)} %mix.15.refs_0_), channel_id=1, source_target_pairs={{0,1},{1,0},{2,3},{3,2},{4,5},{5,4},{6,7},{7,6},{8,9},{9,8},{10,11... | collective-permute-start | bytes 786440 | tf_op jit(solution)/shard_map/ppermute | solution.py:392
  68.3 0.7 collective-permute-start.17
  69.1 1.7 %collective-permute-start.24 = (bf16[128,1024]{1,0:T(8,128)(2,1)S(1)}, bf16[128,1024]{1,0:T(8,128)(2,1)S(1)}, u32[]{:S(2)}, u32[]{:S(2)}) collective-permute-start(bf16[128,1024]{1,0:T(8,128)(2,1)S(1)} %mix.14.refs_3_.refs_0_), channel_id=1, source_target_pairs={{0,1},{1,0},{2,3},{3,2},{4,5},{5,4},{6,7},{7,6},{8,9},{9,8},{10,11... | collective-permute-start | bytes 786440 | tf_op jit(solution)/shard_map/ppermute | solution.py:392
  70.8 2.6 %down.7 = (bf16[64,2048]{1,0:T(8,128)(2,1)S(1)}, bf16[64,2048]{1,0:T(8,128)(2,1)S(1)}) custom-call(s32[8,1,8]{2,1,0:T(1,128)S(1)} %copy-done.3, s32[1,8]{1,0:T(1,128)S(1)} %bitcast.10, bf16[128,1024]{1,0:T(8,128)(2,1)S(1)} %get-tuple-element.62.refs_0_, bf16[128,1024]{1,0:T(8,128)(2,1)S(1)} %collective-permute-done.16.refs_1_, bf16[8192,2048]{1,0:T(8,128)(2,1)} %refs_6_.1, ...), custom_call_target="tpu_custom_call" | custom-call | flops 1 | bytes 1 | tf_op jit(solution)/shard_map/down/pallas_call | solution.py:265
  73.5 1.9 %collective-permute-done.26.refs_1_ = bf16[128,1024]{1,0:T(8,128)(2,1)S(1)} collective-permute-done((bf16[128,1024]{1,0:T(8,128)(2,1)S(1)}, bf16[128,1024]{1,0:T(8,128)(2,1)S(1)}, u32[]{:S(2)}, u32[]{:S(2)}) %collective-permute-start.26) | collective-permute-done | bytes 262176 | tf_op jit(solution)/shard_map/ppermute | solution.py:392
  75.3 2.9 %down.8 = (bf16[64,2048]{1,0:T(8,128)(2,1)S(1)}, bf16[64,2048]{1,0:T(8,128)(2,1)S(1)}) custom-call(s32[8,1,8]{2,1,0:T(1,128)S(1)} %copy-done.3, s32[1,8]{1,0:T(1,128)S(1)} %bitcast.11, bf16[128,1024]{1,0:T(8,128)(2,1)S(1)} %mix.15.refs_0_, bf16[128,1024]{1,0:T(8,128)(2,1)S(1)} %collective-permute-done.26.refs_1_, bf16[8192,2048]{1,0:T(8,128)(2,1)} %refs_6_.1, ...), custom_call_target="tpu_custom_call" | custom-call | flops 1 | bytes 1 | tf_op jit(solution)/shard_map/down/pallas_call | solution.py:265
  78.4 0.5 collective-permute-start.30
  79.0 2.1 %collective-permute-start.18 = (bf16[128,1024]{1,0:T(8,128)(2,1)S(1)}, bf16[128,1024]{1,0:T(8,128)(2,1)S(1)}, u32[]{:S(2)}, u32[]{:S(2)}) collective-permute-start(bf16[128,1024]{1,0:T(8,128)(2,1)S(1)} %mix.12.refs_5_.refs_0_), channel_id=1, source_target_pairs={{0,1},{1,0},{2,3},{3,2},{4,5},{5,4},{6,7},{7,6},{8,9},{9,8},{10,11... | collective-permute-start | bytes 786440 | tf_op jit(solution)/shard_map/ppermute | solution.py:392
  81.1 2.4 %collective-permute-start.31 = (bf16[64,2048]{1,0:T(8,128)(2,1)S(1)}, bf16[64,2048]{1,0:T(8,128)(2,1)S(1)}, u32[]{:S(2)}, u32[]{:S(2)}) collective-permute-start(bf16[64,2048]{1,0:T(8,128)(2,1)S(1)} %get-tuple-element.66.refs_4_), channel_id=1, source_target_pairs={{0,8},{4,12},{8,0},{12,4},{1,9},{5,13},{9,1},{13,5},{2,10},{6,14},... | collective-permute-start | bytes 786440 | tf_op jit(solution)/shard_map/ppermute | solution.py:358
  83.5 3.3 %down.9 = (bf16[64,2048]{1,0:T(8,128)(2,1)S(1)}, bf16[64,2048]{1,0:T(8,128)(2,1)S(1)}) custom-call(s32[8,1,8]{2,1,0:T(1,128)S(1)} %copy-done.3, s32[1,8]{1,0:T(1,128)S(1)} %bitcast.12, bf16[128,1024]{1,0:T(8,128)(2,1)S(1)} %mix.14.refs_3_.refs_0_, bf16[128,1024]{1,0:T(8,128)(2,1)S(1)} %collective-permute-done.24.refs_1_, bf16[8192,2048]{1,0:T(8,128)(2,1)} %refs_6_.1, ...), custom_call_target="tpu_custom_call" | custom-call | flops 1 | bytes 1 | tf_op jit(solution)/shard_map/down/pallas_call | solution.py:265
  86.8 2.1 %collective-permute-start.36 = (bf16[64,2048]{1,0:T(8,128)(2,1)S(1)}, bf16[64,2048]{1,0:T(8,128)(2,1)S(1)}, u32[]{:S(2)}, u32[]{:S(2)}) collective-permute-start(bf16[64,2048]{1,0:T(8,128)(2,1)S(1)} %get-tuple-element.69.refs_3_.refs_4_), channel_id=1, source_target_pairs={{0,8},{4,12},{8,0},{12,4},{1,9},{5,13},{9,1},{13,5},{2,10},{6,14},... | collective-permute-start | bytes 786440 | tf_op jit(solution)/shard_map/ppermute | solution.py:358
  88.9 2.6 %down.10 = (bf16[64,2048]{1,0:T(8,128)(2,1)S(1)}, bf16[64,2048]{1,0:T(8,128)(2,1)S(1)}) custom-call(s32[8,1,8]{2,1,0:T(1,128)S(1)} %copy-done.3, s32[1,8]{1,0:T(1,128)S(1)} %bitcast.13, bf16[128,1024]{1,0:T(8,128)(2,1)S(1)} %mix.12.refs_5_.refs_0_, bf16[128,1024]{1,0:T(8,128)(2,1)S(1)} %collective-permute-done.18.refs_1_, bf16[8192,2048]{1,0:T(8,128)(2,1)} %refs_6_.1, ...), custom_call_target="tpu_custom_call" | custom-call | flops 1 | bytes 1 | tf_op jit(solution)/shard_map/down/pallas_call | solution.py:265
  92.1 4.1 %collective-permute-done.32.refs_11_ = bf16[64,2048]{1,0:T(8,128)(2,1)S(1)} collective-permute-done((bf16[64,2048]{1,0:T(8,128)(2,1)S(1)}, bf16[64,2048]{1,0:T(8,128)(2,1)S(1)}, u32[]{:S(2)}, u32[]{:S(2)}) %collective-permute-start.32) | collective-permute-done | bytes 262176 | tf_op jit(solution)/shard_map/ppermute | solution.py:358
  96.2 4.1 %down.11 = (f32[128,2048]{1,0:T(8,128)S(1)}, bf16[128,2048]{1,0:T(8,128)(2,1)S(1)}, f32[128,2048]{1,0:T(8,128)S(1)}) custom-call(s32[8,1,8]{2,1,0:T(1,128)S(1)} %copy-done.3, s32[1,8]{1,0:T(1,128)S(1)} %bitcast.14, bf16[128,1024]{1,0:T(8,128)(2,1)S(1)} %get-tuple-element.47.refs_0_, bf16[128,1024]{1,0:T(8,128)(2,1)S(1)} %collective-permute-done.5.refs_1_, ...), custom_call_target="tpu_custom_call" | custom-call | flops 1 | bytes 1 | tf_op jit(solution)/shard_map/down/pallas_call | solution.py:265
  100.4 1.4 %collective-permute-done.36 = bf16[64,2048]{1,0:T(8,128)(2,1)S(1)} collective-permute-done((bf16[64,2048]{1,0:T(8,128)(2,1)S(1)}, bf16[64,2048]{1,0:T(8,128)(2,1)S(1)}, u32[]{:S(2)}, u32[]{:S(2)}) %collective-permute-start.36) | collective-permute-done | bytes 262176 | tf_op jit(solution)/shard_map/ppermute | solution.py:358
  101.8 4.7 %collective-permute-done.37 = bf16[64,2048]{1,0:T(8,128)(2,1)S(1)} collective-permute-done((bf16[64,2048]{1,0:T(8,128)(2,1)S(1)}, bf16[64,2048]{1,0:T(8,128)(2,1)S(1)}, u32[]{:S(2)}, u32[]{:S(2)}) %collective-permute-start.37) | collective-permute-done | bytes 262176 | tf_op jit(solution)/shard_map/ppermute | solution.py:358
  107.0 1.5 %pad_maximum_fusion = f32[256,2048]{1,0:T(8,128)} fusion(f32[128,2048]{1,0:T(8,128)S(1)} %convert_add_fusion, f32[128,2048]{1,0:T(8,128)S(1)} %convert_add_fusion.1), kind=kLoop, calls=%fused_computation | loop fusion | flops 524288 | bytes 4194304 | tf_op jit(solution)/shard_map/concatenate | solution.py:425
  (75 shorter events, 3.0 us)
Async XLA Ops:
  0.0 9.5 %copy-start.3 = (s32[8,1,8]{2,1,0:T(1,128)S(1)}, s32[8,1,8]{2,1,0:T(1,128)}, u32[]{:S(2)}) copy-start(s32[8,1,8]{2,1,0:T(1,128)} %ids.23) | copy-start | bytes 772
  0.0 9.5 %copy-start.6 = (s32[8,1]{0,1:T(1,128)S(1)}, s32[8,1]{0,1:T(1,128)}, u32[]{:S(2)}) copy-start(s32[8,1]{0,1:T(1,128)} %param.13) | copy-start | bytes 100
  4.3 5.2 %collective-permute-start.4 = (bf16[128,2048]{1,0:T(8,128)(2,1)}, bf16[128,2048]{1,0:T(8,128)(2,1)S(1)}, u32[]{:S(2)}, u32[]{:S(2)}) collective-permute-start(bf16[128,2048]{1,0:T(8,128)(2,1)} %get-tuple-element.44.refs_1_), channel_id=1, source_target_pairs={{0,4},{4,0},{8,12},{12,8},{1,5},{5,1},{9,13},{13,9},{2,6},{6,2},{1... | collective-permute-start | bytes 1572872 | tf_op jit(solution)/shard_map/ppermute | solution.py:358
  5.5 4.0 %collective-permute-start.3 = (bf16[128,2048]{1,0:T(8,128)(2,1)}, bf16[128,2048]{1,0:T(8,128)(2,1)S(1)}, u32[]{:S(2)}, u32[]{:S(2)}) collective-permute-start(bf16[128,2048]{1,0:T(8,128)(2,1)} %get-tuple-element.43), channel_id=1, source_target_pairs={{0,4},{4,0},{8,12},{12,8},{1,5},{5,1},{9,13},{13,9},{2,6},{6,2},{1... | collective-permute-start | bytes 1572872 | tf_op jit(solution)/shard_map/ppermute | solution.py:358
  5.5 17.3 %collective-permute-start.2 = (bf16[128,2048]{1,0:T(8,128)(2,1)}, bf16[128,2048]{1,0:T(8,128)(2,1)S(1)}, u32[]{:S(2)}, u32[]{:S(2)}) collective-permute-start(bf16[128,2048]{1,0:T(8,128)(2,1)} %get-tuple-element.43), channel_id=1, source_target_pairs={{0,12},{4,8},{8,4},{12,0},{1,13},{5,9},{9,5},{13,1},{2,14},{6,10},... | collective-permute-start | bytes 1572872 | tf_op jit(solution)/shard_map/ppermute | solution.py:358
  7.9 8.5 %collective-permute-start = (bf16[128,1024]{1,0:T(8,128)(2,1)}, bf16[128,1024]{1,0:T(8,128)(2,1)S(1)}, u32[]{:S(2)}, u32[]{:S(2)}) collective-permute-start(bf16[128,1024]{1,0:T(8,128)(2,1)} %get-tuple-element.41.refs_0_.refs_3_), channel_id=1, source_target_pairs={{0,1},{1,0},{2,3},{3,2},{4,5},{5,4},{6,7},{7,6},{8,9},{9,8},{10,11... | collective-permute-start | bytes 786440 | tf_op jit(solution)/shard_map/ppermute | solution.py:392
  9.5 1.0 copy-start.1
  10.5 1.0 copy-start.4
  11.5 4.9 %copy-start.2 = (bf16[128,1024]{1,0:T(8,128)(2,1)S(1)}, bf16[128,1024]{1,0:T(8,128)(2,1)}, u32[]{:S(2)}) copy-start(bf16[128,1024]{1,0:T(8,128)(2,1)} %get-tuple-element.41.refs_0_.refs_3_) | copy-start | bytes 786436
  11.5 5.6 %copy-start.5 = (bf16[128,2048]{1,0:T(8,128)(2,1)S(1)}, bf16[128,2048]{1,0:T(8,128)(2,1)}, u32[]{:S(2)}) copy-start(bf16[128,2048]{1,0:T(8,128)(2,1)} %get-tuple-element.44.refs_1_) | copy-start | bytes 1572868
  15.4 10.9 %collective-permute-start.6 = (bf16[128,1024]{1,0:T(8,128)(2,1)S(1)}, bf16[128,1024]{1,0:T(8,128)(2,1)S(1)}, u32[]{:S(2)}, u32[]{:S(2)}) collective-permute-start(bf16[128,1024]{1,0:T(8,128)(2,1)S(1)} %get-tuple-element.49.refs_0_), channel_id=1, source_target_pairs={{0,1},{1,0},{2,3},{3,2},{4,5},{5,4},{6,7},{7,6},{8,9},{9,8},{10,11... | collective-permute-start | bytes 786440 | tf_op jit(solution)/shard_map/ppermute | solution.py:392
  16.5 10.0 %collective-permute-start.1 = (bf16[128,1024]{1,0:T(8,128)(2,1)S(1)}, bf16[128,1024]{1,0:T(8,128)(2,1)S(1)}, u32[]{:S(2)}, u32[]{:S(2)}) collective-permute-start(bf16[128,1024]{1,0:T(8,128)(2,1)S(1)} %fold.8.refs_0_), channel_id=1, source_target_pairs={{1,2},{2,1},{5,6},{6,5},{9,10},{10,9},{13,14},{14,13},{17,18},{18,... | collective-permute-start | bytes 786440 | tf_op jit(solution)/shard_map/ppermute | solution.py:401
  17.2 22.3 %collective-permute-start.13 = (bf16[128,2048]{1,0:T(8,128)(2,1)S(1)}, bf16[128,2048]{1,0:T(8,128)(2,1)S(1)}, u32[]{:S(2)}, u32[]{:S(2)}) collective-permute-start(bf16[128,2048]{1,0:T(8,128)(2,1)S(1)} %copy-done.5), channel_id=1, source_target_pairs={{0,12},{4,8},{8,4},{12,0},{1,13},{5,9},{9,5},{13,1},{2,14},{6,10},... | collective-permute-start | bytes 1572872 | tf_op jit(solution)/shard_map/ppermute | solution.py:358
  18.8 8.4 %copy-start = (f32[8,1024]{1,0:T(8,128)S(1)}, f32[8,1024]{1,0:T(8,128)}, u32[]{:S(2)}) copy-start(f32[8,1024]{1,0:T(8,128)} %get-tuple-element.42.refs_2_) | copy-start | bytes 98308
  18.8 10.9 %collective-permute-start.11 = (bf16[128,1024]{1,0:T(8,128)(2,1)S(1)}, bf16[128,1024]{1,0:T(8,128)(2,1)S(1)}, u32[]{:S(2)}, u32[]{:S(2)}) collective-permute-start(bf16[128,1024]{1,0:T(8,128)(2,1)S(1)} %get-tuple-element.45.refs_1_.refs_0_), channel_id=1, source_target_pairs={{0,1},{1,0},{2,3},{3,2},{4,5},{5,4},{6,7},{7,6},{8,9},{9,8},{10,11... | collective-permute-start | bytes 786440 | tf_op jit(solution)/shard_map/ppermute | solution.py:392
  25.5 6.7 %collective-permute-start.8 = (bf16[64,2048]{1,0:T(8,128)(2,1)S(1)}, bf16[64,2048]{1,0:T(8,128)(2,1)S(1)}, u32[]{:S(2)}, u32[]{:S(2)}) collective-permute-start(bf16[64,2048]{1,0:T(8,128)(2,1)S(1)} %get-tuple-element.50), channel_id=1, source_target_pairs={{0,4},{4,0},{8,12},{12,8},{1,5},{5,1},{9,13},{13,9},{2,6},{6,2},{1... | collective-permute-start | bytes 786440 | tf_op jit(solution)/shard_map/ppermute | solution.py:358
  26.3 6.6 %collective-permute-start.9 = (bf16[64,2048]{1,0:T(8,128)(2,1)S(1)}, bf16[64,2048]{1,0:T(8,128)(2,1)S(1)}, u32[]{:S(2)}, u32[]{:S(2)}) collective-permute-start(bf16[64,2048]{1,0:T(8,128)(2,1)S(1)} %get-tuple-element.51), channel_id=1, source_target_pairs={{0,4},{4,0},{8,12},{12,8},{1,5},{5,1},{9,13},{13,9},{2,6},{6,2},{1... | collective-permute-start | bytes 786440 | tf_op jit(solution)/shard_map/ppermute | solution.py:358
  26.5 9.1 %collective-permute-start.7 = (bf16[128,1024]{1,0:T(8,128)(2,1)S(1)}, bf16[128,1024]{1,0:T(8,128)(2,1)S(1)}, u32[]{:S(2)}, u32[]{:S(2)}) collective-permute-start(bf16[128,1024]{1,0:T(8,128)(2,1)S(1)} %fold.9.refs_0_), channel_id=1, source_target_pairs={{1,2},{2,1},{5,6},{6,5},{9,10},{10,9},{13,14},{14,13},{17,18},{18,... | collective-permute-start | bytes 786440 | tf_op jit(solution)/shard_map/ppermute | solution.py:401
  29.7 13.4 %collective-permute-start.5 = (bf16[128,1024]{1,0:T(8,128)(2,1)S(1)}, bf16[128,1024]{1,0:T(8,128)(2,1)S(1)}, u32[]{:S(2)}, u32[]{:S(2)}) collective-permute-start(bf16[128,1024]{1,0:T(8,128)(2,1)S(1)} %get-tuple-element.48), channel_id=1, source_target_pairs={{0,1},{1,0},{2,3},{3,2},{4,5},{5,4},{6,7},{7,6},{8,9},{9,8},{10,11... | collective-permute-start | bytes 786440 | tf_op jit(solution)/shard_map/ppermute | solution.py:392
  32.2 11.6 %collective-permute-start.12 = (bf16[128,1024]{1,0:T(8,128)(2,1)S(1)}, bf16[128,1024]{1,0:T(8,128)(2,1)S(1)}, u32[]{:S(2)}, u32[]{:S(2)}) collective-permute-start(bf16[128,1024]{1,0:T(8,128)(2,1)S(1)} %fold.10.refs_0_), channel_id=1, source_target_pairs={{1,2},{2,1},{5,6},{6,5},{9,10},{10,9},{13,14},{14,13},{17,18},{18,... | collective-permute-start | bytes 786440 | tf_op jit(solution)/shard_map/ppermute | solution.py:401
  35.7 11.3 %collective-permute-start.10 = (bf16[128,1024]{1,0:T(8,128)(2,1)S(1)}, bf16[128,1024]{1,0:T(8,128)(2,1)S(1)}, u32[]{:S(2)}, u32[]{:S(2)}) collective-permute-start(bf16[128,1024]{1,0:T(8,128)(2,1)S(1)} %get-tuple-element.53), channel_id=1, source_target_pairs={{0,1},{1,0},{2,3},{3,2},{4,5},{5,4},{6,7},{7,6},{8,9},{9,8},{10,11... | collective-permute-start | bytes 786440 | tf_op jit(solution)/shard_map/ppermute | solution.py:392
  42.5 5.3 %collective-permute-start.19 = (bf16[64,2048]{1,0:T(8,128)(2,1)S(1)}, bf16[64,2048]{1,0:T(8,128)(2,1)S(1)}, u32[]{:S(2)}, u32[]{:S(2)}) collective-permute-start(bf16[64,2048]{1,0:T(8,128)(2,1)S(1)} %get-tuple-element.59), channel_id=1, source_target_pairs={{0,4},{4,0},{8,12},{12,8},{1,5},{5,1},{9,13},{13,9},{2,6},{6,2},{1... | collective-permute-start | bytes 786440 | tf_op jit(solution)/shard_map/ppermute | solution.py:358
  42.6 5.2 %collective-permute-start.20 = (bf16[64,2048]{1,0:T(8,128)(2,1)S(1)}, bf16[64,2048]{1,0:T(8,128)(2,1)S(1)}, u32[]{:S(2)}, u32[]{:S(2)}) collective-permute-start(bf16[64,2048]{1,0:T(8,128)(2,1)S(1)} %get-tuple-element.60), channel_id=1, source_target_pairs={{0,4},{4,0},{8,12},{12,8},{1,5},{5,1},{9,13},{13,9},{2,6},{6,2},{1... | collective-permute-start | bytes 786440 | tf_op jit(solution)/shard_map/ppermute | solution.py:358
  43.1 8.0 %collective-permute-start.21 = (bf16[128,1024]{1,0:T(8,128)(2,1)S(1)}, bf16[128,1024]{1,0:T(8,128)(2,1)S(1)}, u32[]{:S(2)}, u32[]{:S(2)}) collective-permute-start(bf16[128,1024]{1,0:T(8,128)(2,1)S(1)} %fold.13.refs_0_), channel_id=1, source_target_pairs={{1,2},{2,1},{5,6},{6,5},{9,10},{10,9},{13,14},{14,13},{17,18},{18,... | collective-permute-start | bytes 786440 | tf_op jit(solution)/shard_map/ppermute | solution.py:401
  43.9 10.4 %collective-permute-start.14 = (bf16[128,1024]{1,0:T(8,128)(2,1)S(1)}, bf16[128,1024]{1,0:T(8,128)(2,1)S(1)}, u32[]{:S(2)}, u32[]{:S(2)}) collective-permute-start(bf16[128,1024]{1,0:T(8,128)(2,1)S(1)} %get-tuple-element.56), channel_id=1, source_target_pairs={{0,1},{1,0},{2,3},{3,2},{4,5},{5,4},{6,7},{7,6},{8,9},{9,8},{10,11... | collective-permute-start | bytes 786440 | tf_op jit(solution)/shard_map/ppermute | solution.py:392
  47.1 8.1 %collective-permute-start.15 = (bf16[128,1024]{1,0:T(8,128)(2,1)S(1)}, bf16[128,1024]{1,0:T(8,128)(2,1)S(1)}, u32[]{:S(2)}, u32[]{:S(2)}) collective-permute-start(bf16[128,1024]{1,0:T(8,128)(2,1)S(1)} %fold.11.refs_0_), channel_id=1, source_target_pairs={{1,2},{2,1},{5,6},{6,5},{9,10},{10,9},{13,14},{14,13},{17,18},{18,... | collective-permute-start | bytes 786440 | tf_op jit(solution)/shard_map/ppermute | solution.py:401
  51.2 8.3 %collective-permute-start.22 = (bf16[128,1024]{1,0:T(8,128)(2,1)S(1)}, bf16[128,1024]{1,0:T(8,128)(2,1)S(1)}, u32[]{:S(2)}, u32[]{:S(2)}) collective-permute-start(bf16[128,1024]{1,0:T(8,128)(2,1)S(1)} %get-tuple-element.61), channel_id=1, source_target_pairs={{0,1},{1,0},{2,3},{3,2},{4,5},{5,4},{6,7},{7,6},{8,9},{9,8},{10,11... | collective-permute-start | bytes 786440 | tf_op jit(solution)/shard_map/ppermute | solution.py:392
  54.5 9.2 %collective-permute-start.25 = (bf16[128,1024]{1,0:T(8,128)(2,1)S(1)}, bf16[128,1024]{1,0:T(8,128)(2,1)S(1)}, u32[]{:S(2)}, u32[]{:S(2)}) collective-permute-start(bf16[128,1024]{1,0:T(8,128)(2,1)S(1)} %fold.15.refs_0_), channel_id=1, source_target_pairs={{1,2},{2,1},{5,6},{6,5},{9,10},{10,9},{13,14},{14,13},{17,18},{18,... | collective-permute-start | bytes 786440 | tf_op jit(solution)/shard_map/ppermute | solution.py:401
  55.3 13.0 %collective-permute-start.16 = (bf16[128,1024]{1,0:T(8,128)(2,1)S(1)}, bf16[128,1024]{1,0:T(8,128)(2,1)S(1)}, u32[]{:S(2)}, u32[]{:S(2)}) collective-permute-start(bf16[128,1024]{1,0:T(8,128)(2,1)S(1)} %get-tuple-element.58), channel_id=1, source_target_pairs={{0,1},{1,0},{2,3},{3,2},{4,5},{5,4},{6,7},{7,6},{8,9},{9,8},{10,11... | collective-permute-start | bytes 786440 | tf_op jit(solution)/shard_map/ppermute | solution.py:392
  59.6 9.4 %collective-permute-start.23 = (bf16[128,1024]{1,0:T(8,128)(2,1)S(1)}, bf16[128,1024]{1,0:T(8,128)(2,1)S(1)}, u32[]{:S(2)}, u32[]{:S(2)}) collective-permute-start(bf16[128,1024]{1,0:T(8,128)(2,1)S(1)} %fold.14.refs_0_.refs_3_), channel_id=1, source_target_pairs={{1,2},{2,1},{5,6},{6,5},{9,10},{10,9},{13,14},{14,13},{17,18},{18,... | collective-permute-start | bytes 786440 | tf_op jit(solution)/shard_map/ppermute | solution.py:401
  63.1 7.7 %collective-permute-start.27 = (bf16[64,2048]{1,0:T(8,128)(2,1)S(1)}, bf16[64,2048]{1,0:T(8,128)(2,1)S(1)}, u32[]{:S(2)}, u32[]{:S(2)}) collective-permute-start(bf16[64,2048]{1,0:T(8,128)(2,1)S(1)} %get-tuple-element.64.refs_6_), channel_id=1, source_target_pairs={{0,4},{4,0},{8,12},{12,8},{1,5},{5,1},{9,13},{13,9},{2,6},{6,2},{1... | collective-permute-start | bytes 786440 | tf_op jit(solution)/shard_map/ppermute | solution.py:358
  63.2 7.6 %collective-permute-start.28 = (bf16[64,2048]{1,0:T(8,128)(2,1)S(1)}, bf16[64,2048]{1,0:T(8,128)(2,1)S(1)}, u32[]{:S(2)}, u32[]{:S(2)}) collective-permute-start(bf16[64,2048]{1,0:T(8,128)(2,1)S(1)} %get-tuple-element.65), channel_id=1, source_target_pairs={{0,4},{4,0},{8,12},{12,8},{1,5},{5,1},{9,13},{13,9},{2,6},{6,2},{1... | collective-permute-start | bytes 786440 | tf_op jit(solution)/shard_map/ppermute | solution.py:358
  63.8 11.6 %collective-permute-start.26 = (bf16[128,1024]{1,0:T(8,128)(2,1)S(1)}, bf16[128,1024]{1,0:T(8,128)(2,1)S(1)}, u32[]{:S(2)}, u32[]{:S(2)}) collective-permute-start(bf16[128,1024]{1,0:T(8,128)(2,1)S(1)} %mix.15.refs_0_), channel_id=1, source_target_pairs={{0,1},{1,0},{2,3},{3,2},{4,5},{5,4},{6,7},{7,6},{8,9},{9,8},{10,11... | collective-permute-start | bytes 786440 | tf_op jit(solution)/shard_map/ppermute | solution.py:392
  68.3 10.6 %collective-permute-start.17 = (bf16[128,1024]{1,0:T(8,128)(2,1)S(1)}, bf16[128,1024]{1,0:T(8,128)(2,1)S(1)}, u32[]{:S(2)}, u32[]{:S(2)}) collective-permute-start(bf16[128,1024]{1,0:T(8,128)(2,1)S(1)} %fold.12.refs_0_.refs_5_), channel_id=1, source_target_pairs={{1,2},{2,1},{5,6},{6,5},{9,10},{10,9},{13,14},{14,13},{17,18},{18,... | collective-permute-start | bytes 786440 | tf_op jit(solution)/shard_map/ppermute | solution.py:401
  69.1 14.4 %collective-permute-start.24 = (bf16[128,1024]{1,0:T(8,128)(2,1)S(1)}, bf16[128,1024]{1,0:T(8,128)(2,1)S(1)}, u32[]{:S(2)}, u32[]{:S(2)}) collective-permute-start(bf16[128,1024]{1,0:T(8,128)(2,1)S(1)} %mix.14.refs_3_.refs_0_), channel_id=1, source_target_pairs={{0,1},{1,0},{2,3},{3,2},{4,5},{5,4},{6,7},{7,6},{8,9},{9,8},{10,11... | collective-permute-start | bytes 786440 | tf_op jit(solution)/shard_map/ppermute | solution.py:392
  78.3 5.2 %collective-permute-start.29 = (bf16[64,2048]{1,0:T(8,128)(2,1)S(1)}, bf16[64,2048]{1,0:T(8,128)(2,1)S(1)}, u32[]{:S(2)}, u32[]{:S(2)}) collective-permute-start(bf16[64,2048]{1,0:T(8,128)(2,1)S(1)} %get-tuple-element.67.refs_6_), channel_id=1, source_target_pairs={{0,4},{4,0},{8,12},{12,8},{1,5},{5,1},{9,13},{13,9},{2,6},{6,2},{1... | collective-permute-start | bytes 786440 | tf_op jit(solution)/shard_map/ppermute | solution.py:358
  78.4 5.2 %collective-permute-start.30 = (bf16[64,2048]{1,0:T(8,128)(2,1)S(1)}, bf16[64,2048]{1,0:T(8,128)(2,1)S(1)}, u32[]{:S(2)}, u32[]{:S(2)}) collective-permute-start(bf16[64,2048]{1,0:T(8,128)(2,1)S(1)} %get-tuple-element.68), channel_id=1, source_target_pairs={{0,4},{4,0},{8,12},{12,8},{1,5},{5,1},{9,13},{13,9},{2,6},{6,2},{1... | collective-permute-start | bytes 786440 | tf_op jit(solution)/shard_map/ppermute | solution.py:358
  79.0 10.0 %collective-permute-start.18 = (bf16[128,1024]{1,0:T(8,128)(2,1)S(1)}, bf16[128,1024]{1,0:T(8,128)(2,1)S(1)}, u32[]{:S(2)}, u32[]{:S(2)}) collective-permute-start(bf16[128,1024]{1,0:T(8,128)(2,1)S(1)} %mix.12.refs_5_.refs_0_), channel_id=1, source_target_pairs={{0,1},{1,0},{2,3},{3,2},{4,5},{5,4},{6,7},{7,6},{8,9},{9,8},{10,11... | collective-permute-start | bytes 786440 | tf_op jit(solution)/shard_map/ppermute | solution.py:392
  81.1 10.6 %collective-permute-start.31 = (bf16[64,2048]{1,0:T(8,128)(2,1)S(1)}, bf16[64,2048]{1,0:T(8,128)(2,1)S(1)}, u32[]{:S(2)}, u32[]{:S(2)}) collective-permute-start(bf16[64,2048]{1,0:T(8,128)(2,1)S(1)} %get-tuple-element.66.refs_4_), channel_id=1, source_target_pairs={{0,8},{4,12},{8,0},{12,4},{1,9},{5,13},{9,1},{13,5},{2,10},{6,14},... | collective-permute-start | bytes 786440 | tf_op jit(solution)/shard_map/ppermute | solution.py:358
  83.5 12.8 %collective-permute-start.32 = (bf16[64,2048]{1,0:T(8,128)(2,1)S(1)}, bf16[64,2048]{1,0:T(8,128)(2,1)S(1)}, u32[]{:S(2)}, u32[]{:S(2)}) collective-permute-start(bf16[64,2048]{1,0:T(8,128)(2,1)S(1)} %get-tuple-element.71), channel_id=1, source_target_pairs={{0,8},{4,12},{8,0},{12,4},{1,9},{5,13},{9,1},{13,5},{2,10},{6,14},... | collective-permute-start | bytes 786440 | tf_op jit(solution)/shard_map/ppermute | solution.py:358
  86.8 15.1 %collective-permute-start.36 = (bf16[64,2048]{1,0:T(8,128)(2,1)S(1)}, bf16[64,2048]{1,0:T(8,128)(2,1)S(1)}, u32[]{:S(2)}, u32[]{:S(2)}) collective-permute-start(bf16[64,2048]{1,0:T(8,128)(2,1)S(1)} %get-tuple-element.69.refs_3_.refs_4_), channel_id=1, source_target_pairs={{0,8},{4,12},{8,0},{12,4},{1,9},{5,13},{9,1},{13,5},{2,10},{6,14},... | collective-permute-start | bytes 786440 | tf_op jit(solution)/shard_map/ppermute | solution.py:358
  88.8 7.4 %copy-start.7 = (f32[2048]{0:T(1024)S(1)}, f32[2048]{0:T(1024)}, u32[]{:S(2)}) copy-start(f32[2048]{0:T(1024)} %param.11) | copy-start | bytes 24580
  88.8 17.7 %collective-permute-start.37 = (bf16[64,2048]{1,0:T(8,128)(2,1)S(1)}, bf16[64,2048]{1,0:T(8,128)(2,1)S(1)}, u32[]{:S(2)}, u32[]{:S(2)}) collective-permute-start(bf16[64,2048]{1,0:T(8,128)(2,1)S(1)} %get-tuple-element.76), channel_id=1, source_target_pairs={{0,8},{4,12},{8,0},{12,4},{1,9},{5,13},{9,1},{13,5},{2,10},{6,14},... | collective-permute-start | bytes 786440 | tf_op jit(solution)/shard_map/ppermute | solution.py:358
  91.6 15.0 %collective-permute-start.34 = (bf16[64,2048]{1,0:T(8,128)(2,1)S(1)}, bf16[64,2048]{1,0:T(8,128)(2,1)S(1)}, u32[]{:S(2)}, u32[]{:S(2)}) collective-permute-start(bf16[64,2048]{1,0:T(8,128)(2,1)S(1)} %get-tuple-element.70.refs_8_.refs_9_), channel_id=1, source_target_pairs={{0,4},{4,0},{8,12},{12,8},{1,5},{5,1},{9,13},{13,9},{2,6},{6,2},{1... | collective-permute-start | bytes 786440 | tf_op jit(solution)/shard_map/ppermute | solution.py:358
  91.6 14.9 %collective-permute-start.35 = (bf16[64,2048]{1,0:T(8,128)(2,1)S(1)}, bf16[64,2048]{1,0:T(8,128)(2,1)S(1)}, u32[]{:S(2)}, u32[]{:S(2)}) collective-permute-start(bf16[64,2048]{1,0:T(8,128)(2,1)S(1)} %get-tuple-element.75), channel_id=1, source_target_pairs={{0,4},{4,0},{8,12},{12,8},{1,5},{5,1},{9,13},{13,9},{2,6},{6,2},{1... | collective-permute-start | bytes 786440 | tf_op jit(solution)/shard_map/ppermute | solution.py:358
  100.4 6.4 %collective-permute-start.33 = (bf16[128,2048]{1,0:T(8,128)(2,1)S(1)}, bf16[128,2048]{1,0:T(8,128)(2,1)S(1)}, u32[]{:S(2)}, u32[]{:S(2)}) collective-permute-start(bf16[128,2048]{1,0:T(8,128)(2,1)S(1)} %get-tuple-element.73), channel_id=1, source_target_pairs={{0,4},{4,0},{8,12},{12,8},{1,5},{5,1},{9,13},{13,9},{2,6},{6,2},{1... | collective-permute-start | bytes 1572872 | tf_op jit(solution)/shard_map/ppermute | solution.py:358

commit v4 on v3

--- a/solution.py
+++ b/solution.py
@@ -379,7 +379,7 @@
         pairs = [(hidden[i], got[i + lag]) for i in some]
         return down([order[i] for i in some], active_ids, active_counts, pairs, down_weight, after=after, **more)
 
-    ups = {0: [(1, 2, 7)], 2: [(3,)], 3: [(4,)], 4: [(5,)], 5: [(6,)]}
+    ups = {0: [(1, 2)], 2: [(3,)], 3: [(4,)], 4: [(5,)], 5: [(6,)], 6: [(7,)]}
     downs = {7: [(3,)], 8: [(4,)], 9: [(5,)], 10: [(6,)], 11: [(7,), (0, 1, 2)]}
     for i in range(steps + lag + 1):
         back = i - lag
@@ -413,7 +413,7 @@
                 latest = out[0][0]
                 line = [latest]
                 continue
-            (out,) = do_down(some, [latest] + line, inits=terms[j] if flip == 2 else (), parts=2)
+            (out,) = do_down(some, [latest] + line, inits=terms[j] if flip == 2 else (), parts=1 if (flip, j) == (2, 0) else 2)
             latest = out[0]
             line = [latest]
             {1: near, 2: far, 3: terms}[flip][j] = swap(out, 2 if flip == 2 else 1)

time: 110 us -> 103 us (0.936)
  the two profiles are of different devices: /device:TPU:0 before, /device:TPU:7 now
where the time goes in v4:
time: 103 us
  Pallas kernels  49.4 us (48%)
  starting transfers between devices  41.9 us (41%)
  waiting for transfers between devices  7.67 us (7%)
  local copies, waits for them, and re-layouts  2.02 us (2%)
  other arithmetic  1.84 us (2%)
    pallas_call x6, Pallas kernels, down(): pl.pallas_call(functools.partial(down_kernel, whiches, len(inits), bias i...  23.1 us
    ppermute x11, starting transfers between devices, staged(): got[i] = lax.ppermute(sent, 'dp', [(0, 1), (1, 0), (2, 3), (3, 2)])  22.9 us
    pallas_call x6, Pallas kernels, up(): pl.pallas_call(functools.partial(up_kernel, [(w, len(r)) for w, r in zip(...  20 us
    ppermute x18, starting transfers between devices, swap(): lax.ppermute(part, 'tensor', [(t, t ^ flip) for t in range(4)])  13.7 us
    ppermute x8, starting transfers between devices, staged(): other[i - 1] = lax.ppermute(latest, 'dp', [(1, 2), (2, 1)])  5.41 us
    pallas_call x1, Pallas kernels, head(): pl.pallas_call(functools.partial(head_kernel, order), out_shape=[jax.Shap...  4.93 us
    ppermute x11, waiting for transfers between devices, staged(): got[i] = lax.ppermute(sent, 'dp', [(0, 1), (1, 0), (2, 3), (3, 2)])  4.06 us
    ppermute x18, waiting for transfers between devices, swap(): lax.ppermute(part, 'tensor', [(t, t ^ flip) for t in range(4)])  3.59 us
  transfers between devices with their start and end apart: 37, of which 7 were waited for; matrix products, arithmetic and copies ran while one was open for 0% of the time, Pallas kernels for 43%

profile of v4, /device:TPU:7, one launch (start us, length us, event | category | flops | bytes accessed | tf_op | source)
XLA Modules:
  0.0 103.4 jit_solution(5275569554673706442)
XLA Ops:
  0.0 4.9 %head.1 = (bf16[128,1024]{1,0:T(8,128)(2,1)}, bf16[128,2048]{1,0:T(8,128)(2,1)}, bf16[128,2048]{1,0:T(8,128)(2,1)}, f32[8,1024]{1,0:T(8,128)}) custom-call(s32[8,1,8]{2,1,0:T(1,128)} %ids.25, s32[1,8]{1,0:T(1,128)} %bitcast.3, bf16[256,2048]{1,0:T(8,128)(2,1)} %rows.1, bf16[2048,8192]{1,0:T(8,128)(2,1)} %weight.13, f32[64,128]{1,0:T(8,128)} %bitcast.17), custom_call_target="tpu_custom_call" | custom-call | flops 1 | bytes 1 | tf_op jit(solution)/shard_map/head/pallas_call | solution.py:94
  5.2 1.3 %collective-permute-start = (bf16[128,1024]{1,0:T(8,128)(2,1)}, bf16[128,1024]{1,0:T(8,128)(2,1)S(1)}, u32[]{:S(2)}, u32[]{:S(2)}) collective-permute-start(bf16[128,1024]{1,0:T(8,128)(2,1)} %get-tuple-element.38.refs_0_.refs_2_), channel_id=1, source_target_pairs={{0,1},{1,0},{2,3},{3,2},{4,5},{5,4},{6,7},{7,6},{8,9},{9,8},{10,11... | collective-permute-start | bytes 786440 | tf_op jit(solution)/shard_map/ppermute | solution.py:392
  6.5 0.6 collective-permute-done.3.refs_0_
  7.1 0.9 copy-done.1
  8.1 1.0 %copy-done.4 = bf16[128,2048]{1,0:T(8,128)(2,1)S(1)} copy-done((bf16[128,2048]{1,0:T(8,128)(2,1)S(1)}, bf16[128,2048]{1,0:T(8,128)(2,1)}, u32[]{:S(2)}) %copy-start.4) | copy-done | bytes 524312
  9.1 4.8 %up.6 = (bf16[128,1024]{1,0:T(8,128)(2,1)S(1)}, bf16[128,1024]{1,0:T(8,128)(2,1)S(1)}) custom-call(s32[8,1,8]{2,1,0:T(1,128)S(1)} %copy-done.3, s32[1,8]{1,0:T(1,128)S(1)} %bitcast.4, bf16[2048,8192]{1,0:T(8,128)(2,1)} %weight.13, bf16[128,2048]{1,0:T(8,128)(2,1)S(1)} %collective-permute-done.3.refs_0_, bf16[128,2048]{1,0:T(8,128)(2,1)S(1)} %copy-done.4, ...), custom_call_target="tpu_custom_call" | custom-call | flops 1 | bytes 1 | tf_op jit(solution)/shard_map/up/pallas_call | solution.py:158
  13.9 1.4 %collective-permute-start.5 = (bf16[128,1024]{1,0:T(8,128)(2,1)S(1)}, bf16[128,1024]{1,0:T(8,128)(2,1)S(1)}, u32[]{:S(2)}, u32[]{:S(2)}) collective-permute-start(bf16[128,1024]{1,0:T(8,128)(2,1)S(1)} %get-tuple-element.46.refs_0_), channel_id=1, source_target_pairs={{0,1},{1,0},{2,3},{3,2},{4,5},{5,4},{6,7},{7,6},{8,9},{9,8},{10,11... | collective-permute-start | bytes 786440 | tf_op jit(solution)/shard_map/ppermute | solution.py:392
  15.4 0.7 collective-permute-start.1
  16.1 0.5 collective-permute-start.12
  16.5 4.1 %collective-permute-start.10 = (bf16[128,1024]{1,0:T(8,128)(2,1)S(1)}, bf16[128,1024]{1,0:T(8,128)(2,1)S(1)}, u32[]{:S(2)}, u32[]{:S(2)}) collective-permute-start(bf16[128,1024]{1,0:T(8,128)(2,1)S(1)} %get-tuple-element.42.refs_1_.refs_0_), channel_id=1, source_target_pairs={{0,1},{1,0},{2,3},{3,2},{4,5},{5,4},{6,7},{7,6},{8,9},{9,8},{10,11... | collective-permute-start | bytes 786440 | tf_op jit(solution)/shard_map/ppermute | solution.py:392
  20.6 3.3 %up.7 = (bf16[128,1024]{1,0:T(8,128)(2,1)S(1)}, bf16[64,2048]{1,0:T(8,128)(2,1)S(1)}, bf16[64,2048]{1,0:T(8,128)(2,1)S(1)}) custom-call(s32[8,1,8]{2,1,0:T(1,128)S(1)} %copy-done.3, s32[1,8]{1,0:T(1,128)S(1)} %bitcast.5, bf16[2048,8192]{1,0:T(8,128)(2,1)} %weight.13, bf16[128,2048]{1,0:T(8,128)(2,1)S(1)} %collective-permute-done.2.refs_0_, ...), custom_call_target="tpu_custom_call" | custom-call | flops 1 | bytes 1 | tf_op jit(solution)/shard_map/up/pallas_call | solution.py:158
  24.1 0.5 collective-permute-start.8
  24.6 0.7 collective-permute-start.6
  25.4 1.9 %collective-permute-done.10.refs_1_ = bf16[128,1024]{1,0:T(8,128)(2,1)S(1)} collective-permute-done((bf16[128,1024]{1,0:T(8,128)(2,1)S(1)}, bf16[128,1024]{1,0:T(8,128)(2,1)S(1)}, u32[]{:S(2)}, u32[]{:S(2)}) %collective-permute-start.10) | collective-permute-done | bytes 262176 | tf_op jit(solution)/shard_map/ppermute | solution.py:392
  27.4 2.6 %collective-permute-start.4 = (bf16[128,1024]{1,0:T(8,128)(2,1)S(1)}, bf16[128,1024]{1,0:T(8,128)(2,1)S(1)}, u32[]{:S(2)}, u32[]{:S(2)}) collective-permute-start(bf16[128,1024]{1,0:T(8,128)(2,1)S(1)} %get-tuple-element.45), channel_id=1, source_target_pairs={{0,1},{1,0},{2,3},{3,2},{4,5},{5,4},{6,7},{7,6},{8,9},{9,8},{10,11... | collective-permute-start | bytes 786440 | tf_op jit(solution)/shard_map/ppermute | solution.py:392
  30.1 0.7 collective-permute-start.11
  30.8 3.3 %up.8.refs_3_.refs_1_.refs_0_ = bf16[128,1024]{1,0:T(8,128)(2,1)S(1)} custom-call(s32[8,1,8]{2,1,0:T(1,128)S(1)} %copy-done.3, s32[1,8]{1,0:T(1,128)S(1)} %bitcast.6, bf16[2048,8192]{1,0:T(8,128)(2,1)} %weight.13, bf16[64,2048]{1,0:T(8,128)(2,1)S(1)} %collective-permute-done.7.refs_0_, bf16[64,2048]{1,0:T(8,128)(2,1)S(1)} %collective-permute-done.8.refs_1_, ...), custom_call_target="tpu_custom_call" | custom-call | flops 1 | bytes 1 | tf_op jit(solution)/shard_map/up/pallas_call | solution.py:158
  34.2 2.5 %collective-permute-start.9 = (bf16[128,1024]{1,0:T(8,128)(2,1)S(1)}, bf16[128,1024]{1,0:T(8,128)(2,1)S(1)}, u32[]{:S(2)}, u32[]{:S(2)}) collective-permute-start(bf16[128,1024]{1,0:T(8,128)(2,1)S(1)} %get-tuple-element.50), channel_id=1, source_target_pairs={{0,1},{1,0},{2,3},{3,2},{4,5},{5,4},{6,7},{7,6},{8,9},{9,8},{10,11... | collective-permute-start | bytes 786440 | tf_op jit(solution)/shard_map/ppermute | solution.py:392
  36.8 1.0 collective-permute-start.14
  37.7 2.6 %up.9 = (bf16[128,1024]{1,0:T(8,128)(2,1)S(1)}, bf16[64,2048]{1,0:T(8,128)(2,1)S(1)}, bf16[64,2048]{1,0:T(8,128)(2,1)S(1)}) custom-call(s32[8,1,8]{2,1,0:T(1,128)S(1)} %copy-done.3, s32[1,8]{1,0:T(1,128)S(1)} %bitcast.7, bf16[2048,8192]{1,0:T(8,128)(2,1)} %weight.13, bf16[128,2048]{1,0:T(8,128)(2,1)S(1)} %collective-permute-done.12.refs_0_, ...), custom_call_target="tpu_custom_call" | custom-call | flops 1 | bytes 1 | tf_op jit(solution)/shard_map/up/pallas_call | solution.py:158
  40.4 0.7 collective-permute-start.15
  41.3 0.7 collective-permute-start.21
  42.1 0.7 collective-permute-done.9.refs_1_.refs_3_
  42.8 2.5 %collective-permute-start.13 = (bf16[128,1024]{1,0:T(8,128)(2,1)S(1)}, bf16[128,1024]{1,0:T(8,128)(2,1)S(1)}, u32[]{:S(2)}, u32[]{:S(2)}) collective-permute-start(bf16[128,1024]{1,0:T(8,128)(2,1)S(1)} %get-tuple-element.53), channel_id=1, source_target_pairs={{0,1},{1,0},{2,3},{3,2},{4,5},{5,4},{6,7},{7,6},{8,9},{9,8},{10,11... | collective-permute-start | bytes 786440 | tf_op jit(solution)/shard_map/ppermute | solution.py:392
  45.4 0.7 collective-permute-start.17
  46.1 3.3 %up.10.refs_1_.refs_3_.refs_0_ = bf16[128,1024]{1,0:T(8,128)(2,1)S(1)} custom-call(s32[8,1,8]{2,1,0:T(1,128)S(1)} %copy-done.3, s32[1,8]{1,0:T(1,128)S(1)} %bitcast.8, bf16[2048,8192]{1,0:T(8,128)(2,1)} %weight.13, bf16[64,2048]{1,0:T(8,128)(2,1)S(1)} %collective-permute-done.15.refs_0_, bf16[64,2048]{1,0:T(8,128)(2,1)S(1)} %collective-permute-done.16.refs_1_, ...), custom_call_target="tpu_custom_call" | custom-call | flops 1 | bytes 1 | tf_op jit(solution)/shard_map/up/pallas_call | solution.py:158
  49.6 1.6 %collective-permute-start.22 = (bf16[128,1024]{1,0:T(8,128)(2,1)S(1)}, bf16[128,1024]{1,0:T(8,128)(2,1)S(1)}, u32[]{:S(2)}, u32[]{:S(2)}) collective-permute-start(bf16[128,1024]{1,0:T(8,128)(2,1)S(1)} %get-tuple-element.57), channel_id=1, source_target_pairs={{0,1},{1,0},{2,3},{3,2},{4,5},{5,4},{6,7},{7,6},{8,9},{9,8},{10,11... | collective-permute-start | bytes 786440 | tf_op jit(solution)/shard_map/ppermute | solution.py:392
  51.3 0.7 collective-permute-start.25
  52.0 2.6 %up.11.refs_3_.refs_0_ = bf16[128,1024]{1,0:T(8,128)(2,1)S(1)} custom-call(s32[8,1,8]{2,1,0:T(1,128)S(1)} %copy-done.3, s32[1,8]{1,0:T(1,128)S(1)} %bitcast.9, bf16[2048,8192]{1,0:T(8,128)(2,1)} %weight.13, bf16[128,2048]{1,0:T(8,128)(2,1)S(1)} %collective-permute-done.14.refs_0_, bf16[128,1024]{1,0:T(8,128)(2,1)S(1)} %up.10.refs_1_.refs_3_.refs_0_), custom_call_target="tpu_custom_call" | custom-call | flops 1 | bytes 1 | tf_op jit(solution)/shard_map/up/pallas_call | solution.py:158
  54.8 2.5 %collective-permute-start.18 = (bf16[128,1024]{1,0:T(8,128)(2,1)S(1)}, bf16[128,1024]{1,0:T(8,128)(2,1)S(1)}, u32[]{:S(2)}, u32[]{:S(2)}) collective-permute-start(bf16[128,1024]{1,0:T(8,128)(2,1)S(1)} %get-tuple-element.56), channel_id=1, source_target_pairs={{0,1},{1,0},{2,3},{3,2},{4,5},{5,4},{6,7},{7,6},{8,9},{9,8},{10,11... | collective-permute-start | bytes 786440 | tf_op jit(solution)/shard_map/ppermute | solution.py:392
  57.3 3.4 %down.6 = (bf16[64,2048]{1,0:T(8,128)(2,1)S(1)}, bf16[64,2048]{1,0:T(8,128)(2,1)S(1)}) custom-call(s32[8,1,8]{2,1,0:T(1,128)S(1)} %copy-done.3, s32[1,8]{1,0:T(1,128)S(1)} %bitcast.10, bf16[128,1024]{1,0:T(8,128)(2,1)S(1)} %get-tuple-element.59.refs_0_, bf16[128,1024]{1,0:T(8,128)(2,1)S(1)} %collective-permute-done.22.refs_1_, bf16[8192,2048]{1,0:T(8,128)(2,1)} %refs_6_.1, ...), custom_call_target="tpu_custom_call" | custom-call | flops 1 | bytes 1 | tf_op jit(solution)/shard_map/down/pallas_call | solution.py:265
  60.8 4.0 %collective-permute-start.27 = (bf16[64,2048]{1,0:T(8,128)(2,1)S(1)}, bf16[64,2048]{1,0:T(8,128)(2,1)S(1)}, u32[]{:S(2)}, u32[]{:S(2)}) collective-permute-start(bf16[64,2048]{1,0:T(8,128)(2,1)S(1)} %get-tuple-element.60.refs_6_), channel_id=1, source_target_pairs={{0,4},{4,0},{8,12},{12,8},{1,5},{5,1},{9,13},{13,9},{2,6},{6,2},{1... | collective-permute-start | bytes 786440 | tf_op jit(solution)/shard_map/ppermute | solution.py:358
  64.8 0.7 collective-permute-start.23
  65.6 2.2 %collective-permute-start.26 = (bf16[128,1024]{1,0:T(8,128)(2,1)S(1)}, bf16[128,1024]{1,0:T(8,128)(2,1)S(1)}, u32[]{:S(2)}, u32[]{:S(2)}) collective-permute-start(bf16[128,1024]{1,0:T(8,128)(2,1)S(1)} %mix.15.refs_0_), channel_id=1, source_target_pairs={{0,1},{1,0},{2,3},{3,2},{4,5},{5,4},{6,7},{7,6},{8,9},{9,8},{10,11... | collective-permute-start | bytes 786440 | tf_op jit(solution)/shard_map/ppermute | solution.py:392
  67.8 0.7 collective-permute-start.19
  68.5 3.3 %down.7.refs_4_ = bf16[128,2048]{1,0:T(8,128)(2,1)S(1)} custom-call(s32[8,1,8]{2,1,0:T(1,128)S(1)} %copy-done.3, s32[1,8]{1,0:T(1,128)S(1)} %bitcast.11, bf16[128,1024]{1,0:T(8,128)(2,1)S(1)} %get-tuple-element.58.refs_0_, bf16[128,1024]{1,0:T(8,128)(2,1)S(1)} %collective-permute-done.18.refs_1_, bf16[8192,2048]{1,0:T(8,128)(2,1)} %refs_6_.1, ...), custom_call_target="tpu_custom_call" | custom-call | flops 1 | bytes 1 | tf_op jit(solution)/shard_map/down/pallas_call | solution.py:265
  72.0 2.1 %collective-permute-start.24 = (bf16[128,1024]{1,0:T(8,128)(2,1)S(1)}, bf16[128,1024]{1,0:T(8,128)(2,1)S(1)}, u32[]{:S(2)}, u32[]{:S(2)}) collective-permute-start(bf16[128,1024]{1,0:T(8,128)(2,1)S(1)} %mix.14.refs_3_.refs_0_), channel_id=1, source_target_pairs={{0,1},{1,0},{2,3},{3,2},{4,5},{5,4},{6,7},{7,6},{8,9},{9,8},{10,11... | collective-permute-start | bytes 786440 | tf_op jit(solution)/shard_map/ppermute | solution.py:392
  74.1 2.6 %down.8 = (bf16[64,2048]{1,0:T(8,128)(2,1)S(1)}, bf16[64,2048]{1,0:T(8,128)(2,1)S(1)}) custom-call(s32[8,1,8]{2,1,0:T(1,128)S(1)} %copy-done.3, s32[1,8]{1,0:T(1,128)S(1)} %bitcast.12, bf16[128,1024]{1,0:T(8,128)(2,1)S(1)} %mix.15.refs_0_, bf16[128,1024]{1,0:T(8,128)(2,1)S(1)} %collective-permute-done.26.refs_1_, bf16[8192,2048]{1,0:T(8,128)(2,1)} %refs_6_.1, ...), custom_call_target="tpu_custom_call" | custom-call | flops 1 | bytes 1 | tf_op jit(solution)/shard_map/down/pallas_call | solution.py:265
  76.7 3.1 %collective-permute-start.29 = (bf16[64,2048]{1,0:T(8,128)(2,1)S(1)}, bf16[64,2048]{1,0:T(8,128)(2,1)S(1)}, u32[]{:S(2)}, u32[]{:S(2)}) collective-permute-start(bf16[64,2048]{1,0:T(8,128)(2,1)S(1)} %get-tuple-element.62.refs_6_), channel_id=1, source_target_pairs={{0,4},{4,0},{8,12},{12,8},{1,5},{5,1},{9,13},{13,9},{2,6},{6,2},{1... | collective-permute-start | bytes 786440 | tf_op jit(solution)/shard_map/ppermute | solution.py:358
  80.1 0.9 collective-permute-done.29.refs_3_
  81.4 3.3 %down.9 = (bf16[64,2048]{1,0:T(8,128)(2,1)S(1)}, bf16[64,2048]{1,0:T(8,128)(2,1)S(1)}) custom-call(s32[8,1,8]{2,1,0:T(1,128)S(1)} %copy-done.3, s32[1,8]{1,0:T(1,128)S(1)} %bitcast.13, bf16[128,1024]{1,0:T(8,128)(2,1)S(1)} %mix.14.refs_3_.refs_0_, bf16[128,1024]{1,0:T(8,128)(2,1)S(1)} %collective-permute-done.24.refs_1_, bf16[8192,2048]{1,0:T(8,128)(2,1)} %refs_6_.1, ...), custom_call_target="tpu_custom_call" | custom-call | flops 1 | bytes 1 | tf_op jit(solution)/shard_map/down/pallas_call | solution.py:265
  84.7 1.4 %collective-permute-start.36 = (bf16[64,2048]{1,0:T(8,128)(2,1)S(1)}, bf16[64,2048]{1,0:T(8,128)(2,1)S(1)}, u32[]{:S(2)}, u32[]{:S(2)}) collective-permute-start(bf16[64,2048]{1,0:T(8,128)(2,1)S(1)} %get-tuple-element.70), channel_id=1, source_target_pairs={{0,8},{4,12},{8,0},{12,4},{1,9},{5,13},{9,1},{13,5},{2,10},{6,14},... | collective-permute-start | bytes 786440 | tf_op jit(solution)/shard_map/ppermute | solution.py:358
  86.2 1.4 %collective-permute-done.20.refs_1_ = bf16[128,1024]{1,0:T(8,128)(2,1)S(1)} collective-permute-done((bf16[128,1024]{1,0:T(8,128)(2,1)S(1)}, bf16[128,1024]{1,0:T(8,128)(2,1)S(1)}, u32[]{:S(2)}, u32[]{:S(2)}) %collective-permute-start.20) | collective-permute-done | bytes 262176 | tf_op jit(solution)/shard_map/ppermute | solution.py:392
  87.5 2.6 %down.10 = (bf16[64,2048]{1,0:T(8,128)(2,1)S(1)}, bf16[64,2048]{1,0:T(8,128)(2,1)S(1)}) custom-call(s32[8,1,8]{2,1,0:T(1,128)S(1)} %copy-done.3, s32[1,8]{1,0:T(1,128)S(1)} %bitcast.14, bf16[128,1024]{1,0:T(8,128)(2,1)S(1)} %mix.12.refs_5_.refs_0_, bf16[128,1024]{1,0:T(8,128)(2,1)S(1)} %collective-permute-done.20.refs_1_, bf16[8192,2048]{1,0:T(8,128)(2,1)} %refs_6_.1, ...), custom_call_target="tpu_custom_call" | custom-call | flops 1 | bytes 1 | tf_op jit(solution)/shard_map/down/pallas_call | solution.py:265
  90.2 1.7 %collective-permute-start.33 = (bf16[64,2048]{1,0:T(8,128)(2,1)S(1)}, bf16[64,2048]{1,0:T(8,128)(2,1)S(1)}, u32[]{:S(2)}, u32[]{:S(2)}) collective-permute-start(bf16[64,2048]{1,0:T(8,128)(2,1)S(1)} %get-tuple-element.65.refs_8_.refs_9_), channel_id=1, source_target_pairs={{0,4},{4,0},{8,12},{12,8},{1,5},{5,1},{9,13},{13,9},{2,6},{6,2},{1... | collective-permute-start | bytes 786440 | tf_op jit(solution)/shard_map/ppermute | solution.py:358
  91.9 7.9 %down.11 = (f32[128,2048]{1,0:T(8,128)S(1)}, bf16[128,2048]{1,0:T(8,128)(2,1)S(1)}, f32[128,2048]{1,0:T(8,128)S(1)}) custom-call(s32[8,1,8]{2,1,0:T(1,128)S(1)} %copy-done.3, s32[1,8]{1,0:T(1,128)S(1)} %bitcast.15, bf16[128,1024]{1,0:T(8,128)(2,1)S(1)} %get-tuple-element.44.refs_0_, bf16[128,1024]{1,0:T(8,128)(2,1)S(1)} %collective-permute-done.4.refs_1_, ...), custom_call_target="tpu_custom_call" | custom-call | flops 1 | bytes 1 | tf_op jit(solution)/shard_map/down/pallas_call | solution.py:265
  100.1 1.7 %collective-permute-done.32 = bf16[128,2048]{1,0:T(8,128)(2,1)S(1)} collective-permute-done((bf16[128,2048]{1,0:T(8,128)(2,1)S(1)}, bf16[128,2048]{1,0:T(8,128)(2,1)S(1)}, u32[]{:S(2)}, u32[]{:S(2)}) %collective-permute-start.32) | collective-permute-done | bytes 524320 | tf_op jit(solution)/shard_map/ppermute | solution.py:358
  102.0 1.5 %pad_maximum_fusion = f32[256,2048]{1,0:T(8,128)} fusion(f32[128,2048]{1,0:T(8,128)S(1)} %convert_add_fusion, f32[128,2048]{1,0:T(8,128)S(1)} %convert_add_fusion.1), kind=kLoop, calls=%fused_computation | loop fusion | flops 524288 | bytes 4194304 | tf_op jit(solution)/shard_map/concatenate | solution.py:425
  (74 shorter events, 3.2 us)
Async XLA Ops:
  0.0 7.1 %copy-start.3 = (s32[8,1,8]{2,1,0:T(1,128)S(1)}, s32[8,1,8]{2,1,0:T(1,128)}, u32[]{:S(2)}) copy-start(s32[8,1,8]{2,1,0:T(1,128)} %ids.25) | copy-start | bytes 772
  0.0 7.1 %copy-start.6 = (s32[8,1]{0,1:T(1,128)S(1)}, s32[8,1]{0,1:T(1,128)}, u32[]{:S(2)}) copy-start(s32[8,1]{0,1:T(1,128)} %param.13) | copy-start | bytes 100
  4.9 2.2 %collective-permute-start.3 = (bf16[128,2048]{1,0:T(8,128)(2,1)}, bf16[128,2048]{1,0:T(8,128)(2,1)S(1)}, u32[]{:S(2)}, u32[]{:S(2)}) collective-permute-start(bf16[128,2048]{1,0:T(8,128)(2,1)} %get-tuple-element.40), channel_id=1, source_target_pairs={{0,4},{4,0},{8,12},{12,8},{1,5},{5,1},{9,13},{13,9},{2,6},{6,2},{1... | collective-permute-start | bytes 1572872 | tf_op jit(solution)/shard_map/ppermute | solution.py:358
  5.0 15.6 %collective-permute-start.2 = (bf16[128,2048]{1,0:T(8,128)(2,1)}, bf16[128,2048]{1,0:T(8,128)(2,1)S(1)}, u32[]{:S(2)}, u32[]{:S(2)}) collective-permute-start(bf16[128,2048]{1,0:T(8,128)(2,1)} %get-tuple-element.40), channel_id=1, source_target_pairs={{0,12},{4,8},{8,4},{12,0},{1,13},{5,9},{9,5},{13,1},{2,14},{6,10},... | collective-permute-start | bytes 1572872 | tf_op jit(solution)/shard_map/ppermute | solution.py:358
  5.2 10.1 %collective-permute-start = (bf16[128,1024]{1,0:T(8,128)(2,1)}, bf16[128,1024]{1,0:T(8,128)(2,1)S(1)}, u32[]{:S(2)}, u32[]{:S(2)}) collective-permute-start(bf16[128,1024]{1,0:T(8,128)(2,1)} %get-tuple-element.38.refs_0_.refs_2_), channel_id=1, source_target_pairs={{0,1},{1,0},{2,3},{3,2},{4,5},{5,4},{6,7},{7,6},{8,9},{9,8},{10,11... | collective-permute-start | bytes 786440 | tf_op jit(solution)/shard_map/ppermute | solution.py:392
  7.1 1.0 copy-start.1
  8.1 1.0 %copy-start.4 = (bf16[128,2048]{1,0:T(8,128)(2,1)S(1)}, bf16[128,2048]{1,0:T(8,128)(2,1)}, u32[]{:S(2)}) copy-start(bf16[128,2048]{1,0:T(8,128)(2,1)} %get-tuple-element.41.refs_1_) | copy-start | bytes 1572868
  9.1 6.2 %copy-start.2 = (bf16[128,1024]{1,0:T(8,128)(2,1)S(1)}, bf16[128,1024]{1,0:T(8,128)(2,1)}, u32[]{:S(2)}) copy-start(bf16[128,1024]{1,0:T(8,128)(2,1)} %get-tuple-element.38.refs_0_.refs_2_) | copy-start | bytes 786436
  9.1 6.9 %copy-start.5 = (bf16[128,2048]{1,0:T(8,128)(2,1)S(1)}, bf16[128,2048]{1,0:T(8,128)(2,1)}, u32[]{:S(2)}) copy-start(bf16[128,2048]{1,0:T(8,128)(2,1)} %get-tuple-element.41.refs_1_) | copy-start | bytes 1572868
  13.9 10.1 %collective-permute-start.5 = (bf16[128,1024]{1,0:T(8,128)(2,1)S(1)}, bf16[128,1024]{1,0:T(8,128)(2,1)S(1)}, u32[]{:S(2)}, u32[]{:S(2)}) collective-permute-start(bf16[128,1024]{1,0:T(8,128)(2,1)S(1)} %get-tuple-element.46.refs_0_), channel_id=1, source_target_pairs={{0,1},{1,0},{2,3},{3,2},{4,5},{5,4},{6,7},{7,6},{8,9},{9,8},{10,11... | collective-permute-start | bytes 786440 | tf_op jit(solution)/shard_map/ppermute | solution.py:392
  15.4 9.2 %collective-permute-start.1 = (bf16[128,1024]{1,0:T(8,128)(2,1)S(1)}, bf16[128,1024]{1,0:T(8,128)(2,1)S(1)}, u32[]{:S(2)}, u32[]{:S(2)}) collective-permute-start(bf16[128,1024]{1,0:T(8,128)(2,1)S(1)} %fold.8.refs_0_), channel_id=1, source_target_pairs={{1,2},{2,1},{5,6},{6,5},{9,10},{10,9},{13,14},{14,13},{17,18},{18,... | collective-permute-start | bytes 786440 | tf_op jit(solution)/shard_map/ppermute | solution.py:401
  16.1 21.7 %collective-permute-start.12 = (bf16[128,2048]{1,0:T(8,128)(2,1)S(1)}, bf16[128,2048]{1,0:T(8,128)(2,1)S(1)}, u32[]{:S(2)}, u32[]{:S(2)}) collective-permute-start(bf16[128,2048]{1,0:T(8,128)(2,1)S(1)} %copy-done.5), channel_id=1, source_target_pairs={{0,12},{4,8},{8,4},{12,0},{1,13},{5,9},{9,5},{13,1},{2,14},{6,10},... | collective-permute-start | bytes 1572872 | tf_op jit(solution)/shard_map/ppermute | solution.py:358
  16.5 8.8 %copy-start = (f32[8,1024]{1,0:T(8,128)S(1)}, f32[8,1024]{1,0:T(8,128)}, u32[]{:S(2)}) copy-start(f32[8,1024]{1,0:T(8,128)} %get-tuple-element.39.refs_2_) | copy-start | bytes 98308
  16.5 10.9 %collective-permute-start.10 = (bf16[128,1024]{1,0:T(8,128)(2,1)S(1)}, bf16[128,1024]{1,0:T(8,128)(2,1)S(1)}, u32[]{:S(2)}, u32[]{:S(2)}) collective-permute-start(bf16[128,1024]{1,0:T(8,128)(2,1)S(1)} %get-tuple-element.42.refs_1_.refs_0_), channel_id=1, source_target_pairs={{0,1},{1,0},{2,3},{3,2},{4,5},{5,4},{6,7},{7,6},{8,9},{9,8},{10,11... | collective-permute-start | bytes 786440 | tf_op jit(solution)/shard_map/ppermute | solution.py:392
  24.0 6.1 %collective-permute-start.7 = (bf16[64,2048]{1,0:T(8,128)(2,1)S(1)}, bf16[64,2048]{1,0:T(8,128)(2,1)S(1)}, u32[]{:S(2)}, u32[]{:S(2)}) collective-permute-start(bf16[64,2048]{1,0:T(8,128)(2,1)S(1)} %get-tuple-element.47), channel_id=1, source_target_pairs={{0,4},{4,0},{8,12},{12,8},{1,5},{5,1},{9,13},{13,9},{2,6},{6,2},{1... | collective-permute-start | bytes 786440 | tf_op jit(solution)/shard_map/ppermute | solution.py:358
  24.1 6.7 %collective-permute-start.8 = (bf16[64,2048]{1,0:T(8,128)(2,1)S(1)}, bf16[64,2048]{1,0:T(8,128)(2,1)S(1)}, u32[]{:S(2)}, u32[]{:S(2)}) collective-permute-start(bf16[64,2048]{1,0:T(8,128)(2,1)S(1)} %get-tuple-element.48), channel_id=1, source_target_pairs={{0,4},{4,0},{8,12},{12,8},{1,5},{5,1},{9,13},{13,9},{2,6},{6,2},{1... | collective-permute-start | bytes 786440 | tf_op jit(solution)/shard_map/ppermute | solution.py:358
  24.6 9.5 %collective-permute-start.6 = (bf16[128,1024]{1,0:T(8,128)(2,1)S(1)}, bf16[128,1024]{1,0:T(8,128)(2,1)S(1)}, u32[]{:S(2)}, u32[]{:S(2)}) collective-permute-start(bf16[128,1024]{1,0:T(8,128)(2,1)S(1)} %fold.9.refs_0_), channel_id=1, source_target_pairs={{1,2},{2,1},{5,6},{6,5},{9,10},{10,9},{13,14},{14,13},{17,18},{18,... | collective-permute-start | bytes 786440 | tf_op jit(solution)/shard_map/ppermute | solution.py:401
  27.4 13.7 %collective-permute-start.4 = (bf16[128,1024]{1,0:T(8,128)(2,1)S(1)}, bf16[128,1024]{1,0:T(8,128)(2,1)S(1)}, u32[]{:S(2)}, u32[]{:S(2)}) collective-permute-start(bf16[128,1024]{1,0:T(8,128)(2,1)S(1)} %get-tuple-element.45), channel_id=1, source_target_pairs={{0,1},{1,0},{2,3},{3,2},{4,5},{5,4},{6,7},{7,6},{8,9},{9,8},{10,11... | collective-permute-start | bytes 786440 | tf_op jit(solution)/shard_map/ppermute | solution.py:392
  30.1 11.2 %collective-permute-start.11 = (bf16[128,1024]{1,0:T(8,128)(2,1)S(1)}, bf16[128,1024]{1,0:T(8,128)(2,1)S(1)}, u32[]{:S(2)}, u32[]{:S(2)}) collective-permute-start(bf16[128,1024]{1,0:T(8,128)(2,1)S(1)} %fold.10.refs_0_), channel_id=1, source_target_pairs={{1,2},{2,1},{5,6},{6,5},{9,10},{10,9},{13,14},{14,13},{17,18},{18,... | collective-permute-start | bytes 786440 | tf_op jit(solution)/shard_map/ppermute | solution.py:401
  34.2 8.6 %collective-permute-start.9 = (bf16[128,1024]{1,0:T(8,128)(2,1)S(1)}, bf16[128,1024]{1,0:T(8,128)(2,1)S(1)}, u32[]{:S(2)}, u32[]{:S(2)}) collective-permute-start(bf16[128,1024]{1,0:T(8,128)(2,1)S(1)} %get-tuple-element.50), channel_id=1, source_target_pairs={{0,1},{1,0},{2,3},{3,2},{4,5},{5,4},{6,7},{7,6},{8,9},{9,8},{10,11... | collective-permute-start | bytes 786440 | tf_op jit(solution)/shard_map/ppermute | solution.py:392
  36.8 15.2 %collective-permute-start.14 = (bf16[128,2048]{1,0:T(8,128)(2,1)S(1)}, bf16[128,2048]{1,0:T(8,128)(2,1)S(1)}, u32[]{:S(2)}, u32[]{:S(2)}) collective-permute-start(bf16[128,2048]{1,0:T(8,128)(2,1)S(1)} %copy-done.5), channel_id=1, source_target_pairs={{0,4},{4,0},{8,12},{12,8},{1,5},{5,1},{9,13},{13,9},{2,6},{6,2},{1... | collective-permute-start | bytes 1572872 | tf_op jit(solution)/shard_map/ppermute | solution.py:358
  40.4 5.1 %collective-permute-start.15 = (bf16[64,2048]{1,0:T(8,128)(2,1)S(1)}, bf16[64,2048]{1,0:T(8,128)(2,1)S(1)}, u32[]{:S(2)}, u32[]{:S(2)}) collective-permute-start(bf16[64,2048]{1,0:T(8,128)(2,1)S(1)} %get-tuple-element.54), channel_id=1, source_target_pairs={{0,4},{4,0},{8,12},{12,8},{1,5},{5,1},{9,13},{13,9},{2,6},{6,2},{1... | collective-permute-start | bytes 786440 | tf_op jit(solution)/shard_map/ppermute | solution.py:358
  41.1 5.0 %collective-permute-start.16 = (bf16[64,2048]{1,0:T(8,128)(2,1)S(1)}, bf16[64,2048]{1,0:T(8,128)(2,1)S(1)}, u32[]{:S(2)}, u32[]{:S(2)}) collective-permute-start(bf16[64,2048]{1,0:T(8,128)(2,1)S(1)} %get-tuple-element.55), channel_id=1, source_target_pairs={{0,4},{4,0},{8,12},{12,8},{1,5},{5,1},{9,13},{13,9},{2,6},{6,2},{1... | collective-permute-start | bytes 786440 | tf_op jit(solution)/shard_map/ppermute | solution.py:358
  41.3 8.2 %collective-permute-start.21 = (bf16[128,1024]{1,0:T(8,128)(2,1)S(1)}, bf16[128,1024]{1,0:T(8,128)(2,1)S(1)}, u32[]{:S(2)}, u32[]{:S(2)}) collective-permute-start(bf16[128,1024]{1,0:T(8,128)(2,1)S(1)} %fold.13.refs_0_), channel_id=1, source_target_pairs={{1,2},{2,1},{5,6},{6,5},{9,10},{10,9},{13,14},{14,13},{17,18},{18,... | collective-permute-start | bytes 786440 | tf_op jit(solution)/shard_map/ppermute | solution.py:401
  42.8 8.4 %collective-permute-start.13 = (bf16[128,1024]{1,0:T(8,128)(2,1)S(1)}, bf16[128,1024]{1,0:T(8,128)(2,1)S(1)}, u32[]{:S(2)}, u32[]{:S(2)}) collective-permute-start(bf16[128,1024]{1,0:T(8,128)(2,1)S(1)} %get-tuple-element.53), channel_id=1, source_target_pairs={{0,1},{1,0},{2,3},{3,2},{4,5},{5,4},{6,7},{7,6},{8,9},{9,8},{10,11... | collective-permute-start | bytes 786440 | tf_op jit(solution)/shard_map/ppermute | solution.py:392
  45.4 9.2 %collective-permute-start.17 = (bf16[128,1024]{1,0:T(8,128)(2,1)S(1)}, bf16[128,1024]{1,0:T(8,128)(2,1)S(1)}, u32[]{:S(2)}, u32[]{:S(2)}) collective-permute-start(bf16[128,1024]{1,0:T(8,128)(2,1)S(1)} %fold.11.refs_0_), channel_id=1, source_target_pairs={{1,2},{2,1},{5,6},{6,5},{9,10},{10,9},{13,14},{14,13},{17,18},{18,... | collective-permute-start | bytes 786440 | tf_op jit(solution)/shard_map/ppermute | solution.py:401
  49.6 7.6 %collective-permute-start.22 = (bf16[128,1024]{1,0:T(8,128)(2,1)S(1)}, bf16[128,1024]{1,0:T(8,128)(2,1)S(1)}, u32[]{:S(2)}, u32[]{:S(2)}) collective-permute-start(bf16[128,1024]{1,0:T(8,128)(2,1)S(1)} %get-tuple-element.57), channel_id=1, source_target_pairs={{0,1},{1,0},{2,3},{3,2},{4,5},{5,4},{6,7},{7,6},{8,9},{9,8},{10,11... | collective-permute-start | bytes 786440 | tf_op jit(solution)/shard_map/ppermute | solution.py:392
  51.3 14.2 %collective-permute-start.25 = (bf16[128,1024]{1,0:T(8,128)(2,1)S(1)}, bf16[128,1024]{1,0:T(8,128)(2,1)S(1)}, u32[]{:S(2)}, u32[]{:S(2)}) collective-permute-start(bf16[128,1024]{1,0:T(8,128)(2,1)S(1)} %fold.15.refs_0_), channel_id=1, source_target_pairs={{1,2},{2,1},{5,6},{6,5},{9,10},{10,9},{13,14},{14,13},{17,18},{18,... | collective-permute-start | bytes 786440 | tf_op jit(solution)/shard_map/ppermute | solution.py:401
  54.8 13.0 %collective-permute-start.18 = (bf16[128,1024]{1,0:T(8,128)(2,1)S(1)}, bf16[128,1024]{1,0:T(8,128)(2,1)S(1)}, u32[]{:S(2)}, u32[]{:S(2)}) collective-permute-start(bf16[128,1024]{1,0:T(8,128)(2,1)S(1)} %get-tuple-element.56), channel_id=1, source_target_pairs={{0,1},{1,0},{2,3},{3,2},{4,5},{5,4},{6,7},{7,6},{8,9},{9,8},{10,11... | collective-permute-start | bytes 786440 | tf_op jit(solution)/shard_map/ppermute | solution.py:392
  60.8 7.7 %collective-permute-start.27 = (bf16[64,2048]{1,0:T(8,128)(2,1)S(1)}, bf16[64,2048]{1,0:T(8,128)(2,1)S(1)}, u32[]{:S(2)}, u32[]{:S(2)}) collective-permute-start(bf16[64,2048]{1,0:T(8,128)(2,1)S(1)} %get-tuple-element.60.refs_6_), channel_id=1, source_target_pairs={{0,4},{4,0},{8,12},{12,8},{1,5},{5,1},{9,13},{13,9},{2,6},{6,2},{1... | collective-permute-start | bytes 786440 | tf_op jit(solution)/shard_map/ppermute | solution.py:358
  64.7 3.8 %collective-permute-start.28 = (bf16[64,2048]{1,0:T(8,128)(2,1)S(1)}, bf16[64,2048]{1,0:T(8,128)(2,1)S(1)}, u32[]{:S(2)}, u32[]{:S(2)}) collective-permute-start(bf16[64,2048]{1,0:T(8,128)(2,1)S(1)} %get-tuple-element.61), channel_id=1, source_target_pairs={{0,4},{4,0},{8,12},{12,8},{1,5},{5,1},{9,13},{13,9},{2,6},{6,2},{1... | collective-permute-start | bytes 786440 | tf_op jit(solution)/shard_map/ppermute | solution.py:358
  64.8 7.1 %collective-permute-start.23 = (bf16[128,1024]{1,0:T(8,128)(2,1)S(1)}, bf16[128,1024]{1,0:T(8,128)(2,1)S(1)}, u32[]{:S(2)}, u32[]{:S(2)}) collective-permute-start(bf16[128,1024]{1,0:T(8,128)(2,1)S(1)} %fold.14.refs_0_.refs_3_), channel_id=1, source_target_pairs={{1,2},{2,1},{5,6},{6,5},{9,10},{10,9},{13,14},{14,13},{17,18},{18,... | collective-permute-start | bytes 786440 | tf_op jit(solution)/shard_map/ppermute | solution.py:401
  65.6 8.5 %collective-permute-start.26 = (bf16[128,1024]{1,0:T(8,128)(2,1)S(1)}, bf16[128,1024]{1,0:T(8,128)(2,1)S(1)}, u32[]{:S(2)}, u32[]{:S(2)}) collective-permute-start(bf16[128,1024]{1,0:T(8,128)(2,1)S(1)} %mix.15.refs_0_), channel_id=1, source_target_pairs={{0,1},{1,0},{2,3},{3,2},{4,5},{5,4},{6,7},{7,6},{8,9},{9,8},{10,11... | collective-permute-start | bytes 786440 | tf_op jit(solution)/shard_map/ppermute | solution.py:392
  67.8 12.1 %collective-permute-start.19 = (bf16[128,1024]{1,0:T(8,128)(2,1)S(1)}, bf16[128,1024]{1,0:T(8,128)(2,1)S(1)}, u32[]{:S(2)}, u32[]{:S(2)}) collective-permute-start(bf16[128,1024]{1,0:T(8,128)(2,1)S(1)} %fold.12.refs_0_.refs_5_), channel_id=1, source_target_pairs={{1,2},{2,1},{5,6},{6,5},{9,10},{10,9},{13,14},{14,13},{17,18},{18,... | collective-permute-start | bytes 786440 | tf_op jit(solution)/shard_map/ppermute | solution.py:401
  71.8 20.1 %collective-permute-start.31 = (bf16[128,2048]{1,0:T(8,128)(2,1)S(1)}, bf16[128,2048]{1,0:T(8,128)(2,1)S(1)}, u32[]{:S(2)}, u32[]{:S(2)}) collective-permute-start(bf16[128,2048]{1,0:T(8,128)(2,1)S(1)} %down.7.refs_4_), channel_id=1, source_target_pairs={{0,8},{4,12},{8,0},{12,4},{1,9},{5,13},{9,1},{13,5},{2,10},{6,14},... | collective-permute-start | bytes 1572872 | tf_op jit(solution)/shard_map/ppermute | solution.py:358
  72.0 8.1 %collective-permute-start.24 = (bf16[128,1024]{1,0:T(8,128)(2,1)S(1)}, bf16[128,1024]{1,0:T(8,128)(2,1)S(1)}, u32[]{:S(2)}, u32[]{:S(2)}) collective-permute-start(bf16[128,1024]{1,0:T(8,128)(2,1)S(1)} %mix.14.refs_3_.refs_0_), channel_id=1, source_target_pairs={{0,1},{1,0},{2,3},{3,2},{4,5},{5,4},{6,7},{7,6},{8,9},{9,8},{10,11... | collective-permute-start | bytes 786440 | tf_op jit(solution)/shard_map/ppermute | solution.py:392
  76.7 4.3 %collective-permute-start.29 = (bf16[64,2048]{1,0:T(8,128)(2,1)S(1)}, bf16[64,2048]{1,0:T(8,128)(2,1)S(1)}, u32[]{:S(2)}, u32[]{:S(2)}) collective-permute-start(bf16[64,2048]{1,0:T(8,128)(2,1)S(1)} %get-tuple-element.62.refs_6_), channel_id=1, source_target_pairs={{0,4},{4,0},{8,12},{12,8},{1,5},{5,1},{9,13},{13,9},{2,6},{6,2},{1... | collective-permute-start | bytes 786440 | tf_op jit(solution)/shard_map/ppermute | solution.py:358
  79.8 1.5 %collective-permute-start.30 = (bf16[64,2048]{1,0:T(8,128)(2,1)S(1)}, bf16[64,2048]{1,0:T(8,128)(2,1)S(1)}, u32[]{:S(2)}, u32[]{:S(2)}) collective-permute-start(bf16[64,2048]{1,0:T(8,128)(2,1)S(1)} %get-tuple-element.63), channel_id=1, source_target_pairs={{0,4},{4,0},{8,12},{12,8},{1,5},{5,1},{9,13},{13,9},{2,6},{6,2},{1... | collective-permute-start | bytes 786440 | tf_op jit(solution)/shard_map/ppermute | solution.py:358
  80.0 7.5 %collective-permute-start.20 = (bf16[128,1024]{1,0:T(8,128)(2,1)S(1)}, bf16[128,1024]{1,0:T(8,128)(2,1)S(1)}, u32[]{:S(2)}, u32[]{:S(2)}) collective-permute-start(bf16[128,1024]{1,0:T(8,128)(2,1)S(1)} %mix.12.refs_5_.refs_0_), channel_id=1, source_target_pairs={{0,1},{1,0},{2,3},{3,2},{4,5},{5,4},{6,7},{7,6},{8,9},{9,8},{10,11... | collective-permute-start | bytes 786440 | tf_op jit(solution)/shard_map/ppermute | solution.py:392
  84.6 15.2 %collective-permute-start.35 = (bf16[64,2048]{1,0:T(8,128)(2,1)S(1)}, bf16[64,2048]{1,0:T(8,128)(2,1)S(1)}, u32[]{:S(2)}, u32[]{:S(2)}) collective-permute-start(bf16[64,2048]{1,0:T(8,128)(2,1)S(1)} %get-tuple-element.64.refs_3_.refs_4_), channel_id=1, source_target_pairs={{0,8},{4,12},{8,0},{12,4},{1,9},{5,13},{9,1},{13,5},{2,10},{6,14},... | collective-permute-start | bytes 786440 | tf_op jit(solution)/shard_map/ppermute | solution.py:358
  84.7 7.2 %copy-start.7 = (f32[2048]{0:T(1024)S(1)}, f32[2048]{0:T(1024)}, u32[]{:S(2)}) copy-start(f32[2048]{0:T(1024)} %param.11) | copy-start | bytes 24580
  84.7 15.2 %collective-permute-start.36 = (bf16[64,2048]{1,0:T(8,128)(2,1)S(1)}, bf16[64,2048]{1,0:T(8,128)(2,1)S(1)}, u32[]{:S(2)}, u32[]{:S(2)}) collective-permute-start(bf16[64,2048]{1,0:T(8,128)(2,1)S(1)} %get-tuple-element.70), channel_id=1, source_target_pairs={{0,8},{4,12},{8,0},{12,4},{1,9},{5,13},{9,1},{13,5},{2,10},{6,14},... | collective-permute-start | bytes 786440 | tf_op jit(solution)/shard_map/ppermute | solution.py:358
  90.2 9.7 %collective-permute-start.33 = (bf16[64,2048]{1,0:T(8,128)(2,1)S(1)}, bf16[64,2048]{1,0:T(8,128)(2,1)S(1)}, u32[]{:S(2)}, u32[]{:S(2)}) collective-permute-start(bf16[64,2048]{1,0:T(8,128)(2,1)S(1)} %get-tuple-element.65.refs_8_.refs_9_), channel_id=1, source_target_pairs={{0,4},{4,0},{8,12},{12,8},{1,5},{5,1},{9,13},{13,9},{2,6},{6,2},{1... | collective-permute-start | bytes 786440 | tf_op jit(solution)/shard_map/ppermute | solution.py:358
  91.8 8.1 %collective-permute-start.34 = (bf16[64,2048]{1,0:T(8,128)(2,1)S(1)}, bf16[64,2048]{1,0:T(8,128)(2,1)S(1)}, u32[]{:S(2)}, u32[]{:S(2)}) collective-permute-start(bf16[64,2048]{1,0:T(8,128)(2,1)S(1)} %get-tuple-element.69), channel_id=1, source_target_pairs={{0,4},{4,0},{8,12},{12,8},{1,5},{5,1},{9,13},{13,9},{2,6},{6,2},{1... | collective-permute-start | bytes 786440 | tf_op jit(solution)/shard_map/ppermute | solution.py:358
  99.8 2.0 %collective-permute-start.32 = (bf16[128,2048]{1,0:T(8,128)(2,1)S(1)}, bf16[128,2048]{1,0:T(8,128)(2,1)S(1)}, u32[]{:S(2)}, u32[]{:S(2)}) collective-permute-start(bf16[128,2048]{1,0:T(8,128)(2,1)S(1)} %get-tuple-element.67), channel_id=1, source_target_pairs={{0,4},{4,0},{8,12},{12,8},{1,5},{5,1},{9,13},{13,9},{2,6},{6,2},{1... | collective-permute-start | bytes 1572872 | tf_op jit(solution)/shard_map/ppermute | solution.py:358

commit v5 on v4

--- a/solution.py
+++ b/solution.py
@@ -346,6 +346,37 @@
     terms = jnp.concatenate(terms, axis=0)
     owned = lax.psum_scatter(terms, "tensor", scatter_dimension=0, tiled=True).astype(jnp.float32)
     return owned + down_bias[None, :]
+
+
+def finish_kernel(counts, *refs):
+    out, buf, sems = refs[-3:]
+    copies = []
+    for j, (n_near, n_far) in enumerate(counts):
+        own, nears, fars = refs[0], refs[1 : 1 + n_near], refs[1 + n_near : 1 + n_near + n_far]
+        refs = refs[1 + n_near + n_far :]
+        buf[j] = own[...]
+        for parts in (nears, fars):
+            for at, part in enumerate(parts):
+                buf[j, pl.ds(at * part.shape[0], part.shape[0]), :] += part[...].astype(jnp.float32)
+        copies.append(pltpu.make_async_copy(buf.at[j], out.at[pl.ds(j * BLK, BLK)], sems.at[j]))
+        copies[-1].start()
+    for copy in copies:
+        copy.wait()
+
+
+def finish(own, near, far):
+    operands = [x for j in range(2) for x in [own[j], *near[j], *far[j]]]
+    width = own[0].shape[1]
+    return pl.pallas_call(
+        functools.partial(finish_kernel, [(len(near[j]), len(far[j])) for j in range(2)]),
+        out_shape=jax.ShapeDtypeStruct((2 * BLK, width), jnp.float32),
+        in_specs=[VMEM] * len(operands),
+        out_specs=ANY,
+        scratch_shapes=[pltpu.VMEM((2, BLK, width), jnp.float32), pltpu.SemaphoreType.DMA((2,))],
+        compiler_params=pltpu.CompilerParams(vmem_limit_bytes=VMEM_LIMIT),
+        cost_estimate=pl.CostEstimate(flops=COST, bytes_accessed=COST, transcendentals=0),
+        name="finish",
+    )(*operands)
 
 
 def staged(rows_in, up_weight, up_bias, down_weight, down_bias, active_ids, active_counts):
@@ -419,10 +450,7 @@
             {1: near, 2: far, 3: terms}[flip][j] = swap(out, 2 if flip == 2 else 1)
         after = latest
 
-    def joined(parts):
-        return jnp.concatenate(parts, axis=0).astype(f32)
-
-    return jnp.concatenate([own[j] + joined(near[j]) + joined(far[j]) for j in range(2)], axis=0)
+    return finish(own, near, far)
 
 
 def solution(mesh):

time: 103 us -> 135 us (1.31)
  the two profiles are of different devices: /device:TPU:7 before, /device:TPU:12 now
where the time goes in v5:
time: 135 us; the launch traced here: 133 us
  Pallas kernels  45.1 us (33%)
  waiting for transfers between devices  42.6 us (32%)
  starting transfers between devices  41.4 us (31%)
  local copies, waits for them, and re-layouts  2.96 us (2%)
    ppermute x11, waiting for transfers between devices, staged(): got[i] = lax.ppermute(sent, 'dp', [(0, 1), (1, 0), (2, 3), (3, 2)])  28.1 us
    ppermute x8, starting transfers between devices, staged(): other[i - 1] = lax.ppermute(latest, 'dp', [(1, 2), (2, 1)])  24.7 us
    pallas_call x6, Pallas kernels, down(): pl.pallas_call(functools.partial(down_kernel, whiches, len(inits), bias i...  19.3 us
    pallas_call x6, Pallas kernels, up(): pl.pallas_call(functools.partial(up_kernel, [(w, len(r)) for w, r in zip(...  17.9 us
    ppermute x18, waiting for transfers between devices, swap(): lax.ppermute(part, 'tensor', [(t, t ^ flip) for t in range(4)])  11.8 us
    ppermute x18, starting transfers between devices, swap(): lax.ppermute(part, 'tensor', [(t, t ^ flip) for t in range(4)])  9.36 us
    ppermute x11, starting transfers between devices, staged(): got[i] = lax.ppermute(sent, 'dp', [(0, 1), (1, 0), (2, 3), (3, 2)])  7.3 us
    pallas_call x1, Pallas kernels, head(): pl.pallas_call(functools.partial(head_kernel, order), out_shape=[jax.Shap...  4.92 us
  transfers between devices with their start and end apart: 37, of which 10 were waited for; matrix products, arithmetic and copies ran while one was open for 0% of the time, Pallas kernels for 26%

profile of v5, /device:TPU:12, one launch (start us, length us, event | category | flops | bytes accessed | tf_op | source)
XLA Modules:
  0.0 132.7 jit_solution(12147135611642120597)
XLA Ops:
  0.0 4.9 %head.1 = (bf16[128,1024]{1,0:T(8,128)(2,1)}, bf16[128,2048]{1,0:T(8,128)(2,1)}, bf16[128,2048]{1,0:T(8,128)(2,1)}, f32[8,1024]{1,0:T(8,128)}) custom-call(s32[8,1,8]{2,1,0:T(1,128)} %ids.25, s32[1,8]{1,0:T(1,128)} %bitcast.3, bf16[256,2048]{1,0:T(8,128)(2,1)} %rows.1, bf16[2048,8192]{1,0:T(8,128)(2,1)} %weight.13, f32[64,128]{1,0:T(8,128)} %bitcast.17), custom_call_target="tpu_custom_call" | custom-call | flops 1 | bytes 1 | tf_op jit(solution)/shard_map/head/pallas_call | solution.py:94
  5.0 1.0 collective-permute-start.2
  6.0 0.4 collective-permute-start
  6.5 8.4 %collective-permute-done.refs_1_ = bf16[128,1024]{1,0:T(8,128)(2,1)S(1)} collective-permute-done((bf16[128,1024]{1,0:T(8,128)(2,1)}, bf16[128,1024]{1,0:T(8,128)(2,1)S(1)}, u32[]{:S(2)}, u32[]{:S(2)}) %collective-permute-start) | collective-permute-done | bytes 262176 | tf_op jit(solution)/shard_map/ppermute | solution.py:423
  14.9 0.9 copy-done.1
  15.9 3.5 %collective-permute-start.1 = (bf16[128,1024]{1,0:T(8,128)(2,1)S(1)}, bf16[128,1024]{1,0:T(8,128)(2,1)S(1)}, u32[]{:S(2)}, u32[]{:S(2)}) collective-permute-start(bf16[128,1024]{1,0:T(8,128)(2,1)S(1)} %fold.8.refs_0_), channel_id=1, source_target_pairs={{1,2},{2,1},{5,6},{6,5},{9,10},{10,9},{13,14},{14,13},{17,18},{18,... | collective-permute-start | bytes 786440 | tf_op jit(solution)/shard_map/ppermute | solution.py:432
  19.5 0.9 copy-done.2
  20.5 1.0 copy-done.4
  21.5 3.1 %up.6 = (bf16[128,1024]{1,0:T(8,128)(2,1)S(1)}, bf16[128,1024]{1,0:T(8,128)(2,1)S(1)}) custom-call(s32[8,1,8]{2,1,0:T(1,128)S(1)} %copy-done.3, s32[1,8]{1,0:T(1,128)S(1)} %bitcast.4, bf16[2048,8192]{1,0:T(8,128)(2,1)} %weight.13, bf16[128,2048]{1,0:T(8,128)(2,1)S(1)} %collective-permute-done.3.refs_0_, bf16[128,2048]{1,0:T(8,128)(2,1)S(1)} %copy-done.4, ...), custom_call_target="tpu_custom_call" | custom-call | flops 1 | bytes 1 | tf_op jit(solution)/shard_map/up/pallas_call | solution.py:158
  24.7 2.0 %collective-permute-start.10 = (bf16[128,1024]{1,0:T(8,128)(2,1)S(1)}, bf16[128,1024]{1,0:T(8,128)(2,1)S(1)}, u32[]{:S(2)}, u32[]{:S(2)}) collective-permute-start(bf16[128,1024]{1,0:T(8,128)(2,1)S(1)} %get-tuple-element.42.refs_1_.refs_0_), channel_id=1, source_target_pairs={{0,1},{1,0},{2,3},{3,2},{4,5},{5,4},{6,7},{7,6},{8,9},{9,8},{10,11... | collective-permute-start | bytes 786440 | tf_op jit(solution)/shard_map/ppermute | solution.py:423
  26.7 2.1 %up.7 = (bf16[128,1024]{1,0:T(8,128)(2,1)S(1)}, bf16[64,2048]{1,0:T(8,128)(2,1)S(1)}, bf16[64,2048]{1,0:T(8,128)(2,1)S(1)}) custom-call(s32[8,1,8]{2,1,0:T(1,128)S(1)} %copy-done.3, s32[1,8]{1,0:T(1,128)S(1)} %bitcast.5, bf16[2048,8192]{1,0:T(8,128)(2,1)} %weight.13, bf16[128,2048]{1,0:T(8,128)(2,1)S(1)} %collective-permute-done.2.refs_0_, ...), custom_call_target="tpu_custom_call" | custom-call | flops 1 | bytes 1 | tf_op jit(solution)/shard_map/up/pallas_call | solution.py:158
  28.9 1.2 collective-permute-start.7
  30.3 3.6 %collective-permute-done.5.refs_1_ = bf16[128,1024]{1,0:T(8,128)(2,1)S(1)} collective-permute-done((bf16[128,1024]{1,0:T(8,128)(2,1)S(1)}, bf16[128,1024]{1,0:T(8,128)(2,1)S(1)}, u32[]{:S(2)}, u32[]{:S(2)}) %collective-permute-start.5) | collective-permute-done | bytes 262176 | tf_op jit(solution)/shard_map/ppermute | solution.py:423
  34.0 5.5 %collective-permute-done.10.refs_1_ = bf16[128,1024]{1,0:T(8,128)(2,1)S(1)} collective-permute-done((bf16[128,1024]{1,0:T(8,128)(2,1)S(1)}, bf16[128,1024]{1,0:T(8,128)(2,1)S(1)}, u32[]{:S(2)}, u32[]{:S(2)}) %collective-permute-start.10) | collective-permute-done | bytes 262176 | tf_op jit(solution)/shard_map/ppermute | solution.py:423
  39.5 2.3 %collective-permute-start.6 = (bf16[128,1024]{1,0:T(8,128)(2,1)S(1)}, bf16[128,1024]{1,0:T(8,128)(2,1)S(1)}, u32[]{:S(2)}, u32[]{:S(2)}) collective-permute-start(bf16[128,1024]{1,0:T(8,128)(2,1)S(1)} %fold.9.refs_0_), channel_id=1, source_target_pairs={{1,2},{2,1},{5,6},{6,5},{9,10},{10,9},{13,14},{14,13},{17,18},{18,... | collective-permute-start | bytes 786440 | tf_op jit(solution)/shard_map/ppermute | solution.py:432
  41.9 3.5 %collective-permute-start.11 = (bf16[128,1024]{1,0:T(8,128)(2,1)S(1)}, bf16[128,1024]{1,0:T(8,128)(2,1)S(1)}, u32[]{:S(2)}, u32[]{:S(2)}) collective-permute-start(bf16[128,1024]{1,0:T(8,128)(2,1)S(1)} %fold.10.refs_0_), channel_id=1, source_target_pairs={{1,2},{2,1},{5,6},{6,5},{9,10},{10,9},{13,14},{14,13},{17,18},{18,... | collective-permute-start | bytes 786440 | tf_op jit(solution)/shard_map/ppermute | solution.py:432
  45.5 3.3 %up.8.refs_3_.refs_1_.refs_0_ = bf16[128,1024]{1,0:T(8,128)(2,1)S(1)} custom-call(s32[8,1,8]{2,1,0:T(1,128)S(1)} %copy-done.3, s32[1,8]{1,0:T(1,128)S(1)} %bitcast.6, bf16[2048,8192]{1,0:T(8,128)(2,1)} %weight.13, bf16[64,2048]{1,0:T(8,128)(2,1)S(1)} %collective-permute-done.7.refs_0_, bf16[64,2048]{1,0:T(8,128)(2,1)S(1)} %collective-permute-done.8.refs_1_, ...), custom_call_target="tpu_custom_call" | custom-call | flops 1 | bytes 1 | tf_op jit(solution)/shard_map/up/pallas_call | solution.py:158
  48.9 3.3 %up.9 = (bf16[128,1024]{1,0:T(8,128)(2,1)S(1)}, bf16[64,2048]{1,0:T(8,128)(2,1)S(1)}, bf16[64,2048]{1,0:T(8,128)(2,1)S(1)}) custom-call(s32[8,1,8]{2,1,0:T(1,128)S(1)} %copy-done.3, s32[1,8]{1,0:T(1,128)S(1)} %bitcast.7, bf16[2048,8192]{1,0:T(8,128)(2,1)} %weight.13, bf16[128,2048]{1,0:T(8,128)(2,1)S(1)} %collective-permute-done.12.refs_0_, ...), custom_call_target="tpu_custom_call" | custom-call | flops 1 | bytes 1 | tf_op jit(solution)/shard_map/up/pallas_call | solution.py:158
  52.3 0.5 collective-permute-start.16
  52.9 2.4 %collective-permute-start.21 = (bf16[128,1024]{1,0:T(8,128)(2,1)S(1)}, bf16[128,1024]{1,0:T(8,128)(2,1)S(1)}, u32[]{:S(2)}, u32[]{:S(2)}) collective-permute-start(bf16[128,1024]{1,0:T(8,128)(2,1)S(1)} %fold.13.refs_0_), channel_id=1, source_target_pairs={{1,2},{2,1},{5,6},{6,5},{9,10},{10,9},{13,14},{14,13},{17,18},{18,... | collective-permute-start | bytes 786440 | tf_op jit(solution)/shard_map/ppermute | solution.py:432
  55.6 2.1 %collective-permute-start.13 = (bf16[128,1024]{1,0:T(8,128)(2,1)S(1)}, bf16[128,1024]{1,0:T(8,128)(2,1)S(1)}, u32[]{:S(2)}, u32[]{:S(2)}) collective-permute-start(bf16[128,1024]{1,0:T(8,128)(2,1)S(1)} %get-tuple-element.53), channel_id=1, source_target_pairs={{0,1},{1,0},{2,3},{3,2},{4,5},{5,4},{6,7},{7,6},{8,9},{9,8},{10,11... | collective-permute-start | bytes 786440 | tf_op jit(solution)/shard_map/ppermute | solution.py:423
  57.7 2.6 %up.10.refs_1_.refs_3_.refs_0_ = bf16[128,1024]{1,0:T(8,128)(2,1)S(1)} custom-call(s32[8,1,8]{2,1,0:T(1,128)S(1)} %copy-done.3, s32[1,8]{1,0:T(1,128)S(1)} %bitcast.8, bf16[2048,8192]{1,0:T(8,128)(2,1)} %weight.13, bf16[64,2048]{1,0:T(8,128)(2,1)S(1)} %collective-permute-done.15.refs_0_, bf16[64,2048]{1,0:T(8,128)(2,1)S(1)} %collective-permute-done.16.refs_1_, ...), custom_call_target="tpu_custom_call" | custom-call | flops 1 | bytes 1 | tf_op jit(solution)/shard_map/up/pallas_call | solution.py:158
  60.3 2.8 %collective-permute-done.21.refs_1_ = bf16[128,1024]{1,0:T(8,128)(2,1)S(1)} collective-permute-done((bf16[128,1024]{1,0:T(8,128)(2,1)S(1)}, bf16[128,1024]{1,0:T(8,128)(2,1)S(1)}, u32[]{:S(2)}, u32[]{:S(2)}) %collective-permute-start.21) | collective-permute-done | bytes 262176 | tf_op jit(solution)/shard_map/ppermute | solution.py:432
  63.3 1.4 %collective-permute-done.9.refs_1_.refs_3_ = bf16[128,1024]{1,0:T(8,128)(2,1)S(1)} collective-permute-done((bf16[128,1024]{1,0:T(8,128)(2,1)S(1)}, bf16[128,1024]{1,0:T(8,128)(2,1)S(1)}, u32[]{:S(2)}, u32[]{:S(2)}) %collective-permute-start.9) | collective-permute-done | bytes 262176 | tf_op jit(solution)/shard_map/ppermute | solution.py:423
  64.7 3.5 %collective-permute-start.17 = (bf16[128,1024]{1,0:T(8,128)(2,1)S(1)}, bf16[128,1024]{1,0:T(8,128)(2,1)S(1)}, u32[]{:S(2)}, u32[]{:S(2)}) collective-permute-start(bf16[128,1024]{1,0:T(8,128)(2,1)S(1)} %fold.11.refs_0_), channel_id=1, source_target_pairs={{1,2},{2,1},{5,6},{6,5},{9,10},{10,9},{13,14},{14,13},{17,18},{18,... | collective-permute-start | bytes 786440 | tf_op jit(solution)/shard_map/ppermute | solution.py:432
  68.2 3.3 %up.11.refs_3_.refs_0_ = bf16[128,1024]{1,0:T(8,128)(2,1)S(1)} custom-call(s32[8,1,8]{2,1,0:T(1,128)S(1)} %copy-done.3, s32[1,8]{1,0:T(1,128)S(1)} %bitcast.9, bf16[2048,8192]{1,0:T(8,128)(2,1)} %weight.13, bf16[128,2048]{1,0:T(8,128)(2,1)S(1)} %collective-permute-done.14.refs_0_, bf16[128,1024]{1,0:T(8,128)(2,1)S(1)} %up.10.refs_1_.refs_3_.refs_0_), custom_call_target="tpu_custom_call" | custom-call | flops 1 | bytes 1 | tf_op jit(solution)/shard_map/up/pallas_call | solution.py:158
  71.6 2.3 %collective-permute-start.25 = (bf16[128,1024]{1,0:T(8,128)(2,1)S(1)}, bf16[128,1024]{1,0:T(8,128)(2,1)S(1)}, u32[]{:S(2)}, u32[]{:S(2)}) collective-permute-start(bf16[128,1024]{1,0:T(8,128)(2,1)S(1)} %fold.15.refs_0_), channel_id=1, source_target_pairs={{1,2},{2,1},{5,6},{6,5},{9,10},{10,9},{13,14},{14,13},{17,18},{18,... | collective-permute-start | bytes 786440 | tf_op jit(solution)/shard_map/ppermute | solution.py:432
  74.0 0.7 collective-permute-done.22.refs_1_
  74.8 2.4 %down.6 = (bf16[64,2048]{1,0:T(8,128)(2,1)S(1)}, bf16[64,2048]{1,0:T(8,128)(2,1)S(1)}) custom-call(s32[8,1,8]{2,1,0:T(1,128)S(1)} %copy-done.3, s32[1,8]{1,0:T(1,128)S(1)} %bitcast.10, bf16[128,1024]{1,0:T(8,128)(2,1)S(1)} %get-tuple-element.59.refs_0_, bf16[128,1024]{1,0:T(8,128)(2,1)S(1)} %collective-permute-done.22.refs_1_, bf16[8192,2048]{1,0:T(8,128)(2,1)} %refs_6_.1, ...), custom_call_target="tpu_custom_call" | custom-call | flops 1 | bytes 1 | tf_op jit(solution)/shard_map/down/pallas_call | solution.py:265
  77.3 0.3 collective-permute-start.18
  77.6 0.5 collective-permute-start.27
  78.1 3.5 %collective-permute-start.23 = (bf16[128,1024]{1,0:T(8,128)(2,1)S(1)}, bf16[128,1024]{1,0:T(8,128)(2,1)S(1)}, u32[]{:S(2)}, u32[]{:S(2)}) collective-permute-start(bf16[128,1024]{1,0:T(8,128)(2,1)S(1)} %fold.14.refs_0_.refs_3_), channel_id=1, source_target_pairs={{1,2},{2,1},{5,6},{6,5},{9,10},{10,9},{13,14},{14,13},{17,18},{18,... | collective-permute-start | bytes 786440 | tf_op jit(solution)/shard_map/ppermute | solution.py:432
  81.8 4.5 %collective-permute-done.18.refs_1_ = bf16[128,1024]{1,0:T(8,128)(2,1)S(1)} collective-permute-done((bf16[128,1024]{1,0:T(8,128)(2,1)S(1)}, bf16[128,1024]{1,0:T(8,128)(2,1)S(1)}, u32[]{:S(2)}, u32[]{:S(2)}) %collective-permute-start.18) | collective-permute-done | bytes 262176 | tf_op jit(solution)/shard_map/ppermute | solution.py:423
  86.4 3.7 %collective-permute-start.19 = (bf16[128,1024]{1,0:T(8,128)(2,1)S(1)}, bf16[128,1024]{1,0:T(8,128)(2,1)S(1)}, u32[]{:S(2)}, u32[]{:S(2)}) collective-permute-start(bf16[128,1024]{1,0:T(8,128)(2,1)S(1)} %fold.12.refs_0_.refs_5_), channel_id=1, source_target_pairs={{1,2},{2,1},{5,6},{6,5},{9,10},{10,9},{13,14},{14,13},{17,18},{18,... | collective-permute-start | bytes 786440 | tf_op jit(solution)/shard_map/ppermute | solution.py:432
  90.1 3.3 %down.7.refs_4_ = bf16[128,2048]{1,0:T(8,128)(2,1)S(1)} custom-call(s32[8,1,8]{2,1,0:T(1,128)S(1)} %copy-done.3, s32[1,8]{1,0:T(1,128)S(1)} %bitcast.11, bf16[128,1024]{1,0:T(8,128)(2,1)S(1)} %get-tuple-element.58.refs_0_, bf16[128,1024]{1,0:T(8,128)(2,1)S(1)} %collective-permute-done.18.refs_1_, bf16[8192,2048]{1,0:T(8,128)(2,1)} %refs_6_.1, ...), custom_call_target="tpu_custom_call" | custom-call | flops 1 | bytes 1 | tf_op jit(solution)/shard_map/down/pallas_call | solution.py:265
  93.4 2.6 %collective-permute-start.31 = (bf16[128,2048]{1,0:T(8,128)(2,1)S(1)}, bf16[128,2048]{1,0:T(8,128)(2,1)S(1)}, u32[]{:S(2)}, u32[]{:S(2)}) collective-permute-start(bf16[128,2048]{1,0:T(8,128)(2,1)S(1)} %down.7.refs_4_), channel_id=1, source_target_pairs={{0,8},{4,12},{8,0},{12,4},{1,9},{5,13},{9,1},{13,5},{2,10},{6,14},... | collective-permute-start | bytes 1572872 | tf_op jit(solution)/shard_map/ppermute | solution.py:389
  96.2 3.2 %down.8 = (bf16[64,2048]{1,0:T(8,128)(2,1)S(1)}, bf16[64,2048]{1,0:T(8,128)(2,1)S(1)}) custom-call(s32[8,1,8]{2,1,0:T(1,128)S(1)} %copy-done.3, s32[1,8]{1,0:T(1,128)S(1)} %bitcast.12, bf16[128,1024]{1,0:T(8,128)(2,1)S(1)} %mix.15.refs_0_, bf16[128,1024]{1,0:T(8,128)(2,1)S(1)} %collective-permute-done.26.refs_1_, bf16[8192,2048]{1,0:T(8,128)(2,1)} %refs_6_.1, ...), custom_call_target="tpu_custom_call" | custom-call | flops 1 | bytes 1 | tf_op jit(solution)/shard_map/down/pallas_call | solution.py:265
  99.5 0.5 collective-permute-start.29
  100.1 2.1 %collective-permute-start.20 = (bf16[128,1024]{1,0:T(8,128)(2,1)S(1)}, bf16[128,1024]{1,0:T(8,128)(2,1)S(1)}, u32[]{:S(2)}, u32[]{:S(2)}) collective-permute-start(bf16[128,1024]{1,0:T(8,128)(2,1)S(1)} %mix.12.refs_5_.refs_0_), channel_id=1, source_target_pairs={{0,1},{1,0},{2,3},{3,2},{4,5},{5,4},{6,7},{7,6},{8,9},{9,8},{10,11... | collective-permute-start | bytes 786440 | tf_op jit(solution)/shard_map/ppermute | solution.py:423
  102.2 0.3 collective-permute-done.24.refs_1_
  102.5 2.7 %down.9 = (bf16[64,2048]{1,0:T(8,128)(2,1)S(1)}, bf16[64,2048]{1,0:T(8,128)(2,1)S(1)}) custom-call(s32[8,1,8]{2,1,0:T(1,128)S(1)} %copy-done.3, s32[1,8]{1,0:T(1,128)S(1)} %bitcast.13, bf16[128,1024]{1,0:T(8,128)(2,1)S(1)} %mix.14.refs_3_.refs_0_, bf16[128,1024]{1,0:T(8,128)(2,1)S(1)} %collective-permute-done.24.refs_1_, bf16[8192,2048]{1,0:T(8,128)(2,1)} %refs_6_.1, ...), custom_call_target="tpu_custom_call" | custom-call | flops 1 | bytes 1 | tf_op jit(solution)/shard_map/down/pallas_call | solution.py:265
  105.2 3.5 %collective-permute-done.20.refs_1_ = bf16[128,1024]{1,0:T(8,128)(2,1)S(1)} collective-permute-done((bf16[128,1024]{1,0:T(8,128)(2,1)S(1)}, bf16[128,1024]{1,0:T(8,128)(2,1)S(1)}, u32[]{:S(2)}, u32[]{:S(2)}) %collective-permute-start.20) | collective-permute-done | bytes 262176 | tf_op jit(solution)/shard_map/ppermute | solution.py:423
  108.7 3.2 %down.10 = (bf16[64,2048]{1,0:T(8,128)(2,1)S(1)}, bf16[64,2048]{1,0:T(8,128)(2,1)S(1)}) custom-call(s32[8,1,8]{2,1,0:T(1,128)S(1)} %copy-done.3, s32[1,8]{1,0:T(1,128)S(1)} %bitcast.14, bf16[128,1024]{1,0:T(8,128)(2,1)S(1)} %mix.12.refs_5_.refs_0_, bf16[128,1024]{1,0:T(8,128)(2,1)S(1)} %collective-permute-done.20.refs_1_, bf16[8192,2048]{1,0:T(8,128)(2,1)} %refs_6_.1, ...), custom_call_target="tpu_custom_call" | custom-call | flops 1 | bytes 1 | tf_op jit(solution)/shard_map/down/pallas_call | solution.py:265
  112.0 4.5 %down.11 = (f32[128,2048]{1,0:T(8,128)S(1)}, bf16[128,2048]{1,0:T(8,128)(2,1)S(1)}, f32[128,2048]{1,0:T(8,128)S(1)}) custom-call(s32[8,1,8]{2,1,0:T(1,128)S(1)} %copy-done.3, s32[1,8]{1,0:T(1,128)S(1)} %bitcast.15, bf16[128,1024]{1,0:T(8,128)(2,1)S(1)} %get-tuple-element.44.refs_0_, bf16[128,1024]{1,0:T(8,128)(2,1)S(1)} %collective-permute-done.4.refs_1_, ...), custom_call_target="tpu_custom_call" | custom-call | flops 1 | bytes 1 | tf_op jit(solution)/shard_map/down/pallas_call | solution.py:265
  116.7 2.0 %collective-permute-start.36 = (bf16[64,2048]{1,0:T(8,128)(2,1)S(1)}, bf16[64,2048]{1,0:T(8,128)(2,1)S(1)}, u32[]{:S(2)}, u32[]{:S(2)}) collective-permute-start(bf16[64,2048]{1,0:T(8,128)(2,1)S(1)} %get-tuple-element.70), channel_id=1, source_target_pairs={{0,8},{4,12},{8,0},{12,4},{1,9},{5,13},{9,1},{13,5},{2,10},{6,14},... | collective-permute-start | bytes 786440 | tf_op jit(solution)/shard_map/ppermute | solution.py:389
  118.7 0.5 collective-permute-start.33
  119.2 11.7 %collective-permute-done.36.refs_7_ = bf16[64,2048]{1,0:T(8,128)(2,1)S(1)} collective-permute-done((bf16[64,2048]{1,0:T(8,128)(2,1)S(1)}, bf16[64,2048]{1,0:T(8,128)(2,1)S(1)}, u32[]{:S(2)}, u32[]{:S(2)}) %collective-permute-start.36) | collective-permute-done | bytes 262176 | tf_op jit(solution)/shard_map/ppermute | solution.py:389
  131.0 1.6 %finish.1 = f32[256,2048]{1,0:T(8,128)} custom-call(f32[128,2048]{1,0:T(8,128)S(1)} %get-tuple-element.66.refs_0_, bf16[128,2048]{1,0:T(8,128)(2,1)S(1)} %collective-permute-done.32.refs_1_, bf16[128,2048]{1,0:T(8,128)(2,1)S(1)} %collective-permute-done.31.refs_10_.refs_2_, f32[128,2048]{1,0:T(8,128)S(1)} %get-tuple-element.68.refs_3_, ...), custom_call_target="tpu_custom_call" | custom-call | flops 1 | bytes 1 | tf_op jit(solution)/shard_map/finish/pallas_call | solution.py:370
  (72 shorter events, 2.4 us)
Async XLA Ops:
  0.0 19.5 %copy-start.3 = (s32[8,1,8]{2,1,0:T(1,128)S(1)}, s32[8,1,8]{2,1,0:T(1,128)}, u32[]{:S(2)}) copy-start(s32[8,1,8]{2,1,0:T(1,128)} %ids.25) | copy-start | bytes 772
  0.0 19.5 %copy-start.6 = (s32[8,1]{0,1:T(1,128)S(1)}, s32[8,1]{0,1:T(1,128)}, u32[]{:S(2)}) copy-start(s32[8,1]{0,1:T(1,128)} %param.13) | copy-start | bytes 100
  4.9 14.5 %collective-permute-start.3 = (bf16[128,2048]{1,0:T(8,128)(2,1)}, bf16[128,2048]{1,0:T(8,128)(2,1)S(1)}, u32[]{:S(2)}, u32[]{:S(2)}) collective-permute-start(bf16[128,2048]{1,0:T(8,128)(2,1)} %get-tuple-element.40), channel_id=1, source_target_pairs={{0,4},{4,0},{8,12},{12,8},{1,5},{5,1},{9,13},{13,9},{2,6},{6,2},{1... | collective-permute-start | bytes 1572872 | tf_op jit(solution)/shard_map/ppermute | solution.py:389
  5.0 21.7 %collective-permute-start.2 = (bf16[128,2048]{1,0:T(8,128)(2,1)}, bf16[128,2048]{1,0:T(8,128)(2,1)S(1)}, u32[]{:S(2)}, u32[]{:S(2)}) collective-permute-start(bf16[128,2048]{1,0:T(8,128)(2,1)} %get-tuple-element.40), channel_id=1, source_target_pairs={{0,12},{4,8},{8,4},{12,0},{1,13},{5,9},{9,5},{13,1},{2,14},{6,10},... | collective-permute-start | bytes 1572872 | tf_op jit(solution)/shard_map/ppermute | solution.py:389
  6.0 8.9 %collective-permute-start = (bf16[128,1024]{1,0:T(8,128)(2,1)}, bf16[128,1024]{1,0:T(8,128)(2,1)S(1)}, u32[]{:S(2)}, u32[]{:S(2)}) collective-permute-start(bf16[128,1024]{1,0:T(8,128)(2,1)} %get-tuple-element.38.refs_0_.refs_2_), channel_id=1, source_target_pairs={{0,1},{1,0},{2,3},{3,2},{4,5},{5,4},{6,7},{7,6},{8,9},{9,8},{10,11... | collective-permute-start | bytes 786440 | tf_op jit(solution)/shard_map/ppermute | solution.py:423
  14.9 1.0 copy-start.1
  15.9 14.2 %collective-permute-start.1 = (bf16[128,1024]{1,0:T(8,128)(2,1)S(1)}, bf16[128,1024]{1,0:T(8,128)(2,1)S(1)}, u32[]{:S(2)}, u32[]{:S(2)}) collective-permute-start(bf16[128,1024]{1,0:T(8,128)(2,1)S(1)} %fold.8.refs_0_), channel_id=1, source_target_pairs={{1,2},{2,1},{5,6},{6,5},{9,10},{10,9},{13,14},{14,13},{17,18},{18,... | collective-permute-start | bytes 786440 | tf_op jit(solution)/shard_map/ppermute | solution.py:432
  19.4 10.8 %copy-start = (f32[8,1024]{1,0:T(8,128)S(1)}, f32[8,1024]{1,0:T(8,128)}, u32[]{:S(2)}) copy-start(f32[8,1024]{1,0:T(8,128)} %get-tuple-element.39.refs_2_) | copy-start | bytes 98308
  19.4 29.5 %collective-permute-start.12 = (bf16[128,2048]{1,0:T(8,128)(2,1)}, bf16[128,2048]{1,0:T(8,128)(2,1)S(1)}, u32[]{:S(2)}, u32[]{:S(2)}) collective-permute-start(bf16[128,2048]{1,0:T(8,128)(2,1)} %get-tuple-element.41.refs_1_), channel_id=1, source_target_pairs={{0,12},{4,8},{8,4},{12,0},{1,13},{5,9},{9,5},{13,1},{2,14},{6,10},... | collective-permute-start | bytes 1572872 | tf_op jit(solution)/shard_map/ppermute | solution.py:389
  19.5 1.0 copy-start.2
  20.5 1.0 copy-start.4
  21.5 23.9 %copy-start.5 = (bf16[128,2048]{1,0:T(8,128)(2,1)S(1)}, bf16[128,2048]{1,0:T(8,128)(2,1)}, u32[]{:S(2)}) copy-start(bf16[128,2048]{1,0:T(8,128)(2,1)} %get-tuple-element.41.refs_1_) | copy-start | bytes 1572868
  24.6 9.2 %collective-permute-start.5 = (bf16[128,1024]{1,0:T(8,128)(2,1)S(1)}, bf16[128,1024]{1,0:T(8,128)(2,1)S(1)}, u32[]{:S(2)}, u32[]{:S(2)}) collective-permute-start(bf16[128,1024]{1,0:T(8,128)(2,1)S(1)} %get-tuple-element.46.refs_0_), channel_id=1, source_target_pairs={{0,1},{1,0},{2,3},{3,2},{4,5},{5,4},{6,7},{7,6},{8,9},{9,8},{10,11... | collective-permute-start | bytes 786440 | tf_op jit(solution)/shard_map/ppermute | solution.py:423
  24.7 14.8 %collective-permute-start.10 = (bf16[128,1024]{1,0:T(8,128)(2,1)S(1)}, bf16[128,1024]{1,0:T(8,128)(2,1)S(1)}, u32[]{:S(2)}, u32[]{:S(2)}) collective-permute-start(bf16[128,1024]{1,0:T(8,128)(2,1)S(1)} %get-tuple-element.42.refs_1_.refs_0_), channel_id=1, source_target_pairs={{0,1},{1,0},{2,3},{3,2},{4,5},{5,4},{6,7},{7,6},{8,9},{9,8},{10,11... | collective-permute-start | bytes 786440 | tf_op jit(solution)/shard_map/ppermute | solution.py:423
  28.9 13.1 %collective-permute-start.7 = (bf16[64,2048]{1,0:T(8,128)(2,1)S(1)}, bf16[64,2048]{1,0:T(8,128)(2,1)S(1)}, u32[]{:S(2)}, u32[]{:S(2)}) collective-permute-start(bf16[64,2048]{1,0:T(8,128)(2,1)S(1)} %get-tuple-element.47), channel_id=1, source_target_pairs={{0,4},{4,0},{8,12},{12,8},{1,5},{5,1},{9,13},{13,9},{2,6},{6,2},{1... | collective-permute-start | bytes 786440 | tf_op jit(solution)/shard_map/ppermute | solution.py:389
  30.1 15.4 %collective-permute-start.8 = (bf16[64,2048]{1,0:T(8,128)(2,1)S(1)}, bf16[64,2048]{1,0:T(8,128)(2,1)S(1)}, u32[]{:S(2)}, u32[]{:S(2)}) collective-permute-start(bf16[64,2048]{1,0:T(8,128)(2,1)S(1)} %get-tuple-element.48), channel_id=1, source_target_pairs={{0,4},{4,0},{8,12},{12,8},{1,5},{5,1},{9,13},{13,9},{2,6},{6,2},{1... | collective-permute-start | bytes 786440 | tf_op jit(solution)/shard_map/ppermute | solution.py:389
  33.9 18.4 %collective-permute-start.4 = (bf16[128,1024]{1,0:T(8,128)(2,1)S(1)}, bf16[128,1024]{1,0:T(8,128)(2,1)S(1)}, u32[]{:S(2)}, u32[]{:S(2)}) collective-permute-start(bf16[128,1024]{1,0:T(8,128)(2,1)S(1)} %get-tuple-element.45), channel_id=1, source_target_pairs={{0,1},{1,0},{2,3},{3,2},{4,5},{5,4},{6,7},{7,6},{8,9},{9,8},{10,11... | collective-permute-start | bytes 786440 | tf_op jit(solution)/shard_map/ppermute | solution.py:423
  39.5 13.4 %collective-permute-start.6 = (bf16[128,1024]{1,0:T(8,128)(2,1)S(1)}, bf16[128,1024]{1,0:T(8,128)(2,1)S(1)}, u32[]{:S(2)}, u32[]{:S(2)}) collective-permute-start(bf16[128,1024]{1,0:T(8,128)(2,1)S(1)} %fold.9.refs_0_), channel_id=1, source_target_pairs={{1,2},{2,1},{5,6},{6,5},{9,10},{10,9},{13,14},{14,13},{17,18},{18,... | collective-permute-start | bytes 786440 | tf_op jit(solution)/shard_map/ppermute | solution.py:432
  41.9 13.4 %collective-permute-start.11 = (bf16[128,1024]{1,0:T(8,128)(2,1)S(1)}, bf16[128,1024]{1,0:T(8,128)(2,1)S(1)}, u32[]{:S(2)}, u32[]{:S(2)}) collective-permute-start(bf16[128,1024]{1,0:T(8,128)(2,1)S(1)} %fold.10.refs_0_), channel_id=1, source_target_pairs={{1,2},{2,1},{5,6},{6,5},{9,10},{10,9},{13,14},{14,13},{17,18},{18,... | collective-permute-start | bytes 786440 | tf_op jit(solution)/shard_map/ppermute | solution.py:432
  45.5 22.7 %collective-permute-start.14 = (bf16[128,2048]{1,0:T(8,128)(2,1)S(1)}, bf16[128,2048]{1,0:T(8,128)(2,1)S(1)}, u32[]{:S(2)}, u32[]{:S(2)}) collective-permute-start(bf16[128,2048]{1,0:T(8,128)(2,1)S(1)} %copy-done.5), channel_id=1, source_target_pairs={{0,4},{4,0},{8,12},{12,8},{1,5},{5,1},{9,13},{13,9},{2,6},{6,2},{1... | collective-permute-start | bytes 1572872 | tf_op jit(solution)/shard_map/ppermute | solution.py:389
  52.2 3.4 %collective-permute-start.15 = (bf16[64,2048]{1,0:T(8,128)(2,1)S(1)}, bf16[64,2048]{1,0:T(8,128)(2,1)S(1)}, u32[]{:S(2)}, u32[]{:S(2)}) collective-permute-start(bf16[64,2048]{1,0:T(8,128)(2,1)S(1)} %get-tuple-element.54), channel_id=1, source_target_pairs={{0,4},{4,0},{8,12},{12,8},{1,5},{5,1},{9,13},{13,9},{2,6},{6,2},{1... | collective-permute-start | bytes 786440 | tf_op jit(solution)/shard_map/ppermute | solution.py:389
  52.3 5.4 %collective-permute-start.16 = (bf16[64,2048]{1,0:T(8,128)(2,1)S(1)}, bf16[64,2048]{1,0:T(8,128)(2,1)S(1)}, u32[]{:S(2)}, u32[]{:S(2)}) collective-permute-start(bf16[64,2048]{1,0:T(8,128)(2,1)S(1)} %get-tuple-element.55), channel_id=1, source_target_pairs={{0,4},{4,0},{8,12},{12,8},{1,5},{5,1},{9,13},{13,9},{2,6},{6,2},{1... | collective-permute-start | bytes 786440 | tf_op jit(solution)/shard_map/ppermute | solution.py:389
  52.9 10.2 %collective-permute-start.21 = (bf16[128,1024]{1,0:T(8,128)(2,1)S(1)}, bf16[128,1024]{1,0:T(8,128)(2,1)S(1)}, u32[]{:S(2)}, u32[]{:S(2)}) collective-permute-start(bf16[128,1024]{1,0:T(8,128)(2,1)S(1)} %fold.13.refs_0_), channel_id=1, source_target_pairs={{1,2},{2,1},{5,6},{6,5},{9,10},{10,9},{13,14},{14,13},{17,18},{18,... | collective-permute-start | bytes 786440 | tf_op jit(solution)/shard_map/ppermute | solution.py:432
  55.4 9.3 %collective-permute-start.9 = (bf16[128,1024]{1,0:T(8,128)(2,1)S(1)}, bf16[128,1024]{1,0:T(8,128)(2,1)S(1)}, u32[]{:S(2)}, u32[]{:S(2)}) collective-permute-start(bf16[128,1024]{1,0:T(8,128)(2,1)S(1)} %get-tuple-element.50), channel_id=1, source_target_pairs={{0,1},{1,0},{2,3},{3,2},{4,5},{5,4},{6,7},{7,6},{8,9},{9,8},{10,11... | collective-permute-start | bytes 786440 | tf_op jit(solution)/shard_map/ppermute | solution.py:423
  55.6 16.0 %collective-permute-start.13 = (bf16[128,1024]{1,0:T(8,128)(2,1)S(1)}, bf16[128,1024]{1,0:T(8,128)(2,1)S(1)}, u32[]{:S(2)}, u32[]{:S(2)}) collective-permute-start(bf16[128,1024]{1,0:T(8,128)(2,1)S(1)} %get-tuple-element.53), channel_id=1, source_target_pairs={{0,1},{1,0},{2,3},{3,2},{4,5},{5,4},{6,7},{7,6},{8,9},{9,8},{10,11... | collective-permute-start | bytes 786440 | tf_op jit(solution)/shard_map/ppermute | solution.py:423
  63.2 11.5 %collective-permute-start.22 = (bf16[128,1024]{1,0:T(8,128)(2,1)S(1)}, bf16[128,1024]{1,0:T(8,128)(2,1)S(1)}, u32[]{:S(2)}, u32[]{:S(2)}) collective-permute-start(bf16[128,1024]{1,0:T(8,128)(2,1)S(1)} %get-tuple-element.57), channel_id=1, source_target_pairs={{0,1},{1,0},{2,3},{3,2},{4,5},{5,4},{6,7},{7,6},{8,9},{9,8},{10,11... | collective-permute-start | bytes 786440 | tf_op jit(solution)/shard_map/ppermute | solution.py:423
  64.7 12.4 %collective-permute-start.17 = (bf16[128,1024]{1,0:T(8,128)(2,1)S(1)}, bf16[128,1024]{1,0:T(8,128)(2,1)S(1)}, u32[]{:S(2)}, u32[]{:S(2)}) collective-permute-start(bf16[128,1024]{1,0:T(8,128)(2,1)S(1)} %fold.11.refs_0_), channel_id=1, source_target_pairs={{1,2},{2,1},{5,6},{6,5},{9,10},{10,9},{13,14},{14,13},{17,18},{18,... | collective-permute-start | bytes 786440 | tf_op jit(solution)/shard_map/ppermute | solution.py:432
  71.6 10.0 %collective-permute-start.25 = (bf16[128,1024]{1,0:T(8,128)(2,1)S(1)}, bf16[128,1024]{1,0:T(8,128)(2,1)S(1)}, u32[]{:S(2)}, u32[]{:S(2)}) collective-permute-start(bf16[128,1024]{1,0:T(8,128)(2,1)S(1)} %fold.15.refs_0_), channel_id=1, source_target_pairs={{1,2},{2,1},{5,6},{6,5},{9,10},{10,9},{13,14},{14,13},{17,18},{18,... | collective-permute-start | bytes 786440 | tf_op jit(solution)/shard_map/ppermute | solution.py:432
  77.3 9.1 %collective-permute-start.18 = (bf16[128,1024]{1,0:T(8,128)(2,1)S(1)}, bf16[128,1024]{1,0:T(8,128)(2,1)S(1)}, u32[]{:S(2)}, u32[]{:S(2)}) collective-permute-start(bf16[128,1024]{1,0:T(8,128)(2,1)S(1)} %get-tuple-element.56), channel_id=1, source_target_pairs={{0,1},{1,0},{2,3},{3,2},{4,5},{5,4},{6,7},{7,6},{8,9},{9,8},{10,11... | collective-permute-start | bytes 786440 | tf_op jit(solution)/shard_map/ppermute | solution.py:423
  77.6 12.5 %collective-permute-start.28 = (bf16[64,2048]{1,0:T(8,128)(2,1)S(1)}, bf16[64,2048]{1,0:T(8,128)(2,1)S(1)}, u32[]{:S(2)}, u32[]{:S(2)}) collective-permute-start(bf16[64,2048]{1,0:T(8,128)(2,1)S(1)} %get-tuple-element.61), channel_id=1, source_target_pairs={{0,4},{4,0},{8,12},{12,8},{1,5},{5,1},{9,13},{13,9},{2,6},{6,2},{1... | collective-permute-start | bytes 786440 | tf_op jit(solution)/shard_map/ppermute | solution.py:389
  77.6 12.5 %collective-permute-start.27 = (bf16[64,2048]{1,0:T(8,128)(2,1)S(1)}, bf16[64,2048]{1,0:T(8,128)(2,1)S(1)}, u32[]{:S(2)}, u32[]{:S(2)}) collective-permute-start(bf16[64,2048]{1,0:T(8,128)(2,1)S(1)} %get-tuple-element.60.refs_6_), channel_id=1, source_target_pairs={{0,4},{4,0},{8,12},{12,8},{1,5},{5,1},{9,13},{13,9},{2,6},{6,2},{1... | collective-permute-start | bytes 786440 | tf_op jit(solution)/shard_map/ppermute | solution.py:389
  78.1 17.9 %collective-permute-start.23 = (bf16[128,1024]{1,0:T(8,128)(2,1)S(1)}, bf16[128,1024]{1,0:T(8,128)(2,1)S(1)}, u32[]{:S(2)}, u32[]{:S(2)}) collective-permute-start(bf16[128,1024]{1,0:T(8,128)(2,1)S(1)} %fold.14.refs_0_.refs_3_), channel_id=1, source_target_pairs={{1,2},{2,1},{5,6},{6,5},{9,10},{10,9},{13,14},{14,13},{17,18},{18,... | collective-permute-start | bytes 786440 | tf_op jit(solution)/shard_map/ppermute | solution.py:432
  81.7 14.4 %collective-permute-start.26 = (bf16[128,1024]{1,0:T(8,128)(2,1)S(1)}, bf16[128,1024]{1,0:T(8,128)(2,1)S(1)}, u32[]{:S(2)}, u32[]{:S(2)}) collective-permute-start(bf16[128,1024]{1,0:T(8,128)(2,1)S(1)} %mix.15.refs_0_), channel_id=1, source_target_pairs={{0,1},{1,0},{2,3},{3,2},{4,5},{5,4},{6,7},{7,6},{8,9},{9,8},{10,11... | collective-permute-start | bytes 786440 | tf_op jit(solution)/shard_map/ppermute | solution.py:423
  86.4 13.6 %collective-permute-start.19 = (bf16[128,1024]{1,0:T(8,128)(2,1)S(1)}, bf16[128,1024]{1,0:T(8,128)(2,1)S(1)}, u32[]{:S(2)}, u32[]{:S(2)}) collective-permute-start(bf16[128,1024]{1,0:T(8,128)(2,1)S(1)} %fold.12.refs_0_.refs_5_), channel_id=1, source_target_pairs={{1,2},{2,1},{5,6},{6,5},{9,10},{10,9},{13,14},{14,13},{17,18},{18,... | collective-permute-start | bytes 786440 | tf_op jit(solution)/shard_map/ppermute | solution.py:432
  93.4 18.6 %collective-permute-start.31 = (bf16[128,2048]{1,0:T(8,128)(2,1)S(1)}, bf16[128,2048]{1,0:T(8,128)(2,1)S(1)}, u32[]{:S(2)}, u32[]{:S(2)}) collective-permute-start(bf16[128,2048]{1,0:T(8,128)(2,1)S(1)} %down.7.refs_4_), channel_id=1, source_target_pairs={{0,8},{4,12},{8,0},{12,4},{1,9},{5,13},{9,1},{13,5},{2,10},{6,14},... | collective-permute-start | bytes 1572872 | tf_op jit(solution)/shard_map/ppermute | solution.py:389
  96.1 6.4 %collective-permute-start.24 = (bf16[128,1024]{1,0:T(8,128)(2,1)S(1)}, bf16[128,1024]{1,0:T(8,128)(2,1)S(1)}, u32[]{:S(2)}, u32[]{:S(2)}) collective-permute-start(bf16[128,1024]{1,0:T(8,128)(2,1)S(1)} %mix.14.refs_3_.refs_0_), channel_id=1, source_target_pairs={{0,1},{1,0},{2,3},{3,2},{4,5},{5,4},{6,7},{7,6},{8,9},{9,8},{10,11... | collective-permute-start | bytes 786440 | tf_op jit(solution)/shard_map/ppermute | solution.py:423
  99.4 3.1 %collective-permute-start.30 = (bf16[64,2048]{1,0:T(8,128)(2,1)S(1)}, bf16[64,2048]{1,0:T(8,128)(2,1)S(1)}, u32[]{:S(2)}, u32[]{:S(2)}) collective-permute-start(bf16[64,2048]{1,0:T(8,128)(2,1)S(1)} %get-tuple-element.63), channel_id=1, source_target_pairs={{0,4},{4,0},{8,12},{12,8},{1,5},{5,1},{9,13},{13,9},{2,6},{6,2},{1... | collective-permute-start | bytes 786440 | tf_op jit(solution)/shard_map/ppermute | solution.py:389
  99.5 3.0 %collective-permute-start.29 = (bf16[64,2048]{1,0:T(8,128)(2,1)S(1)}, bf16[64,2048]{1,0:T(8,128)(2,1)S(1)}, u32[]{:S(2)}, u32[]{:S(2)}) collective-permute-start(bf16[64,2048]{1,0:T(8,128)(2,1)S(1)} %get-tuple-element.62.refs_6_), channel_id=1, source_target_pairs={{0,4},{4,0},{8,12},{12,8},{1,5},{5,1},{9,13},{13,9},{2,6},{6,2},{1... | collective-permute-start | bytes 786440 | tf_op jit(solution)/shard_map/ppermute | solution.py:389
  100.1 11.9 %copy-start.7 = (f32[2048]{0:T(1024)S(1)}, f32[2048]{0:T(1024)}, u32[]{:S(2)}) copy-start(f32[2048]{0:T(1024)} %param.11) | copy-start | bytes 24580
  100.1 8.6 %collective-permute-start.20 = (bf16[128,1024]{1,0:T(8,128)(2,1)S(1)}, bf16[128,1024]{1,0:T(8,128)(2,1)S(1)}, u32[]{:S(2)}, u32[]{:S(2)}) collective-permute-start(bf16[128,1024]{1,0:T(8,128)(2,1)S(1)} %mix.12.refs_5_.refs_0_), channel_id=1, source_target_pairs={{0,1},{1,0},{2,3},{3,2},{4,5},{5,4},{6,7},{7,6},{8,9},{9,8},{10,11... | collective-permute-start | bytes 786440 | tf_op jit(solution)/shard_map/ppermute | solution.py:423
  116.5 14.4 %collective-permute-start.32 = (bf16[128,2048]{1,0:T(8,128)(2,1)S(1)}, bf16[128,2048]{1,0:T(8,128)(2,1)S(1)}, u32[]{:S(2)}, u32[]{:S(2)}) collective-permute-start(bf16[128,2048]{1,0:T(8,128)(2,1)S(1)} %get-tuple-element.67), channel_id=1, source_target_pairs={{0,4},{4,0},{8,12},{12,8},{1,5},{5,1},{9,13},{13,9},{2,6},{6,2},{1... | collective-permute-start | bytes 1572872 | tf_op jit(solution)/shard_map/ppermute | solution.py:389
  116.6 14.3 %collective-permute-start.35 = (bf16[64,2048]{1,0:T(8,128)(2,1)S(1)}, bf16[64,2048]{1,0:T(8,128)(2,1)S(1)}, u32[]{:S(2)}, u32[]{:S(2)}) collective-permute-start(bf16[64,2048]{1,0:T(8,128)(2,1)S(1)} %get-tuple-element.64.refs_3_.refs_4_), channel_id=1, source_target_pairs={{0,8},{4,12},{8,0},{12,4},{1,9},{5,13},{9,1},{13,5},{2,10},{6,14},... | collective-permute-start | bytes 786440 | tf_op jit(solution)/shard_map/ppermute | solution.py:389
  116.7 14.3 %collective-permute-start.36 = (bf16[64,2048]{1,0:T(8,128)(2,1)S(1)}, bf16[64,2048]{1,0:T(8,128)(2,1)S(1)}, u32[]{:S(2)}, u32[]{:S(2)}) collective-permute-start(bf16[64,2048]{1,0:T(8,128)(2,1)S(1)} %get-tuple-element.70), channel_id=1, source_target_pairs={{0,8},{4,12},{8,0},{12,4},{1,9},{5,13},{9,1},{13,5},{2,10},{6,14},... | collective-permute-start | bytes 786440 | tf_op jit(solution)/shard_map/ppermute | solution.py:389
  118.7 12.3 %collective-permute-start.34 = (bf16[64,2048]{1,0:T(8,128)(2,1)S(1)}, bf16[64,2048]{1,0:T(8,128)(2,1)S(1)}, u32[]{:S(2)}, u32[]{:S(2)}) collective-permute-start(bf16[64,2048]{1,0:T(8,128)(2,1)S(1)} %get-tuple-element.69), channel_id=1, source_target_pairs={{0,4},{4,0},{8,12},{12,8},{1,5},{5,1},{9,13},{13,9},{2,6},{6,2},{1... | collective-permute-start | bytes 786440 | tf_op jit(solution)/shard_map/ppermute | solution.py:389
  118.7 12.3 %collective-permute-start.33 = (bf16[64,2048]{1,0:T(8,128)(2,1)S(1)}, bf16[64,2048]{1,0:T(8,128)(2,1)S(1)}, u32[]{:S(2)}, u32[]{:S(2)}) collective-permute-start(bf16[64,2048]{1,0:T(8,128)(2,1)S(1)} %get-tuple-element.65.refs_8_.refs_9_), channel_id=1, source_target_pairs={{0,4},{4,0},{8,12},{12,8},{1,5},{5,1},{9,13},{13,9},{2,6},{6,2},{1... | collective-permute-start | bytes 786440 | tf_op jit(solution)/shard_map/ppermute | solution.py:389
